TPU v7x, 512 devices: a whole 4x4x16 slice. The times are simulated.
512 devices in a mesh: segment: 8 (over z_lo), wide: 64 (over y, z_hi, x, core).
Axes of the slice: x: 4, y: 4, z: 16 (z_hi: 2, z_lo: 8; z = z_hi * 8 + z_lo), core: 2. Of those that a mesh axis runs over, the one named last changes fastest.
Arguments:
- hidden_in: bfloat16 [256, 8192], P(None, 'wide'), may hold values from -9 to 9
- gain: float32 [8, 8192], P('segment'), may hold values from 0.25 to 1.75
- w_query: bfloat16 [8, 8192, 8192], P('segment', None, 'wide'), may hold values from -1 to 1
- w_key: bfloat16 [8, 8192, 1024], P('segment', None, 'wide'), may hold values from -1 to 1
- w_value: bfloat16 [8, 8192, 1024], P('segment', None, 'wide'), may hold values from -0.0625 to 0.0625
- w_out: bfloat16 [8, 8192, 8192], P('segment', None, 'wide'), may hold values from -0.1875 to 0.1875
- length: int32 [1], replicated, may hold values from 129 to 256
- placement: int32 [256, 1], replicated, may hold values from 0 to 63, as said below
Outputs:
- layer_out: bfloat16 [8, 256, 8192], P('segment', None, 'wide')
- kv_cache: bfloat16 [8, 512, 8, 256], P('segment', 'wide')
Inputs may be any that keep to these rules, and one draw needn't show every extreme that they name: `placement`: no owner holds more than 8 pairs; some owner holds exactly 8; every owner holds at least one.
All inputs are finite; a program needn't handle non-finite values.
Results may differ from a plain program's by a relative error of at most 0.02.
Values may be sent and summed in bfloat16 or wider, within the bound.
No kernel may reach another device: no remote copies, remote signals or barrier semaphores. Data moves between devices by JAX's collectives and lax.ppermute only.
A program may use at most 64 MiB of HBM per device.

v0:
```python
import math

import jax
import jax.numpy as jnp
from jax import lax
from jax.sharding import PartitionSpec as P

SPAN = 128
BLOCK = 8


epsilon = 1e-05
rope_base = 500000.0
masked_value = -1e30


def from_partner(value, axis, distance):
    mask = 2**distance
    pairs = [(source, source ^ mask) for source in range(lax.axis_size(axis))]
    return lax.ppermute(value, axis, pairs)


def from_behind(value, axis, by):
    length = lax.axis_size(axis)
    pairs = [(i, i + by) for i in range(length) if 0 <= i + by < length]
    return lax.ppermute(value, axis, pairs)


def rotate(values, angles):
    dims_in = values.shape
    paired = values.reshape(dims_in[:-1] + (dims_in[-1] // 2, 2))
    cosine = jnp.cos(angles)
    sine_part = jnp.sin(angles)
    first_half = paired[..., 0]
    second_half = paired[..., 1]
    turned = jnp.stack(
        [
            first_half * cosine - second_half * sine_part,
            first_half * sine_part + second_half * cosine,
        ],
        axis=-1,
    )
    return turned.reshape(dims_in)


def pair_freq(pair_index, head_dim):
    return jnp.power(rope_base, -2.0 * pair_index.astype(jnp.float32) / head_dim)


def shards(hidden_in, gain, w_query, w_key, w_value, w_out, length, placement):
    segment_count = lax.axis_size("segment")
    wide_count = lax.axis_size("wide")
    segment_id = lax.axis_index("segment")
    wide_id = lax.axis_index("wide")
    row_total = hidden_in.shape[0]
    shard_width = hidden_in.shape[1]
    head_dim = w_query.shape[2]
    kv_cols = w_key.shape[2]
    group_size = head_dim // kv_cols
    bit_count = group_size.bit_length() - 1
    kv_heads = wide_count // group_size
    span_rows = SPAN
    span_count = row_total // span_rows
    block_rows = BLOCK
    block_count = row_total // block_rows
    item_count = block_count * kv_heads
    capacity = 2 * item_count // wide_count
    member = wide_id % group_size
    gain_row = gain[0]
    query_freq = pair_freq(jnp.arange(head_dim // 2, dtype=jnp.int32), head_dim)
    key_freq = pair_freq(
        member * (kv_cols // 2) + jnp.arange(kv_cols // 2, dtype=jnp.int32), head_dim
    )
    key_pos = jnp.arange(row_total, dtype=jnp.int32)
    length_now = length[0]
    score_scale = 1.0 / math.sqrt(head_dim)

    def project(operands):
        full_rows, positions = operands
        widened = full_rows.astype(jnp.float32)
        normed = (
            widened
            * lax.rsqrt(jnp.mean(widened * widened, axis=-1, keepdims=True) + epsilon)
            * gain_row
        ).astype(jnp.bfloat16)
        row_pos = positions.astype(jnp.float32)[:, None]
        query = jnp.dot(normed, w_query[0], preferred_element_type=jnp.float32)
        query = rotate(query, row_pos * query_freq[None, :]).astype(jnp.bfloat16)
        key_part = jnp.dot(normed, w_key[0], preferred_element_type=jnp.float32)
        key_part = rotate(key_part, row_pos * key_freq[None, :])
        value_part = jnp.dot(normed, w_value[0], preferred_element_type=jnp.float32)
        kv_slice = jnp.concatenate([key_part, value_part], axis=1).astype(jnp.bfloat16)
        return (query, kv_slice)

    def skip_project(operands):
        return (
            jnp.zeros((span_rows, head_dim), jnp.bfloat16),
            jnp.zeros((span_rows, 2 * kv_cols), jnp.bfloat16),
        )

    def attention(operands):
        query, own_store, positions = operands
        key_rows = own_store[:, :head_dim]
        value_rows = own_store[:, head_dim:]
        scores = (
            jnp.einsum("qd,kd->qk", query, key_rows, preferred_element_type=jnp.float32)
            * score_scale
        )
        allowed = (key_pos[None, :] <= positions[:, None]) & (key_pos[None, :] < length_now)
        scores = jnp.where(allowed, scores, masked_value)
        row_max = jnp.max(scores, axis=-1, keepdims=True)
        weights = jnp.exp(scores - row_max)
        probabilities = (weights / jnp.sum(weights, axis=-1, keepdims=True)).astype(jnp.bfloat16)
        return jnp.dot(probabilities, value_rows, preferred_element_type=jnp.float32).astype(
            jnp.bfloat16
        )

    def skip_attention(operands):
        return jnp.zeros((span_rows, head_dim), jnp.bfloat16)

    def add_heads(piece):
        weight_rows = w_out[0]
        return jnp.dot(piece, weight_rows, preferred_element_type=jnp.float32)

    def keep_rows(store, fresh, row_start, active_now):
        older = lax.dynamic_slice_in_dim(store, row_start, span_rows, 0)
        return lax.dynamic_update_slice_in_dim(
            store, jnp.where(active_now, fresh, older), row_start, 0
        )

    def section_step(tick_index, state_tuple):
        incoming, own_store, wide_store, outputs = state_tuple
        span_index = tick_index - segment_id
        active_now = (span_index >= 0) & (span_index < span_count)
        span_slot = jnp.clip(span_index, 0, span_count - 1)
        row_start = span_slot * span_rows
        positions = row_start + jnp.arange(span_rows, dtype=jnp.int32)
        fresh_rows = lax.dynamic_slice_in_dim(hidden_in, row_start, span_rows, 0)
        own_rows = jnp.where(segment_id == 0, fresh_rows, incoming)
        full_rows = lax.all_gather(own_rows, "wide", axis=1, tiled=True)
        query, kv_slice = lax.cond(active_now, project, skip_project, (full_rows, positions))
        collected = kv_slice
        for bit in range(bit_count):
            partner = from_partner(collected, "wide", bit)
            upper = wide_id // (1 << bit) % 2 == 1
            collected = jnp.concatenate(
                [jnp.where(upper, partner, collected), jnp.where(upper, collected, partner)], axis=1
            )
        own_head = collected.reshape(span_rows, group_size, 2, kv_cols)
        own_head = jnp.transpose(own_head, (0, 2, 1, 3)).reshape(span_rows, 2 * head_dim)
        own_store = keep_rows(own_store, own_head, row_start, active_now)
        context = lax.cond(active_now, attention, skip_attention, (query, own_store, positions))
        update = add_heads(lax.all_gather(context, "wide", axis=1, tiled=True))
        result = (own_rows.astype(jnp.float32) + update).astype(jnp.bfloat16)
        result = jnp.where(active_now, result, incoming)
        older_out = lax.dynamic_slice_in_dim(outputs[0], row_start, span_rows, 0)
        written = jnp.where(active_now, result, older_out)
        outputs = lax.dynamic_update_slice_in_dim(outputs, written[None], row_start, 1)
        incoming = from_behind(result, "segment", 1)
        return (incoming, own_store, wide_store, outputs)

    incoming = jnp.zeros((span_rows, shard_width), jnp.bfloat16)
    own_store = jnp.zeros((row_total, 2 * head_dim), jnp.bfloat16)
    wide_store = jnp.zeros((1,), jnp.bfloat16)
    outputs = jnp.zeros((1, row_total, shard_width), jnp.bfloat16)
    incoming, own_store, wide_store, outputs = lax.fori_loop(
        0, span_count + segment_count - 1, section_step, (incoming, own_store, wide_store, outputs)
    )
    owners = placement[:, 0]
    order_index = jnp.arange(item_count, dtype=jnp.int32)
    earlier = order_index[None, :] < order_index[:, None]
    same_owner = owners[:, None] == owners[None, :]
    item_order = jnp.sum((earlier & same_owner).astype(jnp.int32), axis=1)
    slot_ids = jnp.arange(capacity, dtype=jnp.int32)
    send_count = block_count // group_size
    blocks = own_store.reshape(send_count, group_size, block_rows, 2 * head_dim)
    own_blocks = lax.dynamic_slice_in_dim(blocks, member, 1, 1)[:, 0]
    item_rows = lax.all_gather(own_blocks, "wide", axis=0, tiled=True)
    source = jnp.arange(wide_count * send_count, dtype=jnp.int32) // send_count
    turn_index = jnp.arange(wide_count * send_count, dtype=jnp.int32) % send_count
    item_id = (source % group_size + group_size * turn_index) * kv_heads + source // group_size
    matches = item_id[:, None] == order_index[None, :]
    item_owner = jnp.sum(jnp.where(matches, owners[None, :], 0), axis=1)
    item_rank = jnp.sum(jnp.where(matches, item_order[None, :], 0), axis=1)
    wanted = (item_owner[None, :] == wide_id) & (item_rank[None, :] == slot_ids[:, None])
    kv_cache = jnp.einsum(
        "rj,jbc->rbc", wanted.astype(jnp.bfloat16), item_rows, preferred_element_type=jnp.float32
    ).astype(jnp.bfloat16)
    return (outputs, kv_cache[None])


def solution(mesh):
    in_specs = (
        P(None, "wide"),
        P("segment", None),
        P("segment", None, "wide"),
        P("segment", None, "wide"),
        P("segment", None, "wide"),
        P("segment", None, "wide"),
        P(),
        P(),
    )
    out_specs = (P("segment", None, "wide"), P("segment", "wide", None, None))
    return jax.shard_map(shards, mesh=mesh, in_specs=in_specs, out_specs=out_specs, check_vma=False)
```

profile of v0, /device:TPU:481, one launch (start us, length us, event | category | flops | bytes accessed | tf_op | source)
XLA Modules:
  0.0 2463.7 jit_solution(18032065607743536399)
XLA Ops:
  11.2 2346.9 %while.23 = (s32[]{:T(128)}, bf16[128,128]{1,0:T(8,128)(2,1)S(1)}, bf16[256,256]{0,1:T(8,128)(2,1)S(1)}, bf16[1,256,128]{2,1,0:T(8,128)(2,1)S(1)}, s32[]{:T(128)...) while((s32[]{:T(128)}, bf16[128,128]{1,0:T(8,128)(2,1)S(1)}, ...), condition=%wide.region_8.9_spmd.clone.clone, body=%wide.region_0.8_spmd.clone.clone.sunk | while | flops 637466112 | bytes 44144856 | solution.py:166
  12.0 116.9 %all-gather.7.cloned.1.call-done = bf16[128,8192]{1,0:T(8,128)(2,1)} async-done(((bf16[128,128]{1,0:T(8,128)(2,1)}), bf16[128,8192]{1,0:T(8,128)(2,1)}) %all-gather.7.cloned.1.call-update) | async-done | bytes 2097168 | tf_op jit(solution)/shard_map/while/body/eval_jaxpr/all_gather | solution.py:140
  136.6 3.7 collective-permute-start.2
  143.6 124.4 %all-gather.9.cloned.1.call-done = bf16[128,8192]{1,0:T(8,128)(2,1)} async-done(((bf16[128,128]{1,0:T(8,128)(2,1)}), bf16[128,8192]{1,0:T(8,128)(2,1)}) %all-gather.9.cloned.1.call-update) | async-done | bytes 2097168 | tf_op jit(solution)/shard_map/while/body/eval_jaxpr/all_gather | solution.py:153
  276.4 114.0 %all-gather.7.cloned.1.call-done = bf16[128,8192]{1,0:T(8,128)(2,1)} async-done(((bf16[128,128]{1,0:T(8,128)(2,1)}), bf16[128,8192]{1,0:T(8,128)(2,1)}) %all-gather.7.cloned.1.call-update) | async-done | bytes 2097168 | tf_op jit(solution)/shard_map/while/body/eval_jaxpr/all_gather | solution.py:140
  398.0 3.7 collective-permute-start.2
  405.0 124.4 %all-gather.9.cloned.1.call-done = bf16[128,8192]{1,0:T(8,128)(2,1)} async-done(((bf16[128,128]{1,0:T(8,128)(2,1)}), bf16[128,8192]{1,0:T(8,128)(2,1)}) %all-gather.9.cloned.1.call-update) | async-done | bytes 2097168 | tf_op jit(solution)/shard_map/while/body/eval_jaxpr/all_gather | solution.py:153
  537.7 113.8 %all-gather.7.cloned.1.call-done = bf16[128,8192]{1,0:T(8,128)(2,1)} async-done(((bf16[128,128]{1,0:T(8,128)(2,1)}), bf16[128,8192]{1,0:T(8,128)(2,1)}) %all-gather.7.cloned.1.call-update) | async-done | bytes 2097168 | tf_op jit(solution)/shard_map/while/body/eval_jaxpr/all_gather | solution.py:140
  659.2 3.7 collective-permute-start.2
  666.1 122.1 %all-gather.9.cloned.1.call-done = bf16[128,8192]{1,0:T(8,128)(2,1)} async-done(((bf16[128,128]{1,0:T(8,128)(2,1)}), bf16[128,8192]{1,0:T(8,128)(2,1)}) %all-gather.9.cloned.1.call-update) | async-done | bytes 2097168 | tf_op jit(solution)/shard_map/while/body/eval_jaxpr/all_gather | solution.py:153
  796.7 114.0 %all-gather.7.cloned.1.call-done = bf16[128,8192]{1,0:T(8,128)(2,1)} async-done(((bf16[128,128]{1,0:T(8,128)(2,1)}), bf16[128,8192]{1,0:T(8,128)(2,1)}) %all-gather.7.cloned.1.call-update) | async-done | bytes 2097168 | tf_op jit(solution)/shard_map/while/body/eval_jaxpr/all_gather | solution.py:140
  918.3 3.7 collective-permute-start.2
  925.3 122.1 %all-gather.9.cloned.1.call-done = bf16[128,8192]{1,0:T(8,128)(2,1)} async-done(((bf16[128,128]{1,0:T(8,128)(2,1)}), bf16[128,8192]{1,0:T(8,128)(2,1)}) %all-gather.9.cloned.1.call-update) | async-done | bytes 2097168 | tf_op jit(solution)/shard_map/while/body/eval_jaxpr/all_gather | solution.py:153
  1055.8 114.0 %all-gather.7.cloned.1.call-done = bf16[128,8192]{1,0:T(8,128)(2,1)} async-done(((bf16[128,128]{1,0:T(8,128)(2,1)}), bf16[128,8192]{1,0:T(8,128)(2,1)}) %all-gather.7.cloned.1.call-update) | async-done | bytes 2097168 | tf_op jit(solution)/shard_map/while/body/eval_jaxpr/all_gather | solution.py:140
  1177.5 3.7 collective-permute-start.2
  1184.4 120.6 %all-gather.9.cloned.1.call-done = bf16[128,8192]{1,0:T(8,128)(2,1)} async-done(((bf16[128,128]{1,0:T(8,128)(2,1)}), bf16[128,8192]{1,0:T(8,128)(2,1)}) %all-gather.9.cloned.1.call-update) | async-done | bytes 2097168 | tf_op jit(solution)/shard_map/while/body/eval_jaxpr/all_gather | solution.py:153
  1313.5 114.0 %all-gather.7.cloned.1.call-done = bf16[128,8192]{1,0:T(8,128)(2,1)} async-done(((bf16[128,128]{1,0:T(8,128)(2,1)}), bf16[128,8192]{1,0:T(8,128)(2,1)}) %all-gather.7.cloned.1.call-update) | async-done | bytes 2097168 | tf_op jit(solution)/shard_map/while/body/eval_jaxpr/all_gather | solution.py:140
  1435.1 3.7 collective-permute-start.2
  1442.1 124.9 %all-gather.9.cloned.1.call-done = bf16[128,8192]{1,0:T(8,128)(2,1)} async-done(((bf16[128,128]{1,0:T(8,128)(2,1)}), bf16[128,8192]{1,0:T(8,128)(2,1)}) %all-gather.9.cloned.1.call-update) | async-done | bytes 2097168 | tf_op jit(solution)/shard_map/while/body/eval_jaxpr/all_gather | solution.py:153
  1575.4 114.0 %all-gather.7.cloned.1.call-done = bf16[128,8192]{1,0:T(8,128)(2,1)} async-done(((bf16[128,128]{1,0:T(8,128)(2,1)}), bf16[128,8192]{1,0:T(8,128)(2,1)}) %all-gather.7.cloned.1.call-update) | async-done | bytes 2097168 | tf_op jit(solution)/shard_map/while/body/eval_jaxpr/all_gather | solution.py:140
  1697.0 3.7 collective-permute-start.2
  1704.0 124.9 %all-gather.9.cloned.1.call-done = bf16[128,8192]{1,0:T(8,128)(2,1)} async-done(((bf16[128,128]{1,0:T(8,128)(2,1)}), bf16[128,8192]{1,0:T(8,128)(2,1)}) %all-gather.9.cloned.1.call-update) | async-done | bytes 2097168 | tf_op jit(solution)/shard_map/while/body/eval_jaxpr/all_gather | solution.py:153
  1837.2 113.8 %all-gather.7.cloned.1.call-done = bf16[128,8192]{1,0:T(8,128)(2,1)} async-done(((bf16[128,128]{1,0:T(8,128)(2,1)}), bf16[128,8192]{1,0:T(8,128)(2,1)}) %all-gather.7.cloned.1.call-update) | async-done | bytes 2097168 | tf_op jit(solution)/shard_map/while/body/eval_jaxpr/all_gather | solution.py:140
  1951.0 12.9 conditional.8
  1955.9 4.2 fusion.11
  1979.9 110.2 %all-gather.9.cloned.1.call-done = bf16[128,8192]{1,0:T(8,128)(2,1)} async-done(((bf16[128,128]{1,0:T(8,128)(2,1)}), bf16[128,8192]{1,0:T(8,128)(2,1)}) %all-gather.9.cloned.1.call-update) | async-done | bytes 2097168 | tf_op jit(solution)/shard_map/while/body/eval_jaxpr/all_gather | solution.py:153
  2098.5 113.8 %all-gather.7.cloned.1.call-done = bf16[128,8192]{1,0:T(8,128)(2,1)} async-done(((bf16[128,128]{1,0:T(8,128)(2,1)}), bf16[128,8192]{1,0:T(8,128)(2,1)}) %all-gather.7.cloned.1.call-update) | async-done | bytes 2097168 | tf_op jit(solution)/shard_map/while/body/eval_jaxpr/all_gather | solution.py:140
  2212.3 12.9 conditional.8
  2217.2 4.2 fusion.11
  2232.8 3.7 collective-permute-start.2
  2241.2 109.3 %all-gather.9.cloned.1.call-done = bf16[128,8192]{1,0:T(8,128)(2,1)} async-done(((bf16[128,128]{1,0:T(8,128)(2,1)}), bf16[128,8192]{1,0:T(8,128)(2,1)}) %all-gather.9.cloned.1.call-update) | async-done | bytes 2097168 | tf_op jit(solution)/shard_map/while/body/eval_jaxpr/all_gather | solution.py:153
  2359.3 94.8 %all-gather.5.cloned.1.call-done = bf16[256,1,8,256]{3,2,1,0:T(8,128)(2,1)} async-done(((bf16[4,1,8,256]{3,2,1,0:T(8,128)(2,1)}), bf16[256,1,8,256]{3,2,1,0:T(8,128)(2,1)}) %all-gather.5.cloned.1.call-update) | async-done | bytes 1048592 | tf_op jit(solution)/shard_map/all_gather | solution.py:178
  (380 shorter events, 204.8 us)
Async XLA Ops:
  11.2 117.8 %all-gather.7.cloned.1.call-start = ((), (), s32[]{:S(2)}) async-start(), calls=%async_computation.1 | async-start | bytes 2129920 | tf_op jit(solution)/shard_map/while/body/eval_jaxpr/all_gather | solution.py:140
  11.9 256.0 %all-gather.9.cloned.1.call-start = ((), (), s32[]{:S(2)}) async-start(), calls=%async_computation.2 | async-start | bytes 2129920 | tf_op jit(solution)/shard_map/while/body/eval_jaxpr/all_gather | solution.py:153
  136.6 6.2 collective-permute-start.2
  275.6 114.9 %all-gather.7.cloned.1.call-start = ((), (), s32[]{:S(2)}) async-start(), calls=%async_computation.1 | async-start | bytes 2129920 | tf_op jit(solution)/shard_map/while/body/eval_jaxpr/all_gather | solution.py:140
  276.3 253.1 %all-gather.9.cloned.1.call-start = ((), (), s32[]{:S(2)}) async-start(), calls=%async_computation.2 | async-start | bytes 2129920 | tf_op jit(solution)/shard_map/while/body/eval_jaxpr/all_gather | solution.py:153
  398.0 6.2 collective-permute-start.2
  532.3 4.7 collective-permute-start.3
  537.0 114.5 %all-gather.7.cloned.1.call-start = ((), (), s32[]{:S(2)}) async-start(), calls=%async_computation.1 | async-start | bytes 2129920 | tf_op jit(solution)/shard_map/while/body/eval_jaxpr/all_gather | solution.py:140
  537.6 250.6 %all-gather.9.cloned.1.call-start = ((), (), s32[]{:S(2)}) async-start(), calls=%async_computation.2 | async-start | bytes 2129920 | tf_op jit(solution)/shard_map/while/body/eval_jaxpr/all_gather | solution.py:153
  659.2 6.2 collective-permute-start.2
  795.8 114.9 %all-gather.7.cloned.1.call-start = ((), (), s32[]{:S(2)}) async-start(), calls=%async_computation.1 | async-start | bytes 2129920 | tf_op jit(solution)/shard_map/while/body/eval_jaxpr/all_gather | solution.py:140
  796.6 250.8 %all-gather.9.cloned.1.call-start = ((), (), s32[]{:S(2)}) async-start(), calls=%async_computation.2 | async-start | bytes 2129920 | tf_op jit(solution)/shard_map/while/body/eval_jaxpr/all_gather | solution.py:153
  918.3 6.2 collective-permute-start.2
  1050.3 4.7 collective-permute-start.3
  1055.0 114.9 %all-gather.7.cloned.1.call-start = ((), (), s32[]{:S(2)}) async-start(), calls=%async_computation.1 | async-start | bytes 2129920 | tf_op jit(solution)/shard_map/while/body/eval_jaxpr/all_gather | solution.py:140
  1055.7 249.4 %all-gather.9.cloned.1.call-start = ((), (), s32[]{:S(2)}) async-start(), calls=%async_computation.2 | async-start | bytes 2129920 | tf_op jit(solution)/shard_map/while/body/eval_jaxpr/all_gather | solution.py:153
  1177.5 6.2 collective-permute-start.2
  1308.0 4.7 collective-permute-start.3
  1312.7 114.9 %all-gather.7.cloned.1.call-start = ((), (), s32[]{:S(2)}) async-start(), calls=%async_computation.1 | async-start | bytes 2129920 | tf_op jit(solution)/shard_map/while/body/eval_jaxpr/all_gather | solution.py:140
  1313.4 253.6 %all-gather.9.cloned.1.call-start = ((), (), s32[]{:S(2)}) async-start(), calls=%async_computation.2 | async-start | bytes 2129920 | tf_op jit(solution)/shard_map/while/body/eval_jaxpr/all_gather | solution.py:153
  1435.1 6.2 collective-permute-start.2
  1574.6 114.9 %all-gather.7.cloned.1.call-start = ((), (), s32[]{:S(2)}) async-start(), calls=%async_computation.1 | async-start | bytes 2129920 | tf_op jit(solution)/shard_map/while/body/eval_jaxpr/all_gather | solution.py:140
  1575.3 253.6 %all-gather.9.cloned.1.call-start = ((), (), s32[]{:S(2)}) async-start(), calls=%async_computation.2 | async-start | bytes 2129920 | tf_op jit(solution)/shard_map/while/body/eval_jaxpr/all_gather | solution.py:153
  1697.0 6.2 collective-permute-start.2
  1836.5 114.6 %all-gather.7.cloned.1.call-start = ((), (), s32[]{:S(2)}) async-start(), calls=%async_computation.1 | async-start | bytes 2129920 | tf_op jit(solution)/shard_map/while/body/eval_jaxpr/all_gather | solution.py:140
  1837.1 253.0 %all-gather.9.cloned.1.call-start = ((), (), s32[]{:S(2)}) async-start(), calls=%async_computation.2 | async-start | bytes 2129920 | tf_op jit(solution)/shard_map/while/body/eval_jaxpr/all_gather | solution.py:153
  1971.5 6.2 collective-permute-start.2
  2093.1 4.7 collective-permute-start.3
  2097.7 114.6 %all-gather.7.cloned.1.call-start = ((), (), s32[]{:S(2)}) async-start(), calls=%async_computation.1 | async-start | bytes 2129920 | tf_op jit(solution)/shard_map/while/body/eval_jaxpr/all_gather | solution.py:140
  2098.4 252.2 %all-gather.9.cloned.1.call-start = ((), (), s32[]{:S(2)}) async-start(), calls=%async_computation.2 | async-start | bytes 2129920 | tf_op jit(solution)/shard_map/while/body/eval_jaxpr/all_gather | solution.py:153
  2232.8 6.2 collective-permute-start.2
  2358.1 96.0 %all-gather.5.cloned.1.call-start = ((), (), s32[]{:S(2)}) async-start(), calls=%async_computation | async-start | bytes 1064960 | tf_op jit(solution)/shard_map/all_gather | solution.py:178
  (49 other events, 3776.3 us)
Sparse Core Ops, SparseCore 0:
  16.8 112.1 all-gather.6
  143.7 124.2 all-gather.8
  281.2 109.2 all-gather.6
  405.1 124.2 all-gather.8
  542.3 109.2 all-gather.6
  666.2 121.9 all-gather.8
  801.4 109.2 all-gather.6
  925.4 121.9 all-gather.8
  1060.6 109.2 all-gather.6
  1184.5 120.4 all-gather.8
  1318.3 109.2 all-gather.6
  1442.2 124.7 all-gather.8
  1580.2 109.2 all-gather.6
  1704.1 124.7 all-gather.8
  1841.8 109.2 all-gather.6
  1980.0 110.0 all-gather.8
  2103.0 109.2 all-gather.6
  2241.3 109.1 all-gather.8
Sparse Core Ops, SparseCore 1:
  2363.6 90.5 all-gather.4
where the time goes:
time: 2480 us; the launch traced here: 2460 us
  waiting for transfers between devices  2280 us (92%)
  starting transfers between devices  90.5 us (4%)
  matrix products  43.5 us (2%)
    all_gather x9, waiting for transfers between devices, section_step(): update = add_heads(lax.all_gather(context, 'wide', axis=1, tiled=True))  1080 us
    all_gather x9, waiting for transfers between devices, section_step(): full_rows = lax.all_gather(own_rows, 'wide', axis=1, tiled=True)  1030 us
    all_gather x1, waiting for transfers between devices, shards(): item_rows = lax.all_gather(own_blocks, 'wide', axis=0, tiled=True)  94.8 us
    ppermute x27, starting transfers between devices, from_partner(): return lax.ppermute(value, axis, pairs)  78.5 us
  transfers between devices with their start and end apart: 55, of which 55 were waited for; matrix products, arithmetic and copies ran while one was open for 0% of the time, Pallas kernels for 0%

commit v1 on v0

v1 whole, which is shorter than its diff:
```python
import functools
import math

import jax
import jax.numpy as jnp
from jax import lax
from jax.experimental import pallas as pl
from jax.experimental.pallas import tpu as pltpu
from jax.sharding import PartitionSpec as P

HD = 128
BLOCK = 8
NY, NZ, NX, NC = 4, 2, 4, 2
NG = NY * NZ
CHIP = NC * HD
WIDE = NG * NX * NC
SECTIONS = 8
HALF = 128
EPS = 1e-05
ROPE_BASE = 500000.0
MASKED = -1e30
VMEM = 32 * 1024 * 1024

OVER_X = [[g * 8 + x * 2 + c for x in range(NX)] for g in range(NG) for c in range(NC)]
OVER_G = [[g * 8 + x * 2 + c for g in range(NG)] for x in range(NX) for c in range(NC)]
OVER_Y = [
    [(y * 2 + z) * 8 + x * 2 + c for y in range(NY)]
    for z in range(NZ)
    for x in range(NX)
    for c in range(NC)
]
CORE_SWAP = [(w, w ^ 1) for w in range(WIDE)]
CORE_UP = [(w, w + 1) for w in range(0, WIDE, 2)]


def exchange(value, groups):
    return lax.all_to_all(value, "wide", 0, 0, axis_index_groups=groups, tiled=True)


def swap_cores(value):
    return lax.ppermute(value, "wide", CORE_SWAP)


def by_core(core, own, other, axis):
    first = jnp.where(core == 0, own, other)
    second = jnp.where(core == 0, other, own)
    return jnp.concatenate([first, second], axis=axis)


def relayout(weight, core):
    rows = weight.reshape(NG, NX, CHIP, HD).transpose(1, 0, 2, 3).reshape(NX, NG * CHIP, HD)
    mine = exchange(rows, OVER_X)
    return by_core(core, mine, swap_cores(mine), 2)


def relayout_kv(w_key, w_value, core):
    both = jnp.stack([w_key.T, w_value.T])
    width = both.shape[1]
    both = both.reshape(2, width, NG, NX, CHIP).transpose(3, 0, 1, 2, 4)
    mine = exchange(both.reshape(NX, 2 * width, NG * CHIP), OVER_X)
    other = swap_cores(mine)
    mine = mine.reshape(NX, 2, 1, width, NG * CHIP)
    other = other.reshape(NX, 2, 1, width, NG * CHIP)
    full = by_core(core, mine, other, 2)
    return full.transpose(1, 0, 2, 3, 4).reshape(2 * HD, NG * CHIP)


def eye(n):
    return lax.broadcasted_iota(jnp.int32, (n, n), 0) == lax.broadcasted_iota(jnp.int32, (n, n), 1)


def project_kernel(h_ref, gain_ref, wq_ref, wkv_ref, out_ref, normed, kv, squares):
    @pl.when(pl.program_id(0) == 0)
    def _():
        total = jnp.zeros((HALF, 1), jnp.float32)
        for y in range(NY):
            part = h_ref[y].astype(jnp.float32)
            cols = slice(y * NZ * CHIP, (y + 1) * NZ * CHIP)
            normed[:, cols] = (part * gain_ref[:, cols]).astype(jnp.bfloat16)
            total = total + jnp.sum(part * part, axis=1, keepdims=True)
        row = jnp.sum(jnp.where(eye(HALF), total, 0.0), axis=0, keepdims=True)
        high = row.astype(jnp.bfloat16).astype(jnp.float32)
        upper = lax.broadcasted_iota(jnp.int32, (16, HALF), 0) < 8
        squares[...] = jnp.where(upper, high, row - high)
        kv[...] = lax.dot_general(
            normed[...], wkv_ref[...], (((1,), (1,)), ((), ())), preferred_element_type=jnp.float32
        )

    query = jnp.dot(normed[...], wq_ref[0], preferred_element_type=jnp.float32)
    out_ref[0, :HALF, :CHIP] = query.astype(jnp.bfloat16)
    out_ref[0, :HALF, CHIP:] = kv[...].astype(jnp.bfloat16)
    out_ref[0, HALF:, :] = jnp.zeros((16, 2 * CHIP), jnp.bfloat16)
    out_ref[0, HALF:, :HALF] = squares[...].astype(jnp.bfloat16)


def project(gathered, gain, wq, wkv):
    rows = NG * CHIP
    return pl.pallas_call(
        project_kernel,
        grid=(NX,),
        in_specs=[
            pl.BlockSpec((NY, HALF, NZ * CHIP), lambda i: (0, 0, 0)),
            pl.BlockSpec((1, rows), lambda i: (0, 0)),
            pl.BlockSpec((1, rows, CHIP), lambda i: (i, 0, 0)),
            pl.BlockSpec((2 * HD, rows), lambda i: (0, 0)),
        ],
        out_specs=pl.BlockSpec((1, HALF + 16, 2 * CHIP), lambda i: (i, 0, 0)),
        out_shape=jax.ShapeDtypeStruct((NX, HALF + 16, 2 * CHIP), jnp.bfloat16),
        scratch_shapes=[
            pltpu.VMEM((HALF, rows), jnp.bfloat16),
            pltpu.VMEM((HALF, CHIP), jnp.float32),
            pltpu.VMEM((16, HALF), jnp.float32),
        ],
        compiler_params=pltpu.CompilerParams(vmem_limit_bytes=VMEM),
        name="project",
    )(gathered, gain, wq, wkv)


def turn_kernel(features, part_ref, cos_ref, sin_ref, q_ref, kv_ref):
    total = jnp.zeros((HALF, 2 * CHIP), jnp.float32)
    squares = jnp.zeros((16, HALF), jnp.float32)
    for x in range(NX):
        total = total + part_ref[x, :HALF, :].astype(jnp.float32)
        squares = squares + part_ref[x, HALF:, :HALF].astype(jnp.float32)
    row = lax.rsqrt((squares[0:1] + squares[8:9]) / features + EPS)
    scale = jnp.sum(jnp.where(eye(HALF), row, 0.0), axis=1, keepdims=True)
    total = total * scale
    even = lax.broadcasted_iota(jnp.int32, (HALF, HD), 1) % 2 == 0

    def rope(part):
        swapped = jnp.where(even, pltpu.roll(part, HD - 1, 1), pltpu.roll(part, 1, 1))
        return (part * cos_ref[...] + swapped * sin_ref[...]).astype(jnp.bfloat16)

    for head in range(NC):
        cols = slice(head * HD, (head + 1) * HD)
        q_ref[:, cols] = rope(total[:, cols])
    kv_ref[:, :HD] = rope(total[:, CHIP : CHIP + HD])
    kv_ref[:, HD:] = total[:, CHIP + HD :].astype(jnp.bfloat16)


def turn(parts, cos, sin, features):
    return pl.pallas_call(
        functools.partial(turn_kernel, float(features)),
        out_shape=[jax.ShapeDtypeStruct((HALF, CHIP), jnp.bfloat16)] * 2,
        compiler_params=pltpu.CompilerParams(vmem_limit_bytes=VMEM),
        name="turn",
    )(parts, cos, sin)


def attend_kernel(info_ref, q_ref, own_ref, first_ref, out_ref):
    core = info_ref[0]
    length = info_ref[1]
    scale = 1.0 / math.sqrt(HD)
    row = lax.broadcasted_iota(jnp.int32, (HALF, HALF), 0)
    col = lax.broadcasted_iota(jnp.int32, (HALF, HALF), 1)
    seen_own = (col <= row) & (col + core * HALF < length)
    seen_first = col < jnp.where(core == 1, length, 0)
    contract = (((1,), (1,)), ((), ()))
    for head in range(NC):
        cols = slice(head * HD, (head + 1) * HD)
        query = q_ref[:, cols]
        own = lax.dot_general(query, own_ref[:, :HD], contract, preferred_element_type=jnp.float32)
        first = lax.dot_general(
            query, first_ref[:, :HD], contract, preferred_element_type=jnp.float32
        )
        own = jnp.where(seen_own, own * scale, MASKED)
        first = jnp.where(seen_first, first * scale, MASKED)
        top = jnp.maximum(
            jnp.max(own, axis=1, keepdims=True), jnp.max(first, axis=1, keepdims=True)
        )
        own = jnp.exp(own - top)
        first = jnp.exp(first - top)
        total = jnp.sum(own, axis=1, keepdims=True) + jnp.sum(first, axis=1, keepdims=True)
        own = (own / total).astype(jnp.bfloat16)
        first = (first / total).astype(jnp.bfloat16)
        context = jnp.dot(own, own_ref[:, HD:], preferred_element_type=jnp.float32)
        context += jnp.dot(first, first_ref[:, HD:], preferred_element_type=jnp.float32)
        context = context.astype(jnp.bfloat16)
        for g in range(NG):
            out_ref[g, :, cols] = context


def attend(info, query, own, first):
    vmem = pl.BlockSpec(memory_space=pltpu.VMEM)
    return pl.pallas_call(
        attend_kernel,
        in_specs=[pl.BlockSpec(memory_space=pltpu.SMEM), vmem, vmem, vmem],
        out_specs=vmem,
        out_shape=jax.ShapeDtypeStruct((NG, HALF, CHIP), jnp.bfloat16),
        compiler_params=pltpu.CompilerParams(vmem_limit_bytes=VMEM),
        name="attend",
    )(info, query, own, first)


def output_kernel(ctx_ref, w_ref, out_ref, rows):
    @pl.when(pl.program_id(0) == 0)
    def _():
        for g in range(NG):
            rows[:, g * CHIP : (g + 1) * CHIP] = ctx_ref[g]

    part = jnp.dot(rows[...], w_ref[0], preferred_element_type=jnp.float32)
    out_ref[0] = part.astype(jnp.bfloat16)


def output(context, wo):
    rows = NG * CHIP
    return pl.pallas_call(
        output_kernel,
        grid=(NX,),
        in_specs=[
            pl.BlockSpec((NG, HALF, CHIP), lambda i: (0, 0, 0)),
            pl.BlockSpec((1, rows, CHIP), lambda i: (i, 0, 0)),
        ],
        out_specs=pl.BlockSpec((1, HALF, CHIP), lambda i: (i, 0, 0)),
        out_shape=jax.ShapeDtypeStruct((NX, HALF, CHIP), jnp.bfloat16),
        scratch_shapes=[pltpu.VMEM((HALF, rows), jnp.bfloat16)],
        compiler_params=pltpu.CompilerParams(vmem_limit_bytes=VMEM),
        name="output",
    )(context, wo)


def relay_pairs(first):
    same, cross = [], []
    for s in range(first, SECTIONS - 1, 2):
        for w in range(WIDE):
            same.append((s * WIDE + w, (s + 1) * WIDE + w))
            cross.append((s * WIDE + w, (s + 1) * WIDE + (w ^ 8)))
    return same, cross


def shards(hidden_in, gain, w_query, w_key, w_value, w_out, length, placement):
    segment = lax.axis_index("segment")
    wide = lax.axis_index("wide")
    core = wide % 2
    z = wide // 8 % 2
    x = wide // 2 % NX
    features = gain.shape[1]

    halves = hidden_in.reshape(2, HALF, HD)
    kept = lax.dynamic_index_in_dim(halves, core, 0, keepdims=False)
    given = lax.dynamic_index_in_dim(halves, 1 - core, 0, keepdims=False)
    start = by_core(core, kept, swap_cores(given), 1)

    wq = relayout(w_query[0], core)
    wkv = relayout_kv(w_key[0], w_value[0], core)
    wo = relayout(w_out[0], core)
    gain_x = lax.dynamic_index_in_dim(gain.reshape(NG, NX, CHIP), x, 1, keepdims=False)
    gain_x = gain_x.reshape(1, NG * CHIP)

    lane = jnp.arange(HD, dtype=jnp.int32)
    freq = jnp.power(ROPE_BASE, -2.0 * (lane // 2).astype(jnp.float32) / HD)
    position = (core * HALF + jnp.arange(HALF, dtype=jnp.int32)).astype(jnp.float32)
    angle = position[:, None] * freq[None, :]
    cos = jnp.cos(angle)
    sin = jnp.where(lane[None, :] % 2 == 0, -1.0, 1.0) * jnp.sin(angle)
    info = jnp.stack([core.astype(jnp.int32), length[0]])

    def first_gather(value):
        sent = jnp.broadcast_to(value[None], (NG, HALF, CHIP))
        got = exchange(sent, OVER_G).reshape(NY, NZ, HALF, CHIP)
        return got.transpose(0, 2, 1, 3).reshape(NY, HALF, NZ * CHIP)

    def later_gather(same, cross):
        pair = jnp.concatenate(
            [jnp.where(z == 0, same, cross), jnp.where(z == 0, cross, same)], axis=1
        )
        return exchange(jnp.broadcast_to(pair[None], (NY, HALF, NZ * CHIP)), OVER_Y)

    def layer(own, gathered):
        parts = exchange(project(gathered, gain_x, wq, wkv), OVER_X)
        query, kv = turn(parts, cos, sin, features)
        first = lax.ppermute(kv, "wide", CORE_UP)
        context = exchange(attend(info, query, kv, first), OVER_G)
        parts = exchange(output(context, wo), OVER_X).astype(jnp.float32)
        result = own.astype(jnp.float32) + (parts[0] + parts[1] + parts[2] + parts[3])
        return result.astype(jnp.bfloat16), kv

    def send(pairs):
        same, cross = pairs

        def run(value):
            axes = ("segment", "wide")
            return lax.ppermute(value, axes, same), lax.ppermute(value, axes, cross)

        return run

    even, odd = send(relay_pairs(0)), send(relay_pairs(1))

    def tick(t, state):
        own, gathered, kv = state
        own, kv = lax.cond(
            segment == t, layer, lambda own, gathered: (own, kv), own, gathered
        )

        def hand_on(own, gathered):
            same, cross = lax.cond(t % 2 == 0, even, odd, own)
            return lax.cond(
                segment == t + 1,
                lambda: (same, later_gather(same, cross)),
                lambda: (own, gathered),
            )

        own, gathered = lax.cond(
            ((segment == t) | (segment == t + 1)) & (t < SECTIONS - 1),
            hand_on,
            lambda own, gathered: (own, gathered),
            own,
            gathered,
        )
        return own, gathered, kv

    gathered = lax.cond(
        segment == 0,
        first_gather,
        lambda value: jnp.zeros((NY, HALF, NZ * CHIP), jnp.bfloat16),
        start,
    )
    kv = jnp.zeros((HALF, CHIP), jnp.bfloat16)
    own, gathered, kv = lax.fori_loop(0, SECTIONS, tick, (start, gathered, kv))

    columns = own.reshape(HALF, NC, HD)
    kept = lax.dynamic_index_in_dim(columns, core, 1, keepdims=False)
    given = lax.dynamic_index_in_dim(columns, 1 - core, 1, keepdims=False)
    outputs = by_core(core, kept, swap_cores(given), 0)

    owners = placement[:, 0]
    items = owners.shape[0]
    order = jnp.arange(items, dtype=jnp.int32)
    earlier = (order[None, :] < order[:, None]) & (owners[:, None] == owners[None, :])
    rank = jnp.sum(earlier.astype(jnp.int32), axis=1)
    slots = 2 * items // WIDE
    blocks = HALF // BLOCK
    by_head = (jnp.arange(2 * blocks)[None, :] * NG + jnp.arange(NG)[:, None]).astype(jnp.int32)
    mine = lax.dynamic_slice_in_dim(by_head, core * blocks, blocks, 1).reshape(-1)
    match = mine[:, None] == order[None, :]
    item_owner = jnp.sum(jnp.where(match, owners[None, :], 0), axis=1)
    item_rank = jnp.sum(jnp.where(match, rank[None, :], 0), axis=1)
    slot = jnp.arange(slots, dtype=jnp.int32)

    sent = jnp.broadcast_to(kv[None], (NG, HALF, CHIP))
    rows = exchange(sent, OVER_G).reshape(NG * blocks, BLOCK * CHIP)

    def chosen(owner):
        wanted = (item_owner[None, :] == owner) & (item_rank[None, :] == slot[:, None])
        return jnp.dot(wanted.astype(jnp.bfloat16), rows, preferred_element_type=jnp.float32)

    here = chosen(wide)
    there = chosen(wide ^ 1).astype(jnp.bfloat16)
    cache = (here + swap_cores(there).astype(jnp.float32)).astype(jnp.bfloat16)
    return outputs[None], cache.reshape(1, slots, BLOCK, CHIP)


def solution(mesh):
    in_specs = (
        P(None, "wide"),
        P("segment", None),
        P("segment", None, "wide"),
        P("segment", None, "wide"),
        P("segment", None, "wide"),
        P("segment", None, "wide"),
        P(),
        P(),
    )
    out_specs = (P("segment", None, "wide"), P("segment", "wide", None, None))
    return jax.shard_map(shards, mesh=mesh, in_specs=in_specs, out_specs=out_specs, check_vma=False)
```

time: 2480 us -> 813 us (0.33)
  waiting for transfers between devices: 2280 us -> 678 us
  matrix products: 43.5 us -> 0.36 us
  starting transfers between devices: 90.5 us -> 59.5 us
  blocking collectives: 0 us -> 28.5 us
    all_gather x19 -> x0, waiting for transfers between devices: 2210 us -> none  [the longest x9 1080 us: section_step(): update = add_heads(lax.all_gather(context, 'wide', axis=1, tiled=True))]
    ppermute x36 -> x9, waiting for transfers between devices: 74.9 us -> 613 us  [the longest x2 605 us: run(): return (lax.ppermute(value, axes, same), lax.ppermute(value, axes, cross))]
    all_to_all x0 -> x6, waiting for transfers between devices: none -> 65 us  [exchange(): lax.all_to_all(value, 'wide', 0, 0, axis_index_groups=groups, tiled=True)]
    ppermute x36 -> x9, starting transfers between devices: 90.1 us -> 26.1 us  [the longest x6 22.2 us: swap_cores(): return lax.ppermute(value, 'wide', CORE_SWAP)]
    dot_general x20 -> x2, matrix products: 43.5 us -> 0.36 us  [chosen(): jnp.dot(wanted.astype(jnp.bfloat16), rows, preferred_element_type=jnp.flo...]
    all_to_all x0 -> x6, starting transfers between devices: none -> 33.4 us  [exchange(): lax.all_to_all(value, 'wide', 0, 0, axis_index_groups=groups, tiled=True)]
    all_to_all x0 -> x2, blocking collectives: none -> 28.5 us  [exchange(): lax.all_to_all(value, 'wide', 0, 0, axis_index_groups=groups, tiled=True)]
  transfers between devices with their start and end apart: 55 -> 15, of which waited for: 55 -> 12; matrix products, arithmetic and copies ran while one was open for 0% -> 1% of each run, Pallas kernels for 0% -> 0%
where the time goes in v1:
time: 813 us; the launch traced here: 806 us
  waiting for transfers between devices  678 us (83%)
  starting transfers between devices  59.5 us (7%)
  blocking collectives  28.5 us (4%)
  local copies, waits for them, and re-layouts  13.2 us (2%)
  other arithmetic  12.5 us (2%)
  Pallas kernels  11.3 us (1%)
    ppermute x2, waiting for transfers between devices, run(): return (lax.ppermute(value, axes, same), lax.ppermute(value, axes, cross))  605 us
    all_to_all x6, waiting for transfers between devices, exchange(): lax.all_to_all(value, 'wide', 0, 0, axis_index_groups=groups, tiled=True)  65 us
    all_to_all x6, starting transfers between devices, exchange(): lax.all_to_all(value, 'wide', 0, 0, axis_index_groups=groups, tiled=True)  33.4 us
    all_to_all x2, blocking collectives, exchange(): lax.all_to_all(value, 'wide', 0, 0, axis_index_groups=groups, tiled=True)  28.5 us
    ppermute x6, starting transfers between devices, swap_cores(): return lax.ppermute(value, 'wide', CORE_SWAP)  22.2 us
  transfers between devices with their start and end apart: 15, of which 12 were waited for; matrix products, arithmetic and copies ran while one was open for 1% of the time, Pallas kernels for 0%

profile of v1, /device:TPU:481, one launch (start us, length us, event | category | flops | bytes accessed | tf_op | source)
XLA Modules:
  0.0 806.0 jit_solution(13126902876964641892)
XLA Ops:
  0.6 3.2 copy.37
  3.8 4.6 all-to-all-start.5
  9.9 24.2 %all-to-all-done.5 = bf16[4,2048,128]{2,1,0:T(8,128)(2,1)} async-done(((bf16[4,2048,128]{2,1,0:T(8,128)(2,1)}), bf16[4,2048,128]{2,1,0:T(8,128)(2,1)}, u32[]{:S(2)}, u32[]{:S(2)}) %all-to-all-start.5) | async-done | bytes 2097184 | tf_op jit(solution)/shard_map/all_to_all | solution.py:37
  34.2 4.6 all-to-all-start.7
  38.8 3.5 collective-permute-start.6
  42.2 21.4 %all-to-all-done.7 = bf16[4,2048,128]{2,1,0:T(8,128)(2,1)} async-done(((bf16[4,2048,128]{2,1,0:T(8,128)(2,1)}), bf16[4,2048,128]{2,1,0:T(8,128)(2,1)}, u32[]{:S(2)}, u32[]{:S(2)}) %all-to-all-start.7) | async-done | bytes 2097184 | tf_op jit(solution)/shard_map/all_to_all | solution.py:37
  63.6 4.4 collective-permute-start.8
  69.6 3.5 all-to-all-start.6
  77.1 5.6 all-to-all-done.6
  82.7 2.7 collective-permute-start.7
  87.2 3.7 broadcast_select_fusion.3
  91.0 2.5 pad_maximum_fusion.2
  93.4 2.4 pad_maximum_fusion.1
  96.5 680.4 %while.19 = (s32[]{:T(128)}, bf16[128,256]{1,0:T(8,128)(2,1)S(1)}, bf16[4,128,512]{2,1,0:T(8,128)(2,1)}, bf16[128,256]{1,0:T(8,128)(2,1)}, s32[]{:T(128)}, /*ind...) while((s32[]{:T(128)}, bf16[128,256]{1,0:T(8,128)(2,1)S(1)}, ...), condition=%wide.region_11.12_spmd.clone.clone, body=%wide.region_2.11_spmd.clone.clone.sunk | while | flops 688154 | bytes 8784159 | solution.py:319
  97.7 620.6 %conditional.13 = ((bf16[128,256]{1,0:T(8,128)(2,1)S(1)}, bf16[4,128,512]{2,1,0:T(8,128)(2,1)})) conditional(s32[]{:T(128)} %convert_element_type.85, (bf16[128,256]{1,0:T(8,128)(2,1)S(1)}, bf16[4,128,512]{2,1,0:T(8,128)(2,1)}) %tuple.107, (s32[]{:T(128)}, s32[]{:T(128)}, bf16[128,256]{1,0:T(8,128)(2,1)S(1)}, bf16[4,128,512]{2,1,0:T(8,128)(2,1)}, ...), branch_computations={%region_5.5_spmd, %region_6.10_spmd} | conditional | flops 327697 | bytes 3408223 | solution.py:303
  97.7 607.7 %conditional = (bf16[128,256]{1,0:T(8,128)(2,1)}, bf16[128,256]{1,0:T(8,128)(2,1)}) conditional(s32[]{:T(128)} %convert_element_type.50, bf16[128,256]{1,0:T(8,128)(2,1)S(1)} %get-tuple-element.273, bf16[128,256]{1,0:T(8,128)(2,1)S(1)} %get-tuple-element.273), branch_computations={%region_7.6_spmd, %region_8.7_spmd} | conditional | bytes 524384 | solution.py:296
  100.3 594.6 %collective-permute-done.2 = bf16[128,256]{1,0:T(8,128)(2,1)} collective-permute-done((bf16[128,256]{1,0:T(8,128)(2,1)S(1)}, bf16[128,256]{1,0:T(8,128)(2,1)}, u32[]{:S(2)}, u32[]{:S(2)}) %collective-permute-start.2) | collective-permute-done | bytes 65568 | tf_op jit(solution)/shard_map/while/body/eval_jaxpr/cond/branch_1_fun/cond/branch_1_fun/ppermute | solution.py:283
  694.9 10.5 %collective-permute-done.3 = bf16[128,256]{1,0:T(8,128)(2,1)} collective-permute-done((bf16[128,256]{1,0:T(8,128)(2,1)S(1)}, bf16[128,256]{1,0:T(8,128)(2,1)}, u32[]{:S(2)}, u32[]{:S(2)}) %collective-permute-start.3) | collective-permute-done | bytes 65568 | tf_op jit(solution)/shard_map/while/body/eval_jaxpr/cond/branch_1_fun/cond/branch_1_fun/ppermute | solution.py:283
  705.4 12.9 %conditional.1 = ((bf16[128,256]{1,0:T(8,128)(2,1)S(1)}, bf16[4,128,512]{2,1,0:T(8,128)(2,1)})) conditional(s32[]{:T(128)} %convert_element_type.49, (bf16[128,256]{1,0:T(8,128)(2,1)S(1)}, bf16[4,128,512]{2,1,0:T(8,128)(2,1)}) %tuple.45, (s32[]{:T(128)}, bf16[128,256]{1,0:T(8,128)(2,1)}, bf16[128,256]{1,0:T(8,128)(2,1)}) %tuple.46), branch_computations={%region_9.8_spmd, %region_10.9_spmd} | conditional | flops 327681 | bytes 2883650 | solution.py:297
  707.1 4.1 all-to-all-start.4
  712.1 6.2 all-to-all-done.4
  718.4 58.5 %conditional.12 = ((bf16[128,256]{1,0:T(8,128)(2,1)S(1)}, bf16[128,256]{1,0:T(8,128)(2,1)})) conditional(s32[]{:T(128)} %convert_element_type.86, (bf16[128,256]{1,0:T(8,128)(2,1)S(1)}, bf16[128,256]{1,0:T(8,128)(2,1)}) %tuple.105, (bf16[128,256]{1,0:T(8,128)(2,1)S(1)}, bf16[4,128,512]{2,1,0:T(8,128)(2,1)}, f32[1,2048]{1,0:T(1,128)S(1)}, ...), branch_computations={%region_3.3_spmd, %region_4.4_spmd} | conditional | flops 344064 | bytes 5309024 | solution.py:291
  718.4 5.1 project.1
  723.5 3.5 all-to-all-start.1
  727.5 6.8 all-to-all-done.1.part_ref
  736.4 6.5 collective-permute-done.4.first_ref
  744.7 20.6 %all_to_all.41.ctx_ref = bf16[8,128,256]{2,1,0:T(8,128)(2,1)S(1)} all-to-all(bf16[8,128,256]{2,1,0:T(8,128)(2,1)S(1)} %attend.1), channel_id=1, replica_groups={{0,8,16,24,32,40,48,56},{1,9,17,25,33,41,49,57},{2,10,18,26,34,42,50,58..., dimensions={0} | all-to-all | bytes 1048576 | tf_op jit(solution)/shard_map/while/body/eval_jaxpr/cond/branch_1_fun/all_to_all | solution.py:37
  765.3 3.6 output.1
  768.8 7.9 all_to_all.42
  778.6 13.2 %all-to-all-start.8 = ((bf16[8,128,256]{2,1,0:T(8,128)(2,1)}), bf16[8,128,256]{2,1,0:T(8,128)(2,1)S(1)}, u32[]{:S(2)}, u32[]{:S(2)}) async-start(bf16[8,128,256]{2,1,0:T(8,128)(2,1)} %broadcast_in_dim.75), calls=%async_computation.8 | async-start | bytes 1048576 | tf_op jit(solution)/shard_map/all_to_all | solution.py:37
  792.5 4.6 collective-permute-start.9
  799.1 5.2 collective-permute-start.10
  (95 shorter events, 26.0 us)
Async XLA Ops:
  3.8 4.6 copy-start
  3.8 30.4 %all-to-all-start.5 = ((bf16[4,2048,128]{2,1,0:T(8,128)(2,1)}), bf16[4,2048,128]{2,1,0:T(8,128)(2,1)}, u32[]{:S(2)}, u32[]{:S(2)}) async-start(bf16[4,2048,128]{2,1,0:T(8,128)(2,1)} %bitcast.9), calls=%async_computation.5 | async-start | bytes 4194304 | tf_op jit(solution)/shard_map/all_to_all | solution.py:37
  34.2 33.8 %copy-start.1 = (bf16[1,8192,16]{1,2,0:T(8,128)(2,1)S(1)}, bf16[1,8192,16]{1,2,0:T(8,128)(2,1)}, u32[]{:S(2)}) copy-start(bf16[1,8192,16]{1,2,0:T(8,128)(2,1)} %param.23) | copy-start | bytes 786436
  34.2 34.1 %copy-start.2 = (bf16[1,8192,16]{1,2,0:T(8,128)(2,1)S(1)}, bf16[1,8192,16]{1,2,0:T(8,128)(2,1)}, u32[]{:S(2)}) copy-start(bf16[1,8192,16]{1,2,0:T(8,128)(2,1)} %param.24) | copy-start | bytes 786436
  34.2 29.5 %all-to-all-start.7 = ((bf16[4,2048,128]{2,1,0:T(8,128)(2,1)}), bf16[4,2048,128]{2,1,0:T(8,128)(2,1)}, u32[]{:S(2)}, u32[]{:S(2)}) async-start(bf16[4,2048,128]{2,1,0:T(8,128)(2,1)} %bitcast.22), calls=%async_computation.7 | async-start | bytes 4194304 | tf_op jit(solution)/shard_map/all_to_all | solution.py:37
  38.8 48.5 %collective-permute-start.6 = (bf16[4,2048,128]{2,1,0:T(8,128)(2,1)}, bf16[4,2048,128]{2,1,0:T(8,128)(2,1)}, u32[]{:S(2)}, u32[]{:S(2)}) collective-permute-start(bf16[4,2048,128]{2,1,0:T(8,128)(2,1)} %all-to-all-done.5), channel_id=1, source_target_pairs={{0,1},{1,0},{2,3},{3,2},{4,5},{5,4},{6,7},{7,6},{8,9},{9,8},{10,11... | collective-permute-start | bytes 6291464 | tf_op jit(solution)/shard_map/ppermute | solution.py:41
  63.6 23.6 %collective-permute-start.8 = (bf16[4,2048,128]{2,1,0:T(8,128)(2,1)}, bf16[4,2048,128]{2,1,0:T(8,128)(2,1)}, u32[]{:S(2)}, u32[]{:S(2)}) collective-permute-start(bf16[4,2048,128]{2,1,0:T(8,128)(2,1)} %all-to-all-done.7), channel_id=1, source_target_pairs={{0,1},{1,0},{2,3},{3,2},{4,5},{5,4},{6,7},{7,6},{8,9},{9,8},{10,11... | collective-permute-start | bytes 6291464 | tf_op jit(solution)/shard_map/ppermute | solution.py:41
  68.3 4.9 copy-start.3
  68.3 7.4 copy-start.4
  69.6 13.1 %all-to-all-start.6 = ((bf16[4,32,2048]{2,1,0:T(8,128)(2,1)}), bf16[4,32,2048]{2,1,0:T(8,128)(2,1)S(1)}, u32[]{:S(2)}, u32[]{:S(2)}) async-start(bf16[4,32,2048]{2,1,0:T(8,128)(2,1)} %reshape.159), calls=%async_computation.6 | async-start | bytes 1048576 | tf_op jit(solution)/shard_map/all_to_all | solution.py:37
  73.2 12.3 %collective-permute-start.5 = (bf16[128,128]{1,0:T(8,128)(2,1)S(1)}, bf16[128,128]{1,0:T(8,128)(2,1)S(1)}, u32[]{:S(2)}, u32[]{:S(2)}) collective-permute-start(bf16[128,128]{1,0:T(8,128)(2,1)S(1)} %dynamic-slice_bitcast_fusion), channel_id=1, source_target_pairs={{0,1},{1,0},{2,3},{3,2},{4,5},{5,4},{6,7},{7,6},{8,9},{9,8},{10,11... | collective-permute-start | bytes 98312 | tf_op jit(solution)/shard_map/ppermute | solution.py:41
  82.7 4.2 collective-permute-start.7
  96.5 695.4 %copy-start.5 = (s32[256,1]{0,1:T(1,128)S(1)}, s32[256,1]{0,1:T(1,128)}, u32[]{:S(2)}) copy-start(s32[256,1]{0,1:T(1,128)} %param.27) | copy-start | bytes 3076
  97.7 597.2 %collective-permute-start.2 = (bf16[128,256]{1,0:T(8,128)(2,1)S(1)}, bf16[128,256]{1,0:T(8,128)(2,1)}, u32[]{:S(2)}, u32[]{:S(2)}) collective-permute-start(bf16[128,256]{1,0:T(8,128)(2,1)S(1)} %param.6), channel_id=1, source_target_pairs={{0,64},{1,65},{2,66},{3,67},{4,68},{5,69},{6,70},{7,71},{8,72},{9,... | collective-permute-start | bytes 196616 | tf_op jit(solution)/shard_map/while/body/eval_jaxpr/cond/branch_1_fun/cond/branch_1_fun/ppermute | solution.py:283
  99.0 606.4 %collective-permute-start.3 = (bf16[128,256]{1,0:T(8,128)(2,1)S(1)}, bf16[128,256]{1,0:T(8,128)(2,1)}, u32[]{:S(2)}, u32[]{:S(2)}) collective-permute-start(bf16[128,256]{1,0:T(8,128)(2,1)S(1)} %param.6), channel_id=1, source_target_pairs={{0,72},{1,73},{2,74},{3,75},{4,76},{5,77},{6,78},{7,79},{8,64},{9,... | collective-permute-start | bytes 196616 | tf_op jit(solution)/shard_map/while/body/eval_jaxpr/cond/branch_1_fun/cond/branch_1_fun/ppermute | solution.py:283
  707.1 11.1 %all-to-all-start.4 = ((bf16[4,128,512]{2,1,0:T(8,128)(2,1)}), bf16[4,128,512]{2,1,0:T(8,128)(2,1)}, u32[]{:S(2)}, u32[]{:S(2)}) async-start(bf16[4,128,512]{2,1,0:T(8,128)(2,1)} %broadcast_in_dim.32), calls=%async_computation.4 | async-start | bytes 1048576 | tf_op jit(solution)/shard_map/while/body/eval_jaxpr/cond/branch_1_fun/cond/branch_1_fun/all_to_all | solution.py:37
  723.5 10.7 %all-to-all-start.1 = ((bf16[4,144,512]{2,1,0:T(8,128)(2,1)}), bf16[4,144,512]{2,1,0:T(8,128)(2,1)S(1)}, u32[]{:S(2)}, u32[]{:S(2)}) async-start(bf16[4,144,512]{2,1,0:T(8,128)(2,1)} %project.1), calls=%async_computation.1 | async-start | bytes 1179648 | tf_op jit(solution)/shard_map/while/body/eval_jaxpr/cond/branch_1_fun/all_to_all | solution.py:37
  735.2 7.8 collective-permute-start.4
  778.6 20.1 %all-to-all-start.8 = ((bf16[8,128,256]{2,1,0:T(8,128)(2,1)}), bf16[8,128,256]{2,1,0:T(8,128)(2,1)S(1)}, u32[]{:S(2)}, u32[]{:S(2)}) async-start(bf16[8,128,256]{2,1,0:T(8,128)(2,1)} %broadcast_in_dim.75), calls=%async_computation.8 | async-start | bytes 1048576 | tf_op jit(solution)/shard_map/all_to_all | solution.py:37
  792.5 5.5 collective-permute-start.9
  799.1 6.0 collective-permute-start.10

commit v2 on v1

--- a/solution.py
+++ b/solution.py
@@ -29,6 +29,7 @@
     for x in range(NX)
     for c in range(NC)
 ]
+Z_SWAP = [(w, w ^ 8) for w in range(WIDE)]
 CORE_SWAP = [(w, w ^ 1) for w in range(WIDE)]
 CORE_UP = [(w, w + 1) for w in range(0, WIDE, 2)]
 
@@ -47,10 +48,16 @@
     return jnp.concatenate([first, second], axis=axis)
 
 
-def relayout(weight, core):
+def relayout(weight):
     rows = weight.reshape(NG, NX, CHIP, HD).transpose(1, 0, 2, 3).reshape(NX, NG * CHIP, HD)
     mine = exchange(rows, OVER_X)
-    return by_core(core, mine, swap_cores(mine), 2)
+    return mine, swap_cores(mine)
+
+
+def relayout_out(kept, given):
+    near = exchange(kept, OVER_Y)
+    far = exchange(lax.ppermute(given, "wide", Z_SWAP), OVER_Y)
+    return near, swap_cores(near), far, swap_cores(far)
 
 
 def relayout_kv(w_key, w_value, core):
@@ -69,7 +76,13 @@
     return lax.broadcasted_iota(jnp.int32, (n, n), 0) == lax.broadcasted_iota(jnp.int32, (n, n), 1)
 
 
-def project_kernel(h_ref, gain_ref, wq_ref, wkv_ref, out_ref, normed, kv, squares):
+def aligned(block, size=1):
+    return pl.ds(pl.multiple_of(block * HD, HD), size * HD)
+
+
+def project_kernel(
+    info_ref, h_ref, gain_ref, own_ref, other_ref, wkv_ref, out_ref, normed, kv, squares
+):
     @pl.when(pl.program_id(0) == 0)
     def _():
         total = jnp.zeros((HALF, 1), jnp.float32)
@@ -86,22 +99,28 @@
             normed[...], wkv_ref[...], (((1,), (1,)), ((), ())), preferred_element_type=jnp.float32
         )
 
-    query = jnp.dot(normed[...], wq_ref[0], preferred_element_type=jnp.float32)
-    out_ref[0, :HALF, :CHIP] = query.astype(jnp.bfloat16)
+    weight = jnp.concatenate([own_ref[0], other_ref[0]], axis=1)
+    query = jnp.dot(normed[...], weight, preferred_element_type=jnp.float32).astype(jnp.bfloat16)
+    core = info_ref[0]
+    out_ref[0, :HALF, aligned(core)] = query[:, :HD]
+    out_ref[0, :HALF, aligned(1 - core)] = query[:, HD:]
     out_ref[0, :HALF, CHIP:] = kv[...].astype(jnp.bfloat16)
     out_ref[0, HALF:, :] = jnp.zeros((16, 2 * CHIP), jnp.bfloat16)
     out_ref[0, HALF:, :HALF] = squares[...].astype(jnp.bfloat16)
 
 
-def project(gathered, gain, wq, wkv):
+def project(info, gathered, gain, wq, wkv):
     rows = NG * CHIP
+    block = pl.BlockSpec((1, rows, HD), lambda i: (i, 0, 0))
     return pl.pallas_call(
         project_kernel,
         grid=(NX,),
         in_specs=[
+            pl.BlockSpec(memory_space=pltpu.SMEM),
             pl.BlockSpec((NY, HALF, NZ * CHIP), lambda i: (0, 0, 0)),
             pl.BlockSpec((1, rows), lambda i: (0, 0)),
-            pl.BlockSpec((1, rows, CHIP), lambda i: (i, 0, 0)),
+            block,
+            block,
             pl.BlockSpec((2 * HD, rows), lambda i: (0, 0)),
         ],
         out_specs=pl.BlockSpec((1, HALF + 16, 2 * CHIP), lambda i: (i, 0, 0)),
@@ -113,7 +132,7 @@
         ],
         compiler_params=pltpu.CompilerParams(vmem_limit_bytes=VMEM),
         name="project",
-    )(gathered, gain, wq, wkv)
+    )(info, gathered, gain, *wq, wkv)
 
 
 def turn_kernel(features, part_ref, cos_ref, sin_ref, q_ref, kv_ref):
@@ -176,8 +195,8 @@
         context = jnp.dot(own, own_ref[:, HD:], preferred_element_type=jnp.float32)
         context += jnp.dot(first, first_ref[:, HD:], preferred_element_type=jnp.float32)
         context = context.astype(jnp.bfloat16)
-        for g in range(NG):
-            out_ref[g, :, cols] = context
+        for x in range(NX):
+            out_ref[x, :, cols] = context
 
 
 def attend(info, query, own, first):
@@ -186,37 +205,46 @@
         attend_kernel,
         in_specs=[pl.BlockSpec(memory_space=pltpu.SMEM), vmem, vmem, vmem],
         out_specs=vmem,
-        out_shape=jax.ShapeDtypeStruct((NG, HALF, CHIP), jnp.bfloat16),
+        out_shape=jax.ShapeDtypeStruct((NX, HALF, CHIP), jnp.bfloat16),
         compiler_params=pltpu.CompilerParams(vmem_limit_bytes=VMEM),
         name="attend",
     )(info, query, own, first)
 
 
-def output_kernel(ctx_ref, w_ref, out_ref, rows):
+def output_kernel(info_ref, ctx_ref, near_ref, near_other, far_ref, far_other, out_ref, rows):
     @pl.when(pl.program_id(0) == 0)
     def _():
-        for g in range(NG):
-            rows[:, g * CHIP : (g + 1) * CHIP] = ctx_ref[g]
-
-    part = jnp.dot(rows[...], w_ref[0], preferred_element_type=jnp.float32)
-    out_ref[0] = part.astype(jnp.bfloat16)
-
-
-def output(context, wo):
-    rows = NG * CHIP
+        for x in range(NX):
+            rows[:, x * CHIP : (x + 1) * CHIP] = ctx_ref[x]
+
+    core, z = info_ref[0], info_ref[2]
+    for half, pair in ((z, (near_ref, near_other)), (1 - z, (far_ref, far_other))):
+        weight = jnp.concatenate([pair[0][0], pair[1][0]], axis=1)
+        part = jnp.dot(rows[...], weight, preferred_element_type=jnp.float32).astype(jnp.bfloat16)
+        out_ref[0, :, aligned(half * NC + core)] = part[:, :HD]
+        out_ref[0, :, aligned(half * NC + 1 - core)] = part[:, HD:]
+
+
+def output(info, context, wo):
+    rows = NX * CHIP
+    block = pl.BlockSpec((1, rows, HD), lambda i: (i, 0, 0))
     return pl.pallas_call(
         output_kernel,
-        grid=(NX,),
+        grid=(NY,),
         in_specs=[
-            pl.BlockSpec((NG, HALF, CHIP), lambda i: (0, 0, 0)),
-            pl.BlockSpec((1, rows, CHIP), lambda i: (i, 0, 0)),
+            pl.BlockSpec(memory_space=pltpu.SMEM),
+            pl.BlockSpec((NX, HALF, CHIP), lambda i: (0, 0, 0)),
+            block,
+            block,
+            block,
+            block,
         ],
-        out_specs=pl.BlockSpec((1, HALF, CHIP), lambda i: (i, 0, 0)),
-        out_shape=jax.ShapeDtypeStruct((NX, HALF, CHIP), jnp.bfloat16),
+        out_specs=pl.BlockSpec((1, HALF, NZ * CHIP), lambda i: (i, 0, 0)),
+        out_shape=jax.ShapeDtypeStruct((NY, HALF, NZ * CHIP), jnp.bfloat16),
         scratch_shapes=[pltpu.VMEM((HALF, rows), jnp.bfloat16)],
         compiler_params=pltpu.CompilerParams(vmem_limit_bytes=VMEM),
         name="output",
-    )(context, wo)
+    )(info, context, *wo)
 
 
 def relay_pairs(first):
@@ -234,6 +262,7 @@
     core = wide % 2
     z = wide // 8 % 2
     x = wide // 2 % NX
+    y = wide // 16
     features = gain.shape[1]
 
     halves = hidden_in.reshape(2, HALF, HD)
@@ -241,9 +270,6 @@
     given = lax.dynamic_index_in_dim(halves, 1 - core, 0, keepdims=False)
     start = by_core(core, kept, swap_cores(given), 1)
 
-    wq = relayout(w_query[0], core)
-    wkv = relayout_kv(w_key[0], w_value[0], core)
-    wo = relayout(w_out[0], core)
     gain_x = lax.dynamic_index_in_dim(gain.reshape(NG, NX, CHIP), x, 1, keepdims=False)
     gain_x = gain_x.reshape(1, NG * CHIP)
 
@@ -253,27 +279,46 @@
     angle = position[:, None] * freq[None, :]
     cos = jnp.cos(angle)
     sin = jnp.where(lane[None, :] % 2 == 0, -1.0, 1.0) * jnp.sin(angle)
-    info = jnp.stack([core.astype(jnp.int32), length[0]])
+    info = jnp.stack([core, length[0], z]).astype(jnp.int32)
 
     def first_gather(value):
         sent = jnp.broadcast_to(value[None], (NG, HALF, CHIP))
         got = exchange(sent, OVER_G).reshape(NY, NZ, HALF, CHIP)
         return got.transpose(0, 2, 1, 3).reshape(NY, HALF, NZ * CHIP)
 
+    out_rows = w_out[0].reshape(NY, NZ, NX * CHIP, HD)
+    kept = lax.dynamic_index_in_dim(out_rows, z, 1, keepdims=False)
+    given = lax.dynamic_index_in_dim(out_rows, 1 - z, 1, keepdims=False)
+
+    def first_section(start, kept, given):
+        wq = relayout(w_query[0])
+        wkv = relayout_kv(w_key[0], w_value[0], core)
+        return first_gather(start), wq, wkv, relayout_out(kept, given)
+
+    def later_section(start, kept, given):
+        wq = relayout(w_query[0])
+        wkv = relayout_kv(w_key[0], w_value[0], core)
+        given, wq, wkv = lax.optimization_barrier((given, wq, wkv))
+        blank = jnp.zeros((NY, HALF, NZ * CHIP), jnp.bfloat16)
+        return blank, wq, wkv, relayout_out(kept, given)
+
+    gathered, wq, wkv, wo = lax.cond(
+        segment == 0, first_section, later_section, start, kept, given
+    )
+
     def later_gather(same, cross):
-        pair = jnp.concatenate(
-            [jnp.where(z == 0, same, cross), jnp.where(z == 0, cross, same)], axis=1
-        )
+        pair = (same.astype(jnp.float32) + cross.astype(jnp.float32)).astype(jnp.bfloat16)
         return exchange(jnp.broadcast_to(pair[None], (NY, HALF, NZ * CHIP)), OVER_Y)
 
-    def layer(own, gathered):
-        parts = exchange(project(gathered, gain_x, wq, wkv), OVER_X)
+    def layer(gathered):
+        parts = exchange(project(info, gathered, gain_x, wq, wkv), OVER_X)
         query, kv = turn(parts, cos, sin, features)
         first = lax.ppermute(kv, "wide", CORE_UP)
-        context = exchange(attend(info, query, kv, first), OVER_G)
-        parts = exchange(output(context, wo), OVER_X).astype(jnp.float32)
-        result = own.astype(jnp.float32) + (parts[0] + parts[1] + parts[2] + parts[3])
-        return result.astype(jnp.bfloat16), kv
+        context = exchange(attend(info, query, kv, first), OVER_X)
+        parts = exchange(output(info, context, wo), OVER_Y).astype(jnp.float32)
+        own = lax.dynamic_index_in_dim(gathered, y, 0, keepdims=False).astype(jnp.float32)
+        total = parts[0] + parts[1] + parts[2] + parts[3]
+        return (jnp.where(z == 0, own, 0.0) + total).astype(jnp.bfloat16), kv
 
     def send(pairs):
         same, cross = pairs
@@ -287,37 +332,33 @@
     even, odd = send(relay_pairs(0)), send(relay_pairs(1))
 
     def tick(t, state):
-        own, gathered, kv = state
-        own, kv = lax.cond(
-            segment == t, layer, lambda own, gathered: (own, kv), own, gathered
-        )
-
-        def hand_on(own, gathered):
-            same, cross = lax.cond(t % 2 == 0, even, odd, own)
+        gathered, partial, kv = state
+        partial, kv = lax.cond(segment == t, layer, lambda gathered: (partial, kv), gathered)
+
+        def hand_on(partial, gathered):
+            same, cross = lax.cond(t % 2 == 0, even, odd, partial)
             return lax.cond(
-                segment == t + 1,
-                lambda: (same, later_gather(same, cross)),
-                lambda: (own, gathered),
+                segment == t + 1, later_gather, lambda same, cross: gathered, same, cross
             )
 
-        own, gathered = lax.cond(
+        gathered = lax.cond(
             ((segment == t) | (segment == t + 1)) & (t < SECTIONS - 1),
             hand_on,
-            lambda own, gathered: (own, gathered),
-            own,
+            lambda partial, gathered: gathered,
+            partial,
             gathered,
         )
-        return own, gathered, kv
-
-    gathered = lax.cond(
-        segment == 0,
-        first_gather,
-        lambda value: jnp.zeros((NY, HALF, NZ * CHIP), jnp.bfloat16),
-        start,
-    )
+        return gathered, partial, kv
+
+    partial = jnp.zeros((HALF, NZ * CHIP), jnp.bfloat16)
     kv = jnp.zeros((HALF, CHIP), jnp.bfloat16)
-    own, gathered, kv = lax.fori_loop(0, SECTIONS, tick, (start, gathered, kv))
-
+    _, partial, kv = lax.fori_loop(0, SECTIONS, tick, (gathered, partial, kv))
+
+    pair = partial.reshape(HALF, NZ, CHIP)
+    kept = lax.dynamic_index_in_dim(pair, z, 1, keepdims=False)
+    given = lax.dynamic_index_in_dim(pair, 1 - z, 1, keepdims=False)
+    other = lax.ppermute(given, "wide", Z_SWAP)
+    own = (kept.astype(jnp.float32) + other.astype(jnp.float32)).astype(jnp.bfloat16)
     columns = own.reshape(HALF, NC, HD)
     kept = lax.dynamic_index_in_dim(columns, core, 1, keepdims=False)
     given = lax.dynamic_index_in_dim(columns, 1 - core, 1, keepdims=False)

time: 813 us -> 751 us (0.924)
  waiting for transfers between devices: 678 us -> 584 us
  blocking collectives: 28.5 us -> 78.6 us
    ppermute x2, waiting for transfers between devices: 605 us -> 468 us  [run(): return (lax.ppermute(value, axes, same), lax.ppermute(value, axes, cross))]
    ppermute x0 -> x2, waiting for transfers between devices: none -> 79.3 us  [the longest x1 67.7 us: relayout_out(): far = exchange(lax.ppermute(given, 'wide', Z_SWAP), OVER_Y)]
    all_to_all x2 -> x5, blocking collectives: 28.5 us -> 78.6 us  [exchange(): lax.all_to_all(value, 'wide', 0, 0, axis_index_groups=groups, tiled=True)]
    all_to_all x6 -> x4, waiting for transfers between devices: 65 us -> 25.9 us  [exchange(): lax.all_to_all(value, 'wide', 0, 0, axis_index_groups=groups, tiled=True)]
    all_to_all x6 -> x4, starting transfers between devices: 33.4 us -> 23.2 us  [exchange(): lax.all_to_all(value, 'wide', 0, 0, axis_index_groups=groups, tiled=True)]
    ppermute x6 -> x7, starting transfers between devices: 22.2 us -> 23.7 us  [swap_cores(): return lax.ppermute(value, 'wide', CORE_SWAP)]
  transfers between devices with their start and end apart: 15 -> 16, of which waited for: 12 -> 12; matrix products, arithmetic and copies ran while one was open for 1% -> 1% of each run, Pallas kernels for 0% -> 0%
where the time goes in v2:
time: 751 us; the launch traced here: 750 us
  waiting for transfers between devices  584 us (78%)
  blocking collectives  78.6 us (10%)
  starting transfers between devices  58.7 us (8%)
  Pallas kernels  11.1 us (1%)
  local copies, waits for them, and re-layouts  7.68 us (1%)
    ppermute x2, waiting for transfers between devices, run(): return (lax.ppermute(value, axes, same), lax.ppermute(value, axes, cross))  468 us
    all_to_all x5, blocking collectives, exchange(): lax.all_to_all(value, 'wide', 0, 0, axis_index_groups=groups, tiled=True)  78.6 us
    ppermute x1, waiting for transfers between devices, relayout_out(): far = exchange(lax.ppermute(given, 'wide', Z_SWAP), OVER_Y)  67.7 us
    all_to_all x4, waiting for transfers between devices, exchange(): lax.all_to_all(value, 'wide', 0, 0, axis_index_groups=groups, tiled=True)  25.9 us
    ppermute x7, starting transfers between devices, swap_cores(): return lax.ppermute(value, 'wide', CORE_SWAP)  23.7 us
    all_to_all x4, starting transfers between devices, exchange(): lax.all_to_all(value, 'wide', 0, 0, axis_index_groups=groups, tiled=True)  23.2 us
  transfers between devices with their start and end apart: 16, of which 12 were waited for; matrix products, arithmetic and copies ran while one was open for 1% of the time, Pallas kernels for 0%

profile of v2, /device:TPU:481, one launch (start us, length us, event | category | flops | bytes accessed | tf_op | source)
XLA Modules:
  0.0 749.5 jit_solution(4779123305307222668)
XLA Ops:
  7.9 2.8 dynamic-slice_bitcast_fusion
  10.9 168.0 %conditional.5 = (bf16[4,128,512]{2,1,0:T(8,128)(2,1)S(1)}, bf16[4,2048,128]{2,1,0:T(8,128)(2,1)}, bf16[4,2048,128]{2,1,0:T(8,128)(2,1)}, bf16[256,2048]{1,0:T(8...) conditional(s32[]{:T(128)} %convert_element_type.80, ...), branch_computations={%region_0.1_spmd, %region_1.2_spmd} | conditional | flops 1310721 | bytes 64029128 | solution.py:305
  11.1 30.2 %all_to_all.57 = bf16[4,2048,128]{2,1,0:T(8,128)(2,1)} all-to-all(bf16[4,2048,128]{2,1,0:T(8,128)(2,1)S(1)} %bitcast.84), channel_id=1, replica_groups={{0,2,4,6},{1,3,5,7},{8,10,12,14},{9,11,13,15},{16,18,20,22},{17,19,21,2..., dimensions={0} | all-to-all | bytes 4194304 | tf_op jit(solution)/shard_map/cond/branch_0_fun/all_to_all | solution.py:38
  41.3 3.0 collective-permute-start.4
  45.1 11.7 %all_to_all.58 = bf16[4,32,2048]{2,1,0:T(8,128)(2,1)S(1)} all-to-all(bf16[4,32,2048]{2,1,0:T(8,128)(2,1)S(1)} %reshape.209), channel_id=1, replica_groups={{0,2,4,6},{1,3,5,7},{8,10,12,14},{9,11,13,15},{16,18,20,22},{17,19,21,2..., dimensions={0} | all-to-all | bytes 1048576 | tf_op jit(solution)/shard_map/cond/branch_0_fun/all_to_all | solution.py:38
  56.8 3.0 collective-permute-start.5
  61.6 6.1 collective-permute-start.7
  67.7 18.6 %all_to_all.59 = bf16[4,1024,128]{2,1,0:T(8,128)(2,1)} all-to-all(bf16[4,1024,128]{2,1,0:T(8,128)(2,1)} %get-tuple-element.365), channel_id=1, replica_groups={{0,16,32,48},{1,17,33,49},{2,18,34,50},{3,19,35,51},{4,20,36,52},{5,21,..., dimensions={0} | all-to-all | bytes 2097152 | tf_op jit(solution)/shard_map/cond/branch_0_fun/all_to_all | solution.py:38
  86.3 67.7 %collective-permute-done.7 = bf16[4,1024,128]{2,1,0:T(8,128)(2,1)} collective-permute-done((bf16[4,1024,128]{2,1,0:T(8,128)(2,1)S(1)}, bf16[4,1024,128]{2,1,0:T(8,128)(2,1)}, u32[]{:S(2)}, u32[]{:S(2)}) %collective-permute-start.7) | collective-permute-done | bytes 1048608 | tf_op jit(solution)/shard_map/cond/branch_0_fun/ppermute | solution.py:59
  153.9 4.2 all-to-all-start.3
  158.2 2.9 collective-permute-start.6
  161.1 11.2 %all-to-all-done.3 = bf16[4,1024,128]{2,1,0:T(8,128)(2,1)} async-done(((bf16[4,1024,128]{2,1,0:T(8,128)(2,1)}), bf16[4,1024,128]{2,1,0:T(8,128)(2,1)}, u32[]{:S(2)}, u32[]{:S(2)}) %all-to-all-start.3) | async-done | bytes 1048608 | tf_op jit(solution)/shard_map/cond/branch_0_fun/all_to_all | solution.py:38
  172.3 3.9 collective-permute-start.8
  178.9 532.0 %while.25 = (s32[]{:T(128)}, bf16[4,128,512]{2,1,0:T(8,128)(2,1)S(1)}, bf16[128,512]{1,0:T(8,128)(2,1)S(1)}, bf16[128,256]{1,0:T(8,128)(2,1)S(1)}, s32[]{:T(128)...) while((s32[]{:T(128)}, ...), condition=%wide.region_11.12_spmd.clone.clone, body=%wide.region_2.11_spmd.clone.clone.sunk | while | flops 1015837 | bytes 12061053 | solution.py:355
  180.1 480.7 %conditional.13 = (bf16[4,128,512]{2,1,0:T(8,128)(2,1)S(1)}) conditional(s32[]{:T(128)} %convert_element_type.116, bf16[4,128,512]{2,1,0:T(8,128)(2,1)S(1)} %get-tuple-element.808, (s32[]{:T(128)}, s32[]{:T(128)}, bf16[128,512]{1,0:T(8,128)(2,1)S(1)}, bf16[4,128,512]{2,1,0:T(8,128)(2,1)S(1)}) %tuple.109), branch_computations={%region_5.5_spmd, %region_6.10_spmd} | conditional | flops 262160 | bytes 4194557 | solution.py:344
  180.1 470.3 %conditional = (bf16[128,512]{1,0:T(8,128)(2,1)}, bf16[128,512]{1,0:T(8,128)(2,1)}) conditional(s32[]{:T(128)} %convert_element_type.66, bf16[128,512]{1,0:T(8,128)(2,1)S(1)} %get-tuple-element.395, bf16[128,512]{1,0:T(8,128)(2,1)S(1)} %get-tuple-element.395), branch_computations={%region_7.6_spmd, %region_8.7_spmd} | conditional | bytes 1048672 | solution.py:339
  182.7 457.1 %collective-permute-done.2 = bf16[128,512]{1,0:T(8,128)(2,1)} collective-permute-done((bf16[128,512]{1,0:T(8,128)(2,1)S(1)}, bf16[128,512]{1,0:T(8,128)(2,1)}, u32[]{:S(2)}, u32[]{:S(2)}) %collective-permute-start.2) | collective-permute-done | bytes 131104 | tf_op jit(solution)/shard_map/while/body/eval_jaxpr/cond/branch_1_fun/cond/branch_1_fun/ppermute | solution.py:328
  639.9 10.5 %collective-permute-done.3 = bf16[128,512]{1,0:T(8,128)(2,1)} collective-permute-done((bf16[128,512]{1,0:T(8,128)(2,1)S(1)}, bf16[128,512]{1,0:T(8,128)(2,1)}, u32[]{:S(2)}, u32[]{:S(2)}) %collective-permute-start.3) | collective-permute-done | bytes 131104 | tf_op jit(solution)/shard_map/while/body/eval_jaxpr/cond/branch_1_fun/cond/branch_1_fun/ppermute | solution.py:328
  650.4 10.4 %conditional.1 = (bf16[4,128,512]{2,1,0:T(8,128)(2,1)S(1)}) conditional(s32[]{:T(128)} %convert_element_type.65, bf16[4,128,512]{2,1,0:T(8,128)(2,1)S(1)} %get-tuple-element.394, (bf16[128,512]{1,0:T(8,128)(2,1)}, bf16[128,512]{1,0:T(8,128)(2,1)}) %conditional), branch_computations={%region_9.8_spmd, %region_10.9_spmd} | conditional | flops 262144 | bytes 3145736 | solution.py:340
  651.4 9.3 %all_to_all.62 = bf16[4,128,512]{2,1,0:T(8,128)(2,1)S(1)} all-to-all(bf16[4,128,512]{2,1,0:T(8,128)(2,1)S(1)} %broadcast_in_dim.41), channel_id=1, replica_groups={{0,16,32,48},{1,17,33,49},{2,18,34,50},{3,19,35,51},{4,20,36,52},{5,21,..., dimensions={0} | all-to-all | bytes 1048576 | tf_op jit(solution)/shard_map/while/body/eval_jaxpr/cond/branch_1_fun/cond/branch_1_fun/all_to_all | solution.py:38
  660.9 50.0 %conditional.12 = ((bf16[128,512]{1,0:T(8,128)(2,1)S(1)}, bf16[128,256]{1,0:T(8,128)(2,1)S(1)})) conditional(s32[]{:T(128)} %convert_element_type.117, (bf16[128,512]{1,0:T(8,128)(2,1)S(1)}, bf16[128,256]{1,0:T(8,128)(2,1)S(1)}) %tuple.107, (s32[]{:T(128)}, s32[]{:T(128)}, bf16[4,128,512]{2,1,0:T(8,128)(2,1)S(1)}, s32[3]{0:T(128)S(1)}, ...), branch_computations={%region_3.3_spmd, %region_4.4_spmd} | conditional | flops 737284 | bytes 7799528 | solution.py:336
  660.9 5.0 project.1
  665.9 3.5 all-to-all-start.9
  669.9 6.8 all-to-all-done.9.part_ref
  678.2 6.3 collective-permute-done.14.first_ref
  686.0 8.8 %all_to_all.61.ctx_ref = bf16[4,128,256]{2,1,0:T(8,128)(2,1)S(1)} all-to-all(bf16[4,128,256]{2,1,0:T(8,128)(2,1)S(1)} %attend.1), channel_id=1, replica_groups={{0,2,4,6},{1,3,5,7},{8,10,12,14},{9,11,13,15},{16,18,20,22},{17,19,21,2..., dimensions={0} | all-to-all | bytes 524288 | tf_op jit(solution)/shard_map/while/body/eval_jaxpr/cond/branch_1_fun/all_to_all | solution.py:38
  694.8 4.5 output.1
  699.2 3.5 all-to-all-start.11
  702.7 7.9 %all-to-all-done.11 = bf16[4,128,512]{2,1,0:T(8,128)(2,1)S(1)} async-done(((bf16[4,128,512]{2,1,0:T(8,128)(2,1)}), bf16[4,128,512]{2,1,0:T(8,128)(2,1)S(1)}, u32[]{:S(2)}, u32[]{:S(2)}) %all-to-all-start.11) | async-done | bytes 524320 | tf_op jit(solution)/shard_map/while/body/eval_jaxpr/cond/branch_1_fun/all_to_all | solution.py:38
  711.8 12.1 %all-to-all-start.13 = ((bf16[8,128,256]{2,1,0:T(8,128)(2,1)}), bf16[8,128,256]{2,1,0:T(8,128)(2,1)S(1)}, u32[]{:S(2)}, u32[]{:S(2)}) async-start(bf16[8,128,256]{2,1,0:T(8,128)(2,1)} %broadcast_in_dim.83), calls=%async_computation.13 | async-start | bytes 1048576 | tf_op jit(solution)/shard_map/all_to_all | solution.py:38
  726.4 11.6 %collective-permute-done.16 = bf16[128,256]{0,1:T(8,128)(2,1)S(1)} collective-permute-done((bf16[128,256]{0,1:T(8,128)(2,1)S(1)}, bf16[128,256]{0,1:T(8,128)(2,1)S(1)}, u32[]{:S(2)}, u32[]{:S(2)}) %collective-permute-start.16) | collective-permute-done | bytes 65568 | tf_op jit(solution)/shard_map/ppermute | solution.py:360
  738.2 6.1 collective-permute-start.17
  (106 shorter events, 28.7 us)
Async XLA Ops:
  1.4 9.4 %collective-permute-start.15 = (bf16[128,128]{1,0:T(8,128)(2,1)S(1)}, bf16[128,128]{1,0:T(8,128)(2,1)S(1)}, u32[]{:S(2)}, u32[]{:S(2)}) collective-permute-start(bf16[128,128]{1,0:T(8,128)(2,1)S(1)} %dynamic-slice_bitcast_fusion.3), channel_id=1, source_target_pairs={{0,1},{1,0},{2,3},{3,2},{4,5},{5,4},{6,7},{7,6},{8,9},{9,8},{10,11... | collective-permute-start | bytes 98312 | tf_op jit(solution)/shard_map/ppermute | solution.py:42
  7.9 3.0 copy-start.7
  7.9 3.0 copy-start
  7.9 3.0 copy-start.5
  10.9 168.0 %copy-start.8 = (f32[128]{0:T(128)S(1)}, f32[128]{0:T(128)}, u32[]{:S(2)}) copy-start(f32[128]{0:T(128)} %get-tuple-element.802) | copy-start | bytes 1540
  10.9 168.0 %copy-start.9 = (f32[128]{0:T(128)S(1)}, f32[128]{0:T(128)}, u32[]{:S(2)}) copy-start(f32[128]{0:T(128)} %add_convert_fusion.2) | copy-start | bytes 1540
  11.1 33.5 %copy-start.6 = (bf16[1,8192,16]{1,2,0:T(8,128)(2,1)S(1)}, bf16[1,8192,16]{1,2,0:T(8,128)(2,1)}, u32[]{:S(2)}) copy-start(bf16[1,8192,16]{1,2,0:T(8,128)(2,1)} %get-tuple-element.361) | copy-start | bytes 786436 | tf_op jit(solution)/shard_map/cond
  41.3 20.3 %collective-permute-start.4 = (bf16[4,2048,128]{2,1,0:T(8,128)(2,1)}, bf16[4,2048,128]{2,1,0:T(8,128)(2,1)}, u32[]{:S(2)}, u32[]{:S(2)}) collective-permute-start(bf16[4,2048,128]{2,1,0:T(8,128)(2,1)} %all_to_all.57), channel_id=1, source_target_pairs={{0,1},{1,0},{2,3},{3,2},{4,5},{5,4},{6,7},{7,6},{8,9},{9,8},{10,11... | collective-permute-start | bytes 6291464 | tf_op jit(solution)/shard_map/cond/branch_0_fun/ppermute | solution.py:42
  56.8 4.5 collective-permute-start.5
  61.6 92.3 %collective-permute-start.7 = (bf16[4,1024,128]{2,1,0:T(8,128)(2,1)S(1)}, bf16[4,1024,128]{2,1,0:T(8,128)(2,1)}, u32[]{:S(2)}, u32[]{:S(2)}) collective-permute-start(bf16[4,1024,128]{2,1,0:T(8,128)(2,1)S(1)} %get-tuple-element.366), channel_id=1, source_target_pairs={{0,8},{1,9},{2,10},{3,11},{4,12},{5,13},{6,14},{7,15},{8,0},{9,1},... | collective-permute-start | bytes 3145736 | tf_op jit(solution)/shard_map/cond/branch_0_fun/ppermute | solution.py:59
  153.9 18.4 %all-to-all-start.3 = ((bf16[4,1024,128]{2,1,0:T(8,128)(2,1)}), bf16[4,1024,128]{2,1,0:T(8,128)(2,1)}, u32[]{:S(2)}, u32[]{:S(2)}) async-start(bf16[4,1024,128]{2,1,0:T(8,128)(2,1)} %collective-permute-done.7), calls=%async_computation.3 | async-start | bytes 2097152 | tf_op jit(solution)/shard_map/cond/branch_0_fun/all_to_all | solution.py:38
  158.2 18.0 %collective-permute-start.6 = (bf16[4,1024,128]{2,1,0:T(8,128)(2,1)}, bf16[4,1024,128]{2,1,0:T(8,128)(2,1)}, u32[]{:S(2)}, u32[]{:S(2)}) collective-permute-start(bf16[4,1024,128]{2,1,0:T(8,128)(2,1)} %all_to_all.59), channel_id=1, source_target_pairs={{0,1},{1,0},{2,3},{3,2},{4,5},{5,4},{6,7},{7,6},{8,9},{9,8},{10,11... | collective-permute-start | bytes 3145736 | tf_op jit(solution)/shard_map/cond/branch_0_fun/ppermute | solution.py:42
  172.3 6.5 collective-permute-start.8
  178.9 545.1 %copy-start.10 = (s32[256,1]{0,1:T(1,128)S(1)}, s32[256,1]{0,1:T(1,128)}, u32[]{:S(2)}) copy-start(s32[256,1]{0,1:T(1,128)} %param.27) | copy-start | bytes 3076
  180.1 459.7 %collective-permute-start.2 = (bf16[128,512]{1,0:T(8,128)(2,1)S(1)}, bf16[128,512]{1,0:T(8,128)(2,1)}, u32[]{:S(2)}, u32[]{:S(2)}) collective-permute-start(bf16[128,512]{1,0:T(8,128)(2,1)S(1)} %param.6), channel_id=1, source_target_pairs={{0,64},{1,65},{2,66},{3,67},{4,68},{5,69},{6,70},{7,71},{8,72},{9,... | collective-permute-start | bytes 393224 | tf_op jit(solution)/shard_map/while/body/eval_jaxpr/cond/branch_1_fun/cond/branch_1_fun/ppermute | solution.py:328
  181.4 469.0 %collective-permute-start.3 = (bf16[128,512]{1,0:T(8,128)(2,1)S(1)}, bf16[128,512]{1,0:T(8,128)(2,1)}, u32[]{:S(2)}, u32[]{:S(2)}) collective-permute-start(bf16[128,512]{1,0:T(8,128)(2,1)S(1)} %param.6), channel_id=1, source_target_pairs={{0,72},{1,73},{2,74},{3,75},{4,76},{5,77},{6,78},{7,79},{8,64},{9,... | collective-permute-start | bytes 393224 | tf_op jit(solution)/shard_map/while/body/eval_jaxpr/cond/branch_1_fun/cond/branch_1_fun/ppermute | solution.py:328
  665.9 10.7 %all-to-all-start.9 = ((bf16[4,144,512]{2,1,0:T(8,128)(2,1)}), bf16[4,144,512]{2,1,0:T(8,128)(2,1)S(1)}, u32[]{:S(2)}, u32[]{:S(2)}) async-start(bf16[4,144,512]{2,1,0:T(8,128)(2,1)} %project.1), calls=%async_computation.9 | async-start | bytes 1179648 | tf_op jit(solution)/shard_map/while/body/eval_jaxpr/cond/branch_1_fun/all_to_all | solution.py:38
  676.9 22.3 %copy-start.1 = (bf16[128,256]{1,0:T(8,128)(2,1)}, bf16[128,256]{1,0:T(8,128)(2,1)S(1)}, u32[]{:S(2)}) copy-start(bf16[128,256]{1,0:T(8,128)(2,1)S(1)} %get-tuple-element.769.own_ref) | copy-start | bytes 196612 | tf_op jit(solution)/shard_map/while/body/eval_jaxpr/cond
  676.9 7.7 %collective-permute-start.14 = (bf16[128,256]{1,0:T(8,128)(2,1)S(1)}, bf16[128,256]{1,0:T(8,128)(2,1)S(1)}, u32[]{:S(2)}, u32[]{:S(2)}) collective-permute-start(bf16[128,256]{1,0:T(8,128)(2,1)S(1)} %get-tuple-element.769.own_ref), channel_id=1, source_target_pairs={{0,1},{2,3},{4,5},{6,7},{8,9},{10,11},{12,13},{14,15},{16,17},{18,... | collective-permute-start | bytes 196616 | tf_op jit(solution)/shard_map/while/body/eval_jaxpr/cond/branch_1_fun/ppermute | solution.py:316
  699.2 11.4 %all-to-all-start.11 = ((bf16[4,128,512]{2,1,0:T(8,128)(2,1)}), bf16[4,128,512]{2,1,0:T(8,128)(2,1)S(1)}, u32[]{:S(2)}, u32[]{:S(2)}) async-start(bf16[4,128,512]{2,1,0:T(8,128)(2,1)} %output.1), calls=%async_computation.11 | async-start | bytes 1048576 | tf_op jit(solution)/shard_map/while/body/eval_jaxpr/cond/branch_1_fun/all_to_all | solution.py:38
  702.7 8.2 %copy-start.2 = (bf16[128,256]{1,0:T(8,128)(2,1)S(1)}, bf16[128,256]{1,0:T(8,128)(2,1)}, u32[]{:S(2)}) copy-start(bf16[128,256]{1,0:T(8,128)(2,1)} %copy-done.1) | copy-start | bytes 196612 | tf_op jit(solution)/shard_map/while/body/eval_jaxpr/cond
  711.8 33.4 %all-to-all-start.13 = ((bf16[8,128,256]{2,1,0:T(8,128)(2,1)}), bf16[8,128,256]{2,1,0:T(8,128)(2,1)S(1)}, u32[]{:S(2)}, u32[]{:S(2)}) async-start(bf16[8,128,256]{2,1,0:T(8,128)(2,1)} %broadcast_in_dim.83), calls=%async_computation.13 | async-start | bytes 1048576 | tf_op jit(solution)/shard_map/all_to_all | solution.py:38
  724.3 13.7 %collective-permute-start.16 = (bf16[128,256]{0,1:T(8,128)(2,1)S(1)}, bf16[128,256]{0,1:T(8,128)(2,1)S(1)}, u32[]{:S(2)}, u32[]{:S(2)}) collective-permute-start(bf16[128,256]{0,1:T(8,128)(2,1)S(1)} %dynamic-slice_bitcast_fusion.2), channel_id=1, source_target_pairs={{0,8},{1,9},{2,10},{3,11},{4,12},{5,13},{6,14},{7,15},{8,0},{9,1},... | collective-permute-start | bytes 196616 | tf_op jit(solution)/shard_map/ppermute | solution.py:360
  738.2 6.9 collective-permute-start.17
  745.6 3.1 collective-permute-start.18

commit v3 on v2

--- a/solution.py
+++ b/solution.py
@@ -16,10 +16,11 @@
 WIDE = NG * NX * NC
 SECTIONS = 8
 HALF = 128
+ITEMS_HERE = NG * HALF // BLOCK
 EPS = 1e-05
 ROPE_BASE = 500000.0
 MASKED = -1e30
-VMEM = 32 * 1024 * 1024
+VMEM = 16 * 1024 * 1024
 
 OVER_X = [[g * 8 + x * 2 + c for x in range(NX)] for g in range(NG) for c in range(NC)]
 OVER_G = [[g * 8 + x * 2 + c for g in range(NG)] for x in range(NX) for c in range(NC)]
@@ -48,23 +49,28 @@
     return jnp.concatenate([first, second], axis=axis)
 
 
-def relayout(weight):
-    rows = weight.reshape(NG, NX, CHIP, HD).transpose(1, 0, 2, 3).reshape(NX, NG * CHIP, HD)
-    mine = exchange(rows, OVER_X)
-    return mine, swap_cores(mine)
-
-
-def relayout_out(kept, given):
-    near = exchange(kept, OVER_Y)
-    far = exchange(lax.ppermute(given, "wide", Z_SWAP), OVER_Y)
-    return near, swap_cores(near), far, swap_cores(far)
-
-
-def relayout_kv(w_key, w_value, core):
+def x_blocks(weight):
+    return weight.reshape(NG, NX, CHIP, HD).transpose(1, 0, 2, 3).reshape(NX, NG * CHIP, HD)
+
+
+def over_y(piece, y):
+    full = None
+    for step in range(NY):
+        block = piece((y + step) % NY)
+        if step == 0:
+            full = jnp.zeros((NY,) + block.shape[1:], block.dtype)
+        else:
+            pairs = [(w, (w + 16 * step) % WIDE) for w in range(WIDE)]
+            block = lax.ppermute(block, "wide", pairs)
+        full = lax.dynamic_update_slice_in_dim(full, block, (y - step) % NY, 0)
+    return full
+
+
+def relayout_kv(w_key, w_value, core, after):
     both = jnp.stack([w_key.T, w_value.T])
     width = both.shape[1]
     both = both.reshape(2, width, NG, NX, CHIP).transpose(3, 0, 1, 2, 4)
-    mine = exchange(both.reshape(NX, 2 * width, NG * CHIP), OVER_X)
+    mine = exchange(after(both.reshape(NX, 2 * width, NG * CHIP)), OVER_X)
     other = swap_cores(mine)
     mine = mine.reshape(NX, 2, 1, width, NG * CHIP)
     other = other.reshape(NX, 2, 1, width, NG * CHIP)
@@ -247,6 +253,20 @@
     )(info, context, *wo)
 
 
+def ranks(placement, core):
+    owners = placement[:, 0]
+    order = jnp.arange(owners.shape[0], dtype=jnp.int32)
+    earlier = (order[None, :] < order[:, None]) & (owners[:, None] == owners[None, :])
+    rank = jnp.sum(earlier.astype(jnp.int32), axis=1)
+    blocks = HALF // BLOCK
+    here = jnp.arange(ITEMS_HERE, dtype=jnp.int32)
+    mine = (core * blocks + here % blocks) * NG + here // blocks
+    match = mine[:, None] == order[None, :]
+    item_owner = jnp.sum(jnp.where(match, owners[None, :], 0), axis=1)
+    item_rank = jnp.sum(jnp.where(match, rank[None, :], 0), axis=1)
+    return item_owner, item_rank
+
+
 def relay_pairs(first):
     same, cross = [], []
     for s in range(first, SECTIONS - 1, 2):
@@ -287,24 +307,43 @@
         return got.transpose(0, 2, 1, 3).reshape(NY, HALF, NZ * CHIP)
 
     out_rows = w_out[0].reshape(NY, NZ, NX * CHIP, HD)
-    kept = lax.dynamic_index_in_dim(out_rows, z, 1, keepdims=False)
     given = lax.dynamic_index_in_dim(out_rows, 1 - z, 1, keepdims=False)
 
-    def first_section(start, kept, given):
-        wq = relayout(w_query[0])
-        wkv = relayout_kv(w_key[0], w_value[0], core)
-        return first_gather(start), wq, wkv, relayout_out(kept, given)
-
-    def later_section(start, kept, given):
-        wq = relayout(w_query[0])
-        wkv = relayout_kv(w_key[0], w_value[0], core)
-        given, wq, wkv = lax.optimization_barrier((given, wq, wkv))
+    def kept(i):
+        block = lax.dynamic_slice(out_rows, (i, z, 0, 0), (1, 1, NX * CHIP, HD))
+        return block.reshape(1, NX * CHIP, HD)
+
+    def prepare(given, before):
+        rows = lax.optimization_barrier((x_blocks(w_query[0]), before))[0]
+        query = exchange(rows, OVER_X)
+        key_value = relayout_kv(
+            w_key[0],
+            w_value[0],
+            core,
+            lambda both: lax.optimization_barrier((both, query))[0],
+        )
+        near = over_y(kept, y)
+        far = given(key_value)
+        far = over_y(lambda i: lax.dynamic_slice_in_dim(far, i, 1, 0), y)
+        out = (near, swap_cores(near), far, swap_cores(far))
+        return (query, swap_cores(query)), key_value, out
+
+    def first_section(start):
+        far = lax.ppermute(given, "wide", Z_SWAP)
+        gathered = first_gather(start)
+        items = jnp.zeros((ITEMS_HERE,), jnp.int32)
+        return gathered, prepare(lambda key_value: far, gathered), (items, items)
+
+    def later_section(start):
+        def far(key_value):
+            return lax.ppermute(
+                lax.optimization_barrier((given, key_value))[0], "wide", Z_SWAP
+            )
+
         blank = jnp.zeros((NY, HALF, NZ * CHIP), jnp.bfloat16)
-        return blank, wq, wkv, relayout_out(kept, given)
-
-    gathered, wq, wkv, wo = lax.cond(
-        segment == 0, first_section, later_section, start, kept, given
-    )
+        return blank, prepare(far, start), ranks(placement, core)
+
+    gathered, (wq, wkv, wo), items = lax.cond(segment == 0, first_section, later_section, start)
 
     def later_gather(same, cross):
         pair = (same.astype(jnp.float32) + cross.astype(jnp.float32)).astype(jnp.bfloat16)
@@ -325,7 +364,7 @@
 
         def run(value):
             axes = ("segment", "wide")
-            return lax.ppermute(value, axes, same), lax.ppermute(value, axes, cross)
+            return lax.ppermute(value, axes, cross), lax.ppermute(value, axes, same)
 
         return run
 
@@ -336,7 +375,7 @@
         partial, kv = lax.cond(segment == t, layer, lambda gathered: (partial, kv), gathered)
 
         def hand_on(partial, gathered):
-            same, cross = lax.cond(t % 2 == 0, even, odd, partial)
+            cross, same = lax.cond(t % 2 == 0, even, odd, partial)
             return lax.cond(
                 segment == t + 1, later_gather, lambda same, cross: gathered, same, cross
             )
@@ -364,18 +403,11 @@
     given = lax.dynamic_index_in_dim(columns, 1 - core, 1, keepdims=False)
     outputs = by_core(core, kept, swap_cores(given), 0)
 
-    owners = placement[:, 0]
-    items = owners.shape[0]
-    order = jnp.arange(items, dtype=jnp.int32)
-    earlier = (order[None, :] < order[:, None]) & (owners[:, None] == owners[None, :])
-    rank = jnp.sum(earlier.astype(jnp.int32), axis=1)
-    slots = 2 * items // WIDE
+    item_owner, item_rank = lax.cond(
+        segment == 0, lambda: ranks(placement, core), lambda: items
+    )
     blocks = HALF // BLOCK
-    by_head = (jnp.arange(2 * blocks)[None, :] * NG + jnp.arange(NG)[:, None]).astype(jnp.int32)
-    mine = lax.dynamic_slice_in_dim(by_head, core * blocks, blocks, 1).reshape(-1)
-    match = mine[:, None] == order[None, :]
-    item_owner = jnp.sum(jnp.where(match, owners[None, :], 0), axis=1)
-    item_rank = jnp.sum(jnp.where(match, rank[None, :], 0), axis=1)
+    slots = 2 * placement.shape[0] // WIDE
     slot = jnp.arange(slots, dtype=jnp.int32)
 
     sent = jnp.broadcast_to(kv[None], (NG, HALF, CHIP))

time: 751 us -> 721 us (0.960)
  blocking collectives: 78.6 us -> 29 us
  starting transfers between devices: 58.7 us -> 81.4 us
  waiting for transfers between devices: 584 us -> 569 us
  local copies, waits for them, and re-layouts: 7.68 us -> 20.8 us
    all_to_all x5 -> x3, blocking collectives: 78.6 us -> 29 us  [exchange(): lax.all_to_all(value, 'wide', 0, 0, axis_index_groups=groups, tiled=True)]
    ppermute x3 -> x9, waiting for transfers between devices: 535 us -> 506 us  [the longest x2 435 us: run(): return (lax.ppermute(value, axes, cross), lax.ppermute(value, axes, same))]
    ppermute x3 -> x9, starting transfers between devices: 8.64 us -> 30.2 us  [the longest x6 21.4 us: over_y(): block = lax.ppermute(block, 'wide', pairs)]
    all_to_all x4, waiting for transfers between devices: 25.9 us -> 40.5 us  [exchange(): lax.all_to_all(value, 'wide', 0, 0, axis_index_groups=groups, tiled=True)]
  transfers between devices with their start and end apart: 16 -> 22, of which waited for: 12 -> 11; matrix products, arithmetic and copies ran while one was open for 1% -> 3% of each run, Pallas kernels for 0% -> 0%
where the time goes in v3:
time: 721 us; the launch traced here: 719 us
  waiting for transfers between devices  569 us (79%)
  starting transfers between devices  81.4 us (11%)
  blocking collectives  29 us (4%)
  local copies, waits for them, and re-layouts  20.8 us (3%)
  Pallas kernels  11.1 us (2%)
    ppermute x2, waiting for transfers between devices, run(): return (lax.ppermute(value, axes, cross), lax.ppermute(value, axes, same))  435 us
    ppermute x1, waiting for transfers between devices, far(): lax.ppermute(lax.optimization_barrier((given, key_value))[0], 'wide', Z_S...  70.3 us
    all_to_all x4, waiting for transfers between devices, exchange(): lax.all_to_all(value, 'wide', 0, 0, axis_index_groups=groups, tiled=True)  40.5 us
    all_to_all x3, blocking collectives, exchange(): lax.all_to_all(value, 'wide', 0, 0, axis_index_groups=groups, tiled=True)  29 us
    ppermute x7, starting transfers between devices, swap_cores(): return lax.ppermute(value, 'wide', CORE_SWAP)  24.5 us
    all_to_all x4, starting transfers between devices, exchange(): lax.all_to_all(value, 'wide', 0, 0, axis_index_groups=groups, tiled=True)  23.5 us
    ppermute x6, starting transfers between devices, over_y(): block = lax.ppermute(block, 'wide', pairs)  21.4 us
  transfers between devices with their start and end apart: 22, of which 11 were waited for; matrix products, arithmetic and copies ran while one was open for 3% of the time, Pallas kernels for 0%

profile of v3, /device:TPU:481, one launch (start us, length us, event | category | flops | bytes accessed | tf_op | source)
XLA Modules:
  0.0 719.3 jit_solution(10745441699117560957)
XLA Ops:
  9.5 171.9 %conditional.6 = (bf16[4,128,512]{2,1,0:T(8,128)(2,1)S(1)}, bf16[4,2048,128]{2,1,0:T(8,128)(2,1)}, bf16[4,2048,128]{2,1,0:T(8,128)(2,1)}, bf16[256,2048]{1,0:T(8...) conditional(s32[]{:T(128)} %convert_element_type.84, ...), branch_computations={%region_0.4_spmd, %region_4.5_spmd} | conditional | flops 1803757 | bytes 76090160 | solution.py:346
  11.0 4.5 all-to-all-start
  16.2 25.8 %all-to-all-done = bf16[4,2048,128]{2,1,0:T(8,128)(2,1)} async-done(((bf16[4,2048,128]{2,1,0:T(8,128)(2,1)}), bf16[4,2048,128]{2,1,0:T(8,128)(2,1)}, u32[]{:S(2)}, u32[]{:S(2)}) %all-to-all-start) | async-done | bytes 2097184 | tf_op jit(solution)/shard_map/cond/branch_0_fun/all_to_all | solution.py:39
  42.0 10.9 %all_to_all.41 = bf16[4,32,2048]{2,1,0:T(8,128)(2,1)S(1)} all-to-all(bf16[4,32,2048]{2,1,0:T(8,128)(2,1)S(1)} %reshape.263), channel_id=1, replica_groups={{0,2,4,6},{1,3,5,7},{8,10,12,14},{9,11,13,15},{16,18,20,22},{17,19,21,2..., dimensions={0} | all-to-all | bytes 1048576 | tf_op jit(solution)/shard_map/cond/branch_0_fun/all_to_all | solution.py:39
  52.9 3.8 collective-permute-start.5
  58.5 6.2 collective-permute-start.10
  68.3 3.2 collective-permute-start.6
  71.5 4.5 collective-permute-start.7
  76.0 3.0 collective-permute-start.8
  80.9 70.3 %collective-permute-done.10 = bf16[4,1024,128]{2,1,0:T(8,128)(2,1)} collective-permute-done((bf16[4,1024,128]{2,1,0:T(8,128)(2,1)}, bf16[4,1024,128]{2,1,0:T(8,128)(2,1)}, u32[]{:S(2)}, u32[]{:S(2)}) %collective-permute-start.10) | collective-permute-done | bytes 1048608 | tf_op jit(solution)/shard_map/cond/branch_0_fun/ppermute | solution.py:339
  154.3 3.2 collective-permute-start.11
  159.2 4.5 collective-permute-start.12
  169.2 3.5 collective-permute-start.9
  174.9 3.8 collective-permute-start.14
  181.4 499.7 %while.25 = (s32[]{:T(128)}, bf16[4,128,512]{2,1,0:T(8,128)(2,1)S(1)}, bf16[128,512]{1,0:T(8,128)(2,1)S(1)}, bf16[128,256]{1,0:T(8,128)(2,1)S(1)}, s32[]{:T(128)...) while((s32[]{:T(128)}, ...), condition=%wide.region_14.15_spmd.clone.clone, body=%wide.region_5.14_spmd.clone.clone.sunk | while | flops 1015837 | bytes 12061069 | solution.py:394
  182.6 448.4 %conditional.15 = (bf16[4,128,512]{2,1,0:T(8,128)(2,1)S(1)}) conditional(s32[]{:T(128)} %convert_element_type.120, bf16[4,128,512]{2,1,0:T(8,128)(2,1)S(1)} %get-tuple-element.870, (s32[]{:T(128)}, s32[]{:T(128)}, bf16[128,512]{1,0:T(8,128)(2,1)S(1)}, bf16[4,128,512]{2,1,0:T(8,128)(2,1)S(1)}) %tuple.133), branch_computations={%region_8.8_spmd, %region_9.13_spmd} | conditional | flops 262160 | bytes 4194573 | solution.py:383
  182.6 438.0 %conditional = (bf16[128,512]{1,0:T(8,128)(2,1)}, bf16[128,512]{1,0:T(8,128)(2,1)}) conditional(s32[]{:T(128)} %convert_element_type.70, bf16[128,512]{1,0:T(8,128)(2,1)S(1)} %get-tuple-element.419, bf16[128,512]{1,0:T(8,128)(2,1)S(1)} %get-tuple-element.419), branch_computations={%region_10.9_spmd, %region_11.10_spmd} | conditional | bytes 1048672 | solution.py:378
  185.2 435.4 %collective-permute-done.2 = bf16[128,512]{1,0:T(8,128)(2,1)} collective-permute-done((bf16[128,512]{1,0:T(8,128)(2,1)S(1)}, bf16[128,512]{1,0:T(8,128)(2,1)}, u32[]{:S(2)}, u32[]{:S(2)}) %collective-permute-start.2) | collective-permute-done | bytes 131104 | tf_op jit(solution)/shard_map/while/body/eval_jaxpr/cond/branch_1_fun/cond/branch_1_fun/ppermute | solution.py:367
  620.6 10.4 %conditional.1 = (bf16[4,128,512]{2,1,0:T(8,128)(2,1)S(1)}) conditional(s32[]{:T(128)} %convert_element_type.69, bf16[4,128,512]{2,1,0:T(8,128)(2,1)S(1)} %get-tuple-element.418, (bf16[128,512]{1,0:T(8,128)(2,1)}, bf16[128,512]{1,0:T(8,128)(2,1)}) %tuple.60), branch_computations={%region_12.11_spmd, %region_13.12_spmd} | conditional | flops 262144 | bytes 3145736 | solution.py:379
  621.6 9.3 %all_to_all.43 = bf16[4,128,512]{2,1,0:T(8,128)(2,1)S(1)} all-to-all(bf16[4,128,512]{2,1,0:T(8,128)(2,1)S(1)} %broadcast_in_dim.83), channel_id=1, replica_groups={{0,16,32,48},{1,17,33,49},{2,18,34,50},{3,19,35,51},{4,20,36,52},{5,21,..., dimensions={0} | all-to-all | bytes 1048576 | tf_op jit(solution)/shard_map/while/body/eval_jaxpr/cond/branch_1_fun/cond/branch_1_fun/all_to_all | solution.py:39
  631.1 49.9 %conditional.14 = ((bf16[128,512]{1,0:T(8,128)(2,1)S(1)}, bf16[128,256]{1,0:T(8,128)(2,1)S(1)})) conditional(s32[]{:T(128)} %convert_element_type.121, (bf16[128,512]{1,0:T(8,128)(2,1)S(1)}, bf16[128,256]{1,0:T(8,128)(2,1)S(1)}) %tuple.131, (s32[]{:T(128)}, s32[]{:T(128)}, bf16[4,128,512]{2,1,0:T(8,128)(2,1)S(1)}, s32[3]{0:T(128)S(1)}, ...), branch_computations={%region_6.6_spmd, %region_7.7_spmd} | conditional | flops 737284 | bytes 7799528 | solution.py:375
  631.1 5.0 project.1
  636.1 3.5 all-to-all-start.5
  640.0 6.8 all-to-all-done.5.part_ref
  648.4 6.3 collective-permute-done.26.first_ref
  656.2 8.8 %all_to_all.42.ctx_ref = bf16[4,128,256]{2,1,0:T(8,128)(2,1)S(1)} all-to-all(bf16[4,128,256]{2,1,0:T(8,128)(2,1)S(1)} %attend.1), channel_id=1, replica_groups={{0,2,4,6},{1,3,5,7},{8,10,12,14},{9,11,13,15},{16,18,20,22},{17,19,21,2..., dimensions={0} | all-to-all | bytes 524288 | tf_op jit(solution)/shard_map/while/body/eval_jaxpr/cond/branch_1_fun/all_to_all | solution.py:39
  664.9 4.4 output.1
  669.4 3.5 all-to-all-start.7
  672.9 7.9 %all-to-all-done.7 = bf16[4,128,512]{2,1,0:T(8,128)(2,1)S(1)} async-done(((bf16[4,128,512]{2,1,0:T(8,128)(2,1)}), bf16[4,128,512]{2,1,0:T(8,128)(2,1)S(1)}, u32[]{:S(2)}, u32[]{:S(2)}) %all-to-all-start.7) | async-done | bytes 524320 | tf_op jit(solution)/shard_map/while/body/eval_jaxpr/cond/branch_1_fun/all_to_all | solution.py:39
  682.0 12.1 %all-to-all-start.9 = ((bf16[8,128,256]{2,1,0:T(8,128)(2,1)}), bf16[8,128,256]{2,1,0:T(8,128)(2,1)S(1)}, u32[]{:S(2)}, u32[]{:S(2)}) async-start(bf16[8,128,256]{2,1,0:T(8,128)(2,1)} %broadcast_in_dim.99), calls=%async_computation.9 | async-start | bytes 1048576 | tf_op jit(solution)/shard_map/all_to_all | solution.py:39
  696.1 11.8 %collective-permute-done.28 = bf16[128,256]{0,1:T(8,128)(2,1)S(1)} collective-permute-done((bf16[128,256]{0,1:T(8,128)(2,1)S(1)}, bf16[128,256]{0,1:T(8,128)(2,1)S(1)}, u32[]{:S(2)}, u32[]{:S(2)}) %collective-permute-start.28) | collective-permute-done | bytes 65568 | tf_op jit(solution)/shard_map/ppermute | solution.py:399
  708.0 6.1 collective-permute-start.29
  (123 shorter events, 48.7 us)
Async XLA Ops:
  0.6 8.7 %copy-start.9 = (bf16[256,128]{1,0:T(8,128)(2,1)S(1)}, bf16[256,128]{1,0:T(8,128)(2,1)}, u32[]{:S(2)}) copy-start(bf16[256,128]{1,0:T(8,128)(2,1)} %param.22) | copy-start | bytes 196612
  0.6 8.8 %copy-start = (bf16[1,8192,128]{2,1,0:T(8,128)(2,1)S(1)}, bf16[1,8192,128]{2,1,0:T(8,128)(2,1)}, u32[]{:S(2)}) copy-start(bf16[1,8192,128]{2,1,0:T(8,128)(2,1)} %param.24) | copy-start | bytes 6291460
  0.7 8.8 %copy-start.5 = (bf16[1,8192,16]{1,2,0:T(8,128)(2,1)S(1)}, bf16[1,8192,16]{1,2,0:T(8,128)(2,1)}, u32[]{:S(2)}) copy-start(bf16[1,8192,16]{1,2,0:T(8,128)(2,1)} %param.25) | copy-start | bytes 786436
  0.7 8.8 %copy-start.6 = (bf16[1,8192,16]{1,2,0:T(8,128)(2,1)S(1)}, bf16[1,8192,16]{1,2,0:T(8,128)(2,1)}, u32[]{:S(2)}) copy-start(bf16[1,8192,16]{1,2,0:T(8,128)(2,1)} %param.26) | copy-start | bytes 786436
  0.7 8.8 %copy-start.10 = (s32[256,1]{0,1:T(1,128)S(1)}, s32[256,1]{0,1:T(1,128)}, u32[]{:S(2)}) copy-start(s32[256,1]{0,1:T(1,128)} %param.29) | copy-start | bytes 3076
  1.6 7.8 %collective-permute-start.27 = (bf16[128,128]{1,0:T(8,128)(2,1)S(1)}, bf16[128,128]{1,0:T(8,128)(2,1)S(1)}, u32[]{:S(2)}, u32[]{:S(2)}) collective-permute-start(bf16[128,128]{1,0:T(8,128)(2,1)S(1)} %dynamic-slice_bitcast_fusion.8), channel_id=1, source_target_pairs={{0,1},{1,0},{2,3},{3,2},{4,5},{5,4},{6,7},{7,6},{8,9},{9,8},{10,11... | collective-permute-start | bytes 98312 | tf_op jit(solution)/shard_map/ppermute | solution.py:43
  11.0 31.0 %all-to-all-start = ((bf16[4,2048,128]{2,1,0:T(8,128)(2,1)}), bf16[4,2048,128]{2,1,0:T(8,128)(2,1)}, u32[]{:S(2)}, u32[]{:S(2)}) async-start(bf16[4,2048,128]{2,1,0:T(8,128)(2,1)} %bitcast.95), calls=%async_computation | async-start | bytes 4194304 | tf_op jit(solution)/shard_map/cond/branch_0_fun/all_to_all | solution.py:39
  52.9 5.3 collective-permute-start.5
  58.3 9.0 %copy-start.1 = (bf16[4,2,1024,128]{3,2,1,0:T(8,128)(2,1)S(1)}, bf16[4,2,1024,128]{3,2,1,0:T(8,128)(2,1)}, u32[]{:S(2)}) copy-start(bf16[4,2,1024,128]{3,2,1,0:T(8,128)(2,1)} %get-tuple-element.381) | copy-start | bytes 6291460 | tf_op jit(solution)/shard_map/cond
  58.5 92.7 %collective-permute-start.10 = (bf16[4,1024,128]{2,1,0:T(8,128)(2,1)}, bf16[4,1024,128]{2,1,0:T(8,128)(2,1)}, u32[]{:S(2)}, u32[]{:S(2)}) collective-permute-start(bf16[4,1024,128]{2,1,0:T(8,128)(2,1)} %get-tuple-element.385), channel_id=1, source_target_pairs={{0,8},{1,9},{2,10},{3,11},{4,12},{5,13},{6,14},{7,15},{8,0},{9,1},... | collective-permute-start | bytes 3145736 | tf_op jit(solution)/shard_map/cond/branch_0_fun/ppermute | solution.py:339
  64.8 114.3 %collective-permute-start.4 = (bf16[4,2048,128]{2,1,0:T(8,128)(2,1)}, bf16[4,2048,128]{2,1,0:T(8,128)(2,1)}, u32[]{:S(2)}, u32[]{:S(2)}) collective-permute-start(bf16[4,2048,128]{2,1,0:T(8,128)(2,1)} %all-to-all-done), channel_id=1, source_target_pairs={{0,1},{1,0},{2,3},{3,2},{4,5},{5,4},{6,7},{7,6},{8,9},{9,8},{10,11... | collective-permute-start | bytes 6291464 | tf_op jit(solution)/shard_map/cond/branch_0_fun/ppermute | solution.py:43
  68.3 89.2 %collective-permute-start.6 = (bf16[1,1024,128]{2,1,0:T(8,128)(2,1)}, bf16[1,1024,128]{2,1,0:T(8,128)(2,1)}, u32[]{:S(2)}, u32[]{:S(2)}) collective-permute-start(bf16[1,1024,128]{2,1,0:T(8,128)(2,1)} %get-tuple-element.675), channel_id=1, source_target_pairs={{0,16},{1,17},{2,18},{3,19},{4,20},{5,21},{6,22},{7,23},{8,24},{9,... | collective-permute-start | bytes 786440 | tf_op jit(solution)/shard_map/cond/branch_0_fun/ppermute | solution.py:64
  71.5 92.3 %collective-permute-start.7 = (bf16[1,1024,128]{2,1,0:T(8,128)(2,1)}, bf16[1,1024,128]{2,1,0:T(8,128)(2,1)}, u32[]{:S(2)}, u32[]{:S(2)}) collective-permute-start(bf16[1,1024,128]{2,1,0:T(8,128)(2,1)} %get-tuple-element.674), channel_id=1, source_target_pairs={{0,32},{1,33},{2,34},{3,35},{4,36},{5,37},{6,38},{7,39},{8,40},{9,... | collective-permute-start | bytes 786440 | tf_op jit(solution)/shard_map/cond/branch_0_fun/ppermute | solution.py:64
  76.0 92.4 %collective-permute-start.8 = (bf16[1,1024,128]{2,1,0:T(8,128)(2,1)}, bf16[1,1024,128]{2,1,0:T(8,128)(2,1)S(1)}, u32[]{:S(2)}, u32[]{:S(2)}) collective-permute-start(bf16[1,1024,128]{2,1,0:T(8,128)(2,1)} %get-tuple-element.673), channel_id=1, source_target_pairs={{0,48},{1,49},{2,50},{3,51},{4,52},{5,53},{6,54},{7,55},{8,56},{9,... | collective-permute-start | bytes 786440 | tf_op jit(solution)/shard_map/cond/branch_0_fun/ppermute | solution.py:64
  154.3 18.4 %collective-permute-start.11 = (bf16[1,1024,128]{2,1,0:T(8,128)(2,1)S(1)}, bf16[1,1024,128]{2,1,0:T(8,128)(2,1)S(1)}, u32[]{:S(2)}, u32[]{:S(2)}) collective-permute-start(bf16[1,1024,128]{2,1,0:T(8,128)(2,1)S(1)} %get-tuple-element.678), channel_id=1, source_target_pairs={{0,16},{1,17},{2,18},{3,19},{4,20},{5,21},{6,22},{7,23},{8,24},{9,... | collective-permute-start | bytes 786440 | tf_op jit(solution)/shard_map/cond/branch_0_fun/ppermute | solution.py:64
  159.2 14.2 %collective-permute-start.12 = (bf16[1,1024,128]{2,1,0:T(8,128)(2,1)S(1)}, bf16[1,1024,128]{2,1,0:T(8,128)(2,1)S(1)}, u32[]{:S(2)}, u32[]{:S(2)}) collective-permute-start(bf16[1,1024,128]{2,1,0:T(8,128)(2,1)S(1)} %get-tuple-element.677), channel_id=1, source_target_pairs={{0,32},{1,33},{2,34},{3,35},{4,36},{5,37},{6,38},{7,39},{8,40},{9,... | collective-permute-start | bytes 786440 | tf_op jit(solution)/shard_map/cond/branch_0_fun/ppermute | solution.py:64
  165.5 8.7 %collective-permute-start.13 = (bf16[1,1024,128]{2,1,0:T(8,128)(2,1)S(1)}, bf16[1,1024,128]{2,1,0:T(8,128)(2,1)S(1)}, u32[]{:S(2)}, u32[]{:S(2)}) collective-permute-start(bf16[1,1024,128]{2,1,0:T(8,128)(2,1)S(1)} %get-tuple-element.676), channel_id=1, source_target_pairs={{0,48},{1,49},{2,50},{3,51},{4,52},{5,53},{6,54},{7,55},{8,56},{9,... | collective-permute-start | bytes 786440 | tf_op jit(solution)/shard_map/cond/branch_0_fun/ppermute | solution.py:64
  169.2 9.9 %collective-permute-start.9 = (bf16[4,1024,128]{2,1,0:T(8,128)(2,1)}, bf16[4,1024,128]{2,1,0:T(8,128)(2,1)}, u32[]{:S(2)}, u32[]{:S(2)}) collective-permute-start(bf16[4,1024,128]{2,1,0:T(8,128)(2,1)} %constant_dynamic-update-slice_fusion.3), channel_id=1, source_target_pairs={{0,1},{1,0},{2,3},{3,2},{4,5},{5,4},{6,7},{7,6},{8,9},{9,8},{10,11... | collective-permute-start | bytes 3145736 | tf_op jit(solution)/shard_map/cond/branch_0_fun/ppermute | solution.py:43
  174.9 6.4 collective-permute-start.14
  182.6 438.0 %collective-permute-start.2 = (bf16[128,512]{1,0:T(8,128)(2,1)S(1)}, bf16[128,512]{1,0:T(8,128)(2,1)}, u32[]{:S(2)}, u32[]{:S(2)}) collective-permute-start(bf16[128,512]{1,0:T(8,128)(2,1)S(1)} %param.6), channel_id=1, source_target_pairs={{0,72},{1,73},{2,74},{3,75},{4,76},{5,77},{6,78},{7,79},{8,64},{9,... | collective-permute-start | bytes 393224 | tf_op jit(solution)/shard_map/while/body/eval_jaxpr/cond/branch_1_fun/cond/branch_1_fun/ppermute | solution.py:367
  183.9 436.7 %collective-permute-start.3 = (bf16[128,512]{1,0:T(8,128)(2,1)S(1)}, bf16[128,512]{1,0:T(8,128)(2,1)}, u32[]{:S(2)}, u32[]{:S(2)}) collective-permute-start(bf16[128,512]{1,0:T(8,128)(2,1)S(1)} %param.6), channel_id=1, source_target_pairs={{0,64},{1,65},{2,66},{3,67},{4,68},{5,69},{6,70},{7,71},{8,72},{9,... | collective-permute-start | bytes 393224 | tf_op jit(solution)/shard_map/while/body/eval_jaxpr/cond/branch_1_fun/cond/branch_1_fun/ppermute | solution.py:367
  636.1 10.7 %all-to-all-start.5 = ((bf16[4,144,512]{2,1,0:T(8,128)(2,1)}), bf16[4,144,512]{2,1,0:T(8,128)(2,1)S(1)}, u32[]{:S(2)}, u32[]{:S(2)}) async-start(bf16[4,144,512]{2,1,0:T(8,128)(2,1)} %project.1), calls=%async_computation.5 | async-start | bytes 1179648 | tf_op jit(solution)/shard_map/while/body/eval_jaxpr/cond/branch_1_fun/all_to_all | solution.py:39
  647.1 22.3 %copy-start.3 = (bf16[128,256]{1,0:T(8,128)(2,1)}, bf16[128,256]{1,0:T(8,128)(2,1)S(1)}, u32[]{:S(2)}) copy-start(bf16[128,256]{1,0:T(8,128)(2,1)S(1)} %get-tuple-element.827.own_ref) | copy-start | bytes 196612 | tf_op jit(solution)/shard_map/while/body/eval_jaxpr/cond
  647.1 7.6 %collective-permute-start.26 = (bf16[128,256]{1,0:T(8,128)(2,1)S(1)}, bf16[128,256]{1,0:T(8,128)(2,1)S(1)}, u32[]{:S(2)}, u32[]{:S(2)}) collective-permute-start(bf16[128,256]{1,0:T(8,128)(2,1)S(1)} %get-tuple-element.827.own_ref), channel_id=1, source_target_pairs={{0,1},{2,3},{4,5},{6,7},{8,9},{10,11},{12,13},{14,15},{16,17},{18,... | collective-permute-start | bytes 196616 | tf_op jit(solution)/shard_map/while/body/eval_jaxpr/cond/branch_1_fun/ppermute | solution.py:355
  669.4 11.4 %all-to-all-start.7 = ((bf16[4,128,512]{2,1,0:T(8,128)(2,1)}), bf16[4,128,512]{2,1,0:T(8,128)(2,1)S(1)}, u32[]{:S(2)}, u32[]{:S(2)}) async-start(bf16[4,128,512]{2,1,0:T(8,128)(2,1)} %output.1), calls=%async_computation.7 | async-start | bytes 1048576 | tf_op jit(solution)/shard_map/while/body/eval_jaxpr/cond/branch_1_fun/all_to_all | solution.py:39
  672.8 8.2 %copy-start.4 = (bf16[128,256]{1,0:T(8,128)(2,1)S(1)}, bf16[128,256]{1,0:T(8,128)(2,1)}, u32[]{:S(2)}) copy-start(bf16[128,256]{1,0:T(8,128)(2,1)} %copy-done.3) | copy-start | bytes 196612 | tf_op jit(solution)/shard_map/while/body/eval_jaxpr/cond
  682.0 33.0 %all-to-all-start.9 = ((bf16[8,128,256]{2,1,0:T(8,128)(2,1)}), bf16[8,128,256]{2,1,0:T(8,128)(2,1)S(1)}, u32[]{:S(2)}, u32[]{:S(2)}) async-start(bf16[8,128,256]{2,1,0:T(8,128)(2,1)} %broadcast_in_dim.99), calls=%async_computation.9 | async-start | bytes 1048576 | tf_op jit(solution)/shard_map/all_to_all | solution.py:39
  694.2 13.7 %collective-permute-start.28 = (bf16[128,256]{0,1:T(8,128)(2,1)S(1)}, bf16[128,256]{0,1:T(8,128)(2,1)S(1)}, u32[]{:S(2)}, u32[]{:S(2)}) collective-permute-start(bf16[128,256]{0,1:T(8,128)(2,1)S(1)} %dynamic-slice_bitcast_fusion.7), channel_id=1, source_target_pairs={{0,8},{1,9},{2,10},{3,11},{4,12},{5,13},{6,14},{7,15},{8,0},{9,1},... | collective-permute-start | bytes 196616 | tf_op jit(solution)/shard_map/ppermute | solution.py:399
  708.0 6.9 collective-permute-start.29
  715.4 3.1 collective-permute-start.30

commit v4 on v3

--- a/solution.py
+++ b/solution.py
@@ -23,6 +23,9 @@
 VMEM = 16 * 1024 * 1024
 
 OVER_X = [[g * 8 + x * 2 + c for x in range(NX)] for g in range(NG) for c in range(NC)]
+OVER_XZ = [
+    [y * 16 + m * 2 + c for m in range(NZ * NX)] for y in range(NY) for c in range(NC)
+]
 OVER_G = [[g * 8 + x * 2 + c for g in range(NG)] for x in range(NX) for c in range(NC)]
 OVER_Y = [
     [(y * 2 + z) * 8 + x * 2 + c for y in range(NY)]
@@ -31,6 +34,7 @@
     for c in range(NC)
 ]
 Z_SWAP = [(w, w ^ 8) for w in range(WIDE)]
+LAST_TO_FIRST = [((SECTIONS - 1) * WIDE + w, w ^ 8) for w in range(WIDE)]
 CORE_SWAP = [(w, w ^ 1) for w in range(WIDE)]
 CORE_UP = [(w, w + 1) for w in range(0, WIDE, 2)]
 
@@ -51,19 +55,6 @@
 
 def x_blocks(weight):
     return weight.reshape(NG, NX, CHIP, HD).transpose(1, 0, 2, 3).reshape(NX, NG * CHIP, HD)
-
-
-def over_y(piece, y):
-    full = None
-    for step in range(NY):
-        block = piece((y + step) % NY)
-        if step == 0:
-            full = jnp.zeros((NY,) + block.shape[1:], block.dtype)
-        else:
-            pairs = [(w, (w + 16 * step) % WIDE) for w in range(WIDE)]
-            block = lax.ppermute(block, "wide", pairs)
-        full = lax.dynamic_update_slice_in_dim(full, block, (y - step) % NY, 0)
-    return full
 
 
 def relayout_kv(w_key, w_value, core, after):
@@ -217,37 +208,42 @@
     )(info, query, own, first)
 
 
-def output_kernel(info_ref, ctx_ref, near_ref, near_other, far_ref, far_other, out_ref, rows):
+def output_kernel(halves, info_ref, ctx_ref, own_ref, other_ref, out_ref, rows):
+    depth = rows.shape[1]
+
     @pl.when(pl.program_id(0) == 0)
     def _():
-        for x in range(NX):
-            rows[:, x * CHIP : (x + 1) * CHIP] = ctx_ref[x]
+        for i in range(depth // CHIP):
+            rows[:, i * CHIP : (i + 1) * CHIP] = ctx_ref[i]
 
     core, z = info_ref[0], info_ref[2]
-    for half, pair in ((z, (near_ref, near_other)), (1 - z, (far_ref, far_other))):
-        weight = jnp.concatenate([pair[0][0], pair[1][0]], axis=1)
-        part = jnp.dot(rows[...], weight, preferred_element_type=jnp.float32).astype(jnp.bfloat16)
-        out_ref[0, :, aligned(half * NC + core)] = part[:, :HD]
-        out_ref[0, :, aligned(half * NC + 1 - core)] = part[:, HD:]
+    for part in range(halves):
+        cut = slice(part * depth, (part + 1) * depth)
+        weight = jnp.concatenate([own_ref[0, cut], other_ref[0, cut]], axis=1)
+        total = jnp.dot(rows[...], weight, preferred_element_type=jnp.float32)
+        total = total.astype(jnp.bfloat16)
+        first = (z if part == 0 else 1 - z) * NC if halves > 1 else 0
+        out_ref[0, :, aligned(first + core)] = total[:, :HD]
+        out_ref[0, :, aligned(first + 1 - core)] = total[:, HD:]
 
 
 def output(info, context, wo):
-    rows = NX * CHIP
+    count = context.shape[0]
+    halves = NG // count
+    rows = NG * CHIP
     block = pl.BlockSpec((1, rows, HD), lambda i: (i, 0, 0))
     return pl.pallas_call(
-        output_kernel,
+        functools.partial(output_kernel, halves),
         grid=(NY,),
         in_specs=[
             pl.BlockSpec(memory_space=pltpu.SMEM),
-            pl.BlockSpec((NX, HALF, CHIP), lambda i: (0, 0, 0)),
-            block,
-            block,
+            pl.BlockSpec((count, HALF, CHIP), lambda i: (0, 0, 0)),
             block,
             block,
         ],
-        out_specs=pl.BlockSpec((1, HALF, NZ * CHIP), lambda i: (i, 0, 0)),
-        out_shape=jax.ShapeDtypeStruct((NY, HALF, NZ * CHIP), jnp.bfloat16),
-        scratch_shapes=[pltpu.VMEM((HALF, rows), jnp.bfloat16)],
+        out_specs=pl.BlockSpec((1, HALF, halves * CHIP), lambda i: (i, 0, 0)),
+        out_shape=jax.ShapeDtypeStruct((NY, HALF, halves * CHIP), jnp.bfloat16),
+        scratch_shapes=[pltpu.VMEM((HALF, count * CHIP), jnp.bfloat16)],
         compiler_params=pltpu.CompilerParams(vmem_limit_bytes=VMEM),
         name="output",
     )(info, context, *wo)
@@ -301,19 +297,13 @@
     sin = jnp.where(lane[None, :] % 2 == 0, -1.0, 1.0) * jnp.sin(angle)
     info = jnp.stack([core, length[0], z]).astype(jnp.int32)
 
-    def first_gather(value):
-        sent = jnp.broadcast_to(value[None], (NG, HALF, CHIP))
-        got = exchange(sent, OVER_G).reshape(NY, NZ, HALF, CHIP)
-        return got.transpose(0, 2, 1, 3).reshape(NY, HALF, NZ * CHIP)
-
-    out_rows = w_out[0].reshape(NY, NZ, NX * CHIP, HD)
-    given = lax.dynamic_index_in_dim(out_rows, 1 - z, 1, keepdims=False)
-
-    def kept(i):
-        block = lax.dynamic_slice(out_rows, (i, z, 0, 0), (1, 1, NX * CHIP, HD))
-        return block.reshape(1, NX * CHIP, HD)
-
-    def prepare(given, before):
+    def gather(pair):
+        return exchange(jnp.broadcast_to(pair[None], (NY, HALF, NZ * CHIP)), OVER_Y)
+
+    cross = lax.ppermute(start, ("segment", "wide"), LAST_TO_FIRST)
+    raw = w_out[0].reshape(NY, NZ * NX * CHIP, HD)
+
+    def prepare(before, out_rows):
         rows = lax.optimization_barrier((x_blocks(w_query[0]), before))[0]
         query = exchange(rows, OVER_X)
         key_value = relayout_kv(
@@ -322,42 +312,60 @@
             core,
             lambda both: lax.optimization_barrier((both, query))[0],
         )
-        near = over_y(kept, y)
-        far = given(key_value)
-        far = over_y(lambda i: lax.dynamic_slice_in_dim(far, i, 1, 0), y)
-        out = (near, swap_cores(near), far, swap_cores(far))
-        return (query, swap_cores(query)), key_value, out
-
-    def first_section(start):
+        out = exchange(lax.optimization_barrier((out_rows, key_value))[0], OVER_Y)
+        return (query, swap_cores(query)), key_value, (out, swap_cores(out))
+
+    def first_section(start, cross):
+        pair = jnp.where(
+            z == 0,
+            jnp.concatenate([start, cross], axis=1),
+            jnp.concatenate([cross, start], axis=1),
+        )
+        gathered = gather(pair)
+        items = jnp.zeros((ITEMS_HERE,), jnp.int32)
+        return gathered, prepare(gathered, raw), (items, items)
+
+    def later_section(start, cross):
+        halves = raw.reshape(NY, NZ, NX * CHIP, HD)
+        kept = lax.dynamic_index_in_dim(halves, z, 1, keepdims=False)
+        given = lax.dynamic_index_in_dim(halves, 1 - z, 1, keepdims=False)
         far = lax.ppermute(given, "wide", Z_SWAP)
-        gathered = first_gather(start)
-        items = jnp.zeros((ITEMS_HERE,), jnp.int32)
-        return gathered, prepare(lambda key_value: far, gathered), (items, items)
-
-    def later_section(start):
-        def far(key_value):
-            return lax.ppermute(
-                lax.optimization_barrier((given, key_value))[0], "wide", Z_SWAP
-            )
-
+        out_rows = jnp.concatenate([kept, far], axis=1)
         blank = jnp.zeros((NY, HALF, NZ * CHIP), jnp.bfloat16)
-        return blank, prepare(far, start), ranks(placement, core)
-
-    gathered, (wq, wkv, wo), items = lax.cond(segment == 0, first_section, later_section, start)
+        return blank, prepare(far, out_rows), ranks(placement, core)
+
+    gathered, (wq, wkv, wo), items = lax.cond(
+        segment == 0, first_section, later_section, start, cross
+    )
 
     def later_gather(same, cross):
-        pair = (same.astype(jnp.float32) + cross.astype(jnp.float32)).astype(jnp.bfloat16)
-        return exchange(jnp.broadcast_to(pair[None], (NY, HALF, NZ * CHIP)), OVER_Y)
+        return gather((same.astype(jnp.float32) + cross.astype(jnp.float32)).astype(jnp.bfloat16))
+
+    def summed(parts, own):
+        parts = parts.astype(jnp.float32)
+        return own.astype(jnp.float32) + (parts[0] + parts[1] + parts[2] + parts[3])
+
+    def whole_out(context, own):
+        context = jnp.broadcast_to(context[:1], (NG, HALF, CHIP))
+        parts = exchange(output(info, exchange(context, OVER_XZ), wo), OVER_Y)
+        own = jnp.where(z == 0, own[:, :CHIP], own[:, CHIP:])
+        result = summed(parts, own).astype(jnp.bfloat16)
+        zero = jnp.zeros_like(result)
+        return jnp.concatenate(
+            [jnp.where(z == 0, result, zero), jnp.where(z == 0, zero, result)], axis=1
+        )
+
+    def half_out(context, own):
+        parts = exchange(output(info, exchange(context, OVER_X), wo), OVER_Y)
+        return summed(parts, jnp.where(z == 0, own, jnp.zeros_like(own))).astype(jnp.bfloat16)
 
     def layer(gathered):
         parts = exchange(project(info, gathered, gain_x, wq, wkv), OVER_X)
         query, kv = turn(parts, cos, sin, features)
         first = lax.ppermute(kv, "wide", CORE_UP)
-        context = exchange(attend(info, query, kv, first), OVER_X)
-        parts = exchange(output(info, context, wo), OVER_Y).astype(jnp.float32)
-        own = lax.dynamic_index_in_dim(gathered, y, 0, keepdims=False).astype(jnp.float32)
-        total = parts[0] + parts[1] + parts[2] + parts[3]
-        return (jnp.where(z == 0, own, 0.0) + total).astype(jnp.bfloat16), kv
+        context = attend(info, query, kv, first)
+        own = lax.dynamic_index_in_dim(gathered, y, 0, keepdims=False)
+        return lax.cond(segment == 0, whole_out, half_out, context, own), kv
 
     def send(pairs):
         same, cross = pairs

time: 721 us -> 723 us (level)
  waiting for transfers between devices: 569 us -> 593 us
  starting transfers between devices: 81.4 us -> 65.2 us
  local copies, waits for them, and re-layouts: 20.8 us -> 11.8 us
    all_to_all x4 -> x5, waiting for transfers between devices: 40.5 us -> 63.6 us  [exchange(): lax.all_to_all(value, 'wide', 0, 0, axis_index_groups=groups, tiled=True)]
    ppermute x7 -> x2, waiting for transfers between devices: 70.3 us -> 88.7 us  [the longest x1 87.1 us: later_section(): far = lax.ppermute(given, 'wide', Z_SWAP)]
    ppermute x2, waiting for transfers between devices: 435 us -> 418 us  [run(): return (lax.ppermute(value, axes, cross), lax.ppermute(value, axes, same))]
    ppermute x7 -> x2, starting transfers between devices: 27.6 us -> 10.6 us  [the longest x1 9.32 us: later_section(): far = lax.ppermute(given, 'wide', Z_SWAP)]
    all_to_all x4 -> x5, starting transfers between devices: 23.5 us -> 28 us  [exchange(): lax.all_to_all(value, 'wide', 0, 0, axis_index_groups=groups, tiled=True)]
    ppermute x7 -> x6, starting transfers between devices: 24.5 us -> 20.8 us  [swap_cores(): return lax.ppermute(value, 'wide', CORE_SWAP)]
  transfers between devices with their start and end apart: 22 -> 17, of which waited for: 11 -> 12; matrix products, arithmetic and copies ran while one was open for 3% -> 1% of each run, Pallas kernels for 0% -> 0%
where the time goes in v4:
time: 723 us; the launch traced here: 722 us
  waiting for transfers between devices  593 us (82%)
  starting transfers between devices  65.2 us (9%)
  blocking collectives  28.3 us (4%)
  Pallas kernels  12.1 us (2%)
  local copies, waits for them, and re-layouts  11.8 us (2%)
  other arithmetic  7.9 us (1%)
    ppermute x2, waiting for transfers between devices, run(): return (lax.ppermute(value, axes, cross), lax.ppermute(value, axes, same))  418 us
    ppermute x1, waiting for transfers between devices, later_section(): far = lax.ppermute(given, 'wide', Z_SWAP)  87.1 us
    all_to_all x5, waiting for transfers between devices, exchange(): lax.all_to_all(value, 'wide', 0, 0, axis_index_groups=groups, tiled=True)  63.6 us
    all_to_all x3, blocking collectives, exchange(): lax.all_to_all(value, 'wide', 0, 0, axis_index_groups=groups, tiled=True)  28.3 us
    all_to_all x5, starting transfers between devices, exchange(): lax.all_to_all(value, 'wide', 0, 0, axis_index_groups=groups, tiled=True)  28 us
    ppermute x6, starting transfers between devices, swap_cores(): return lax.ppermute(value, 'wide', CORE_SWAP)  20.8 us
  transfers between devices with their start and end apart: 17, of which 12 were waited for; matrix products, arithmetic and copies ran while one was open for 1% of the time, Pallas kernels for 0%

profile of v4, /device:TPU:481, one launch (start us, length us, event | category | flops | bytes accessed | tf_op | source)
XLA Modules:
  0.0 721.7 jit_solution(1520920288299600242)
XLA Ops:
  1.4 2.6 collective-permute-start.12
  10.6 185.6 %conditional.7 = (bf16[4,128,512]{2,1,0:T(8,128)(2,1)S(1)}, bf16[4,2048,128]{2,1,0:T(8,128)(2,1)}, bf16[4,2048,128]{2,1,0:T(8,128)(2,1)}, bf16[256,2048]{1,0:T(8...) conditional(s32[]{:T(128)} %convert_element_type.97, ...), branch_computations={%region_0.4_spmd, %region_4.5_spmd} | conditional | flops 5997961 | bytes 79178288 | solution.py:337
  12.4 9.3 %collective-permute-start.4 = (bf16[4,1024,128]{2,1,0:T(8,128)(2,1)S(1)}, bf16[4,1024,128]{2,1,0:T(8,128)(2,1)S(1)}, u32[]{:S(2)}, u32[]{:S(2)}) collective-permute-start(bf16[4,1024,128]{2,1,0:T(8,128)(2,1)S(1)} %get-tuple-element.615), channel_id=1, source_target_pairs={{0,8},{1,9},{2,10},{3,11},{4,12},{5,13},{6,14},{7,15},{8,0},{9,1},... | collective-permute-start | bytes 3145736 | tf_op jit(solution)/shard_map/cond/branch_0_fun/ppermute | solution.py:332
  23.3 87.1 %collective-permute-done.4 = bf16[4,1024,128]{2,1,0:T(8,128)(2,1)S(1)} collective-permute-done((bf16[4,1024,128]{2,1,0:T(8,128)(2,1)S(1)}, bf16[4,1024,128]{2,1,0:T(8,128)(2,1)S(1)}, u32[]{:S(2)}, u32[]{:S(2)}) %collective-permute-start.4) | collective-permute-done | bytes 1048608 | tf_op jit(solution)/shard_map/cond/branch_0_fun/ppermute | solution.py:332
  111.3 4.6 all-to-all-start
  116.7 25.1 %all-to-all-done = bf16[4,2048,128]{2,1,0:T(8,128)(2,1)} async-done(((bf16[4,2048,128]{2,1,0:T(8,128)(2,1)}), bf16[4,2048,128]{2,1,0:T(8,128)(2,1)}, u32[]{:S(2)}, u32[]{:S(2)}) %all-to-all-start) | async-done | bytes 2097184 | tf_op jit(solution)/shard_map/cond/branch_0_fun/all_to_all | solution.py:43
  141.7 10.2 %all_to_all.57 = bf16[4,32,2048]{2,1,0:T(8,128)(2,1)S(1)} all-to-all(bf16[4,32,2048]{2,1,0:T(8,128)(2,1)S(1)} %reshape.268), channel_id=1, replica_groups={{0,2,4,6},{1,3,5,7},{8,10,12,14},{9,11,13,15},{16,18,20,22},{17,19,21,2..., dimensions={0} | all-to-all | bytes 1048576 | tf_op jit(solution)/shard_map/cond/branch_0_fun/all_to_all | solution.py:43
  152.0 4.5 collective-permute-start.6
  158.3 4.5 all-to-all-start.2
  165.0 23.9 %all-to-all-done.2 = bf16[4,2048,128]{2,1,0:T(8,128)(2,1)} async-done(((bf16[4,2048,128]{2,1,0:T(8,128)(2,1)}), bf16[4,2048,128]{2,1,0:T(8,128)(2,1)}, u32[]{:S(2)}, u32[]{:S(2)}) %all-to-all-start.2) | async-done | bytes 2097184 | tf_op jit(solution)/shard_map/cond/branch_0_fun/all_to_all | solution.py:43
  188.9 3.1 collective-permute-start.7
  192.4 3.7 collective-permute-done.7
  197.5 484.3 %while.25 = (s32[]{:T(128)}, bf16[4,128,512]{2,1,0:T(8,128)(2,1)S(1)}, bf16[128,512]{1,0:T(8,128)(2,1)}, bf16[128,256]{1,0:T(8,128)(2,1)}, s32[]{:T(128)}, /*ind...) while((s32[]{:T(128)}, ...), condition=%wide.region_16.17_spmd.clone.clone, body=%wide.region_5.16_spmd.clone.clone.sunk | while | flops 1015839 | bytes 11798915 | solution.py:402
  198.6 431.3 %conditional.16 = (bf16[4,128,512]{2,1,0:T(8,128)(2,1)S(1)}) conditional(s32[]{:T(128)} %convert_element_type.136, bf16[4,128,512]{2,1,0:T(8,128)(2,1)S(1)} %get-tuple-element.781, (s32[]{:T(128)}, s32[]{:T(128)}, bf16[128,512]{1,0:T(8,128)(2,1)}, bf16[4,128,512]{2,1,0:T(8,128)(2,1)S(1)}) %tuple.126), branch_computations={%region_10.10_spmd, %region_11.15_spmd} | conditional | flops 262160 | bytes 4194573 | solution.py:391
  198.7 420.8 %conditional.1 = (bf16[128,512]{1,0:T(8,128)(2,1)}, bf16[128,512]{1,0:T(8,128)(2,1)}) conditional(s32[]{:T(128)} %convert_element_type.83, bf16[128,512]{1,0:T(8,128)(2,1)} %get-tuple-element.420, bf16[128,512]{1,0:T(8,128)(2,1)} %get-tuple-element.420), branch_computations={%region_12.11_spmd, %region_13.12_spmd} | conditional | bytes 1048672 | solution.py:386
  201.3 418.2 %collective-permute-done.2 = bf16[128,512]{1,0:T(8,128)(2,1)} collective-permute-done((bf16[128,512]{1,0:T(8,128)(2,1)}, bf16[128,512]{1,0:T(8,128)(2,1)}, u32[]{:S(2)}, u32[]{:S(2)}) %collective-permute-start.2) | collective-permute-done | bytes 131104 | tf_op jit(solution)/shard_map/while/body/eval_jaxpr/cond/branch_1_fun/cond/branch_1_fun/ppermute | solution.py:375
  619.5 10.4 %conditional.2 = (bf16[4,128,512]{2,1,0:T(8,128)(2,1)S(1)}) conditional(s32[]{:T(128)} %convert_element_type.82, bf16[4,128,512]{2,1,0:T(8,128)(2,1)S(1)} %get-tuple-element.419, (bf16[128,512]{1,0:T(8,128)(2,1)}, bf16[128,512]{1,0:T(8,128)(2,1)}) %tuple.67), branch_computations={%region_14.13_spmd, %region_15.14_spmd} | conditional | flops 262144 | bytes 3145736 | solution.py:387
  620.5 9.3 %all_to_all.61 = bf16[4,128,512]{2,1,0:T(8,128)(2,1)S(1)} all-to-all(bf16[4,128,512]{2,1,0:T(8,128)(2,1)S(1)} %broadcast_in_dim.82), channel_id=1, replica_groups={{0,16,32,48},{1,17,33,49},{2,18,34,50},{3,19,35,51},{4,20,36,52},{5,21,..., dimensions={0} | all-to-all | bytes 1048576 | tf_op jit(solution)/shard_map/while/body/eval_jaxpr/cond/branch_1_fun/cond/branch_1_fun/all_to_all | solution.py:43
  630.0 51.8 %conditional.15 = ((bf16[128,512]{1,0:T(8,128)(2,1)}, bf16[128,256]{1,0:T(8,128)(2,1)})) conditional(s32[]{:T(128)} %convert_element_type.137, (bf16[128,512]{1,0:T(8,128)(2,1)}, bf16[128,256]{1,0:T(8,128)(2,1)}) %tuple.124, (s32[]{:T(128)}, s32[3]{0:T(128)S(1)}, bf16[4,128,512]{2,1,0:T(8,128)(2,1)S(1)}, f32[1,2048]{1,0:T(1,128)S(1)}, ...), branch_computations={%region_6.6_spmd, %region_7.9_spmd} | conditional | flops 737286 | bytes 7537398 | solution.py:383
  630.0 5.0 project.1
  635.0 3.5 all-to-all-start.12
  639.0 6.8 all-to-all-done.12.part_ref
  648.0 6.5 collective-permute-done.11.first_ref
  656.2 25.6 %conditional = (bf16[128,512]{1,0:T(8,128)(2,1)}) conditional(s32[]{:T(128)} %convert_element_type.78, (s32[]{:T(128)}, bf16[128,512]{1,0:T(8,128)(2,1)S(1)}, bf16[4,128,256]{2,1,0:T(8,128)(2,1)S(1)}, s32[3]{0:T(128)S(1)}, bf16[4,2048,128]{2,1,0:T(8,128)(2,1)}, /*index=5*/bf16[4,2048,128]{2,1,0:T(8,128)(2,1)}) %tuple.62, (s32[]{:T(128)}, ...), branch_computations={%region_8.7_spmd, %region_9.8_spmd} | conditional | flops 720897 | bytes 4980786 | solution.py:368
  656.2 8.8 %all_to_all.59.ctx_ref = bf16[4,128,256]{2,1,0:T(8,128)(2,1)S(1)} all-to-all(bf16[4,128,256]{2,1,0:T(8,128)(2,1)S(1)} %get-tuple-element.391), channel_id=1, replica_groups={{0,2,4,6},{1,3,5,7},{8,10,12,14},{9,11,13,15},{16,18,20,22},{17,19,21,2..., dimensions={0} | all-to-all | bytes 524288 | tf_op jit(solution)/shard_map/while/body/eval_jaxpr/cond/branch_1_fun/cond/branch_0_fun/all_to_all | solution.py:43
  665.0 4.5 output.2
  669.5 3.5 all-to-all-start.8
  672.9 7.9 %all-to-all-done.8 = bf16[4,128,512]{2,1,0:T(8,128)(2,1)S(1)} async-done(((bf16[4,128,512]{2,1,0:T(8,128)(2,1)}), bf16[4,128,512]{2,1,0:T(8,128)(2,1)S(1)}, u32[]{:S(2)}, u32[]{:S(2)}) %all-to-all-start.8) | async-done | bytes 524320 | tf_op jit(solution)/shard_map/while/body/eval_jaxpr/cond/branch_1_fun/cond/branch_0_fun/all_to_all | solution.py:43
  683.4 12.1 %all-to-all-start.13 = ((bf16[8,128,256]{2,1,0:T(8,128)(2,1)}), bf16[8,128,256]{2,1,0:T(8,128)(2,1)S(1)}, u32[]{:S(2)}, u32[]{:S(2)}) async-start(bf16[8,128,256]{2,1,0:T(8,128)(2,1)} %broadcast_in_dim.94), calls=%async_computation.13 | async-start | bytes 1048576 | tf_op jit(solution)/shard_map/all_to_all | solution.py:43
  698.5 11.8 %collective-permute-done.14 = bf16[128,256]{0,1:T(8,128)(2,1)S(1)} collective-permute-done((bf16[128,256]{0,1:T(8,128)(2,1)S(1)}, bf16[128,256]{0,1:T(8,128)(2,1)S(1)}, u32[]{:S(2)}, u32[]{:S(2)}) %collective-permute-start.14) | collective-permute-done | bytes 65568 | tf_op jit(solution)/shard_map/ppermute | solution.py:407
  710.4 6.1 collective-permute-start.15
  717.8 2.3 collective-permute-start.16
  (103 shorter events, 34.7 us)
Async XLA Ops:
  1.4 5.4 collective-permute-start.12
  7.6 3.0 collective-permute-start.13
  10.6 11.2 %copy-start.2 = (bf16[1,8192,128]{2,1,0:T(8,128)(2,1)S(1)}, bf16[1,8192,128]{2,1,0:T(8,128)(2,1)}, u32[]{:S(2)}) copy-start(bf16[1,8192,128]{2,1,0:T(8,128)(2,1)} %get-tuple-element.367) | copy-start | bytes 6291460 | tf_op jit(solution)/shard_map/cond
  12.4 97.9 %collective-permute-start.4 = (bf16[4,1024,128]{2,1,0:T(8,128)(2,1)S(1)}, bf16[4,1024,128]{2,1,0:T(8,128)(2,1)S(1)}, u32[]{:S(2)}, u32[]{:S(2)}) collective-permute-start(bf16[4,1024,128]{2,1,0:T(8,128)(2,1)S(1)} %get-tuple-element.615), channel_id=1, source_target_pairs={{0,8},{1,9},{2,10},{3,11},{4,12},{5,13},{6,14},{7,15},{8,0},{9,1},... | collective-permute-start | bytes 3145736 | tf_op jit(solution)/shard_map/cond/branch_0_fun/ppermute | solution.py:332
  110.3 1.0 copy-start.7
  111.3 4.6 copy-start.3
  111.3 4.8 copy-start.5
  111.3 30.4 %all-to-all-start = ((bf16[4,2048,128]{2,1,0:T(8,128)(2,1)}), bf16[4,2048,128]{2,1,0:T(8,128)(2,1)}, u32[]{:S(2)}, u32[]{:S(2)}) async-start(bf16[4,2048,128]{2,1,0:T(8,128)(2,1)} %bitcast.99), calls=%async_computation | async-start | bytes 4194304 | tf_op jit(solution)/shard_map/cond/branch_0_fun/all_to_all | solution.py:43
  116.3 40.1 %copy-start.8 = (bf16[4,1024,128]{2,1,0:T(8,128)(2,1)S(1)}, bf16[4,1024,128]{2,1,0:T(8,128)(2,1)}, u32[]{:S(2)}) copy-start(bf16[4,1024,128]{2,1,0:T(8,128)(2,1)} %copy-done.7) | copy-start | bytes 3145732 | tf_op jit(solution)/shard_map/cond
  152.0 6.0 collective-permute-start.6
  158.3 33.7 %copy-start.10 = (s32[256,1]{0,1:T(1,128)S(1)}, s32[256,1]{0,1:T(1,128)}, u32[]{:S(2)}) copy-start(s32[256,1]{0,1:T(1,128)} %get-tuple-element.376) | copy-start | bytes 3076 | tf_op jit(solution)/shard_map/cond
  158.3 30.6 %all-to-all-start.2 = ((bf16[4,2048,128]{2,1,0:T(8,128)(2,1)}), bf16[4,2048,128]{2,1,0:T(8,128)(2,1)}, u32[]{:S(2)}, u32[]{:S(2)}) async-start(bf16[4,2048,128]{2,1,0:T(8,128)(2,1)} %pad_maximum_fusion), calls=%async_computation.2 | async-start | bytes 4194304 | tf_op jit(solution)/shard_map/cond/branch_0_fun/all_to_all | solution.py:43
  162.8 29.6 %collective-permute-start.5 = (bf16[4,2048,128]{2,1,0:T(8,128)(2,1)}, bf16[4,2048,128]{2,1,0:T(8,128)(2,1)}, u32[]{:S(2)}, u32[]{:S(2)}) collective-permute-start(bf16[4,2048,128]{2,1,0:T(8,128)(2,1)} %all-to-all-done), channel_id=1, source_target_pairs={{0,1},{1,0},{2,3},{3,2},{4,5},{5,4},{6,7},{7,6},{8,9},{9,8},{10,11... | collective-permute-start | bytes 6291464 | tf_op jit(solution)/shard_map/cond/branch_0_fun/ppermute | solution.py:47
  188.9 7.2 %collective-permute-start.7 = (bf16[4,2048,128]{2,1,0:T(8,128)(2,1)}, bf16[4,2048,128]{2,1,0:T(8,128)(2,1)}, u32[]{:S(2)}, u32[]{:S(2)}) collective-permute-start(bf16[4,2048,128]{2,1,0:T(8,128)(2,1)} %all-to-all-done.2), channel_id=1, source_target_pairs={{0,1},{1,0},{2,3},{3,2},{4,5},{5,4},{6,7},{7,6},{8,9},{9,8},{10,11... | collective-permute-start | bytes 6291464 | tf_op jit(solution)/shard_map/cond/branch_0_fun/ppermute | solution.py:47
  197.5 501.0 %copy-start.9 = (s32[256,1]{0,1:T(1,128)S(1)}, s32[256,1]{0,1:T(1,128)}, u32[]{:S(2)}) copy-start(s32[256,1]{0,1:T(1,128)} %param.31) | copy-start | bytes 3076
  198.7 420.8 %collective-permute-start.2 = (bf16[128,512]{1,0:T(8,128)(2,1)}, bf16[128,512]{1,0:T(8,128)(2,1)}, u32[]{:S(2)}, u32[]{:S(2)}) collective-permute-start(bf16[128,512]{1,0:T(8,128)(2,1)} %param.8), channel_id=1, source_target_pairs={{0,72},{1,73},{2,74},{3,75},{4,76},{5,77},{6,78},{7,79},{8,64},{9,... | collective-permute-start | bytes 393224 | tf_op jit(solution)/shard_map/while/body/eval_jaxpr/cond/branch_1_fun/cond/branch_1_fun/ppermute | solution.py:375
  200.0 419.5 %collective-permute-start.3 = (bf16[128,512]{1,0:T(8,128)(2,1)}, bf16[128,512]{1,0:T(8,128)(2,1)}, u32[]{:S(2)}, u32[]{:S(2)}) collective-permute-start(bf16[128,512]{1,0:T(8,128)(2,1)} %param.8), channel_id=1, source_target_pairs={{0,64},{1,65},{2,66},{3,67},{4,68},{5,69},{6,70},{7,71},{8,72},{9,... | collective-permute-start | bytes 393224 | tf_op jit(solution)/shard_map/while/body/eval_jaxpr/cond/branch_1_fun/cond/branch_1_fun/ppermute | solution.py:375
  635.0 10.7 %all-to-all-start.12 = ((bf16[4,144,512]{2,1,0:T(8,128)(2,1)}), bf16[4,144,512]{2,1,0:T(8,128)(2,1)S(1)}, u32[]{:S(2)}, u32[]{:S(2)}) async-start(bf16[4,144,512]{2,1,0:T(8,128)(2,1)} %project.1), calls=%async_computation.12 | async-start | bytes 1179648 | tf_op jit(solution)/shard_map/while/body/eval_jaxpr/cond/branch_1_fun/all_to_all | solution.py:43
  646.6 7.9 %collective-permute-start.11 = (bf16[128,256]{1,0:T(8,128)(2,1)}, bf16[128,256]{1,0:T(8,128)(2,1)S(1)}, u32[]{:S(2)}, u32[]{:S(2)}) collective-permute-start(bf16[128,256]{1,0:T(8,128)(2,1)} %get-tuple-element.744.own_ref), channel_id=1, source_target_pairs={{0,1},{2,3},{4,5},{6,7},{8,9},{10,11},{12,13},{14,15},{16,17},{18,... | collective-permute-start | bytes 196616 | tf_op jit(solution)/shard_map/while/body/eval_jaxpr/cond/branch_1_fun/ppermute | solution.py:365
  669.5 11.4 %all-to-all-start.8 = ((bf16[4,128,512]{2,1,0:T(8,128)(2,1)}), bf16[4,128,512]{2,1,0:T(8,128)(2,1)S(1)}, u32[]{:S(2)}, u32[]{:S(2)}) async-start(bf16[4,128,512]{2,1,0:T(8,128)(2,1)} %output.2), calls=%async_computation.8 | async-start | bytes 1048576 | tf_op jit(solution)/shard_map/while/body/eval_jaxpr/cond/branch_1_fun/cond/branch_0_fun/all_to_all | solution.py:43
  683.4 33.9 %all-to-all-start.13 = ((bf16[8,128,256]{2,1,0:T(8,128)(2,1)}), bf16[8,128,256]{2,1,0:T(8,128)(2,1)S(1)}, u32[]{:S(2)}, u32[]{:S(2)}) async-start(bf16[8,128,256]{2,1,0:T(8,128)(2,1)} %broadcast_in_dim.94), calls=%async_computation.13 | async-start | bytes 1048576 | tf_op jit(solution)/shard_map/all_to_all | solution.py:43
  696.5 13.7 %collective-permute-start.14 = (bf16[128,256]{0,1:T(8,128)(2,1)S(1)}, bf16[128,256]{0,1:T(8,128)(2,1)S(1)}, u32[]{:S(2)}, u32[]{:S(2)}) collective-permute-start(bf16[128,256]{0,1:T(8,128)(2,1)S(1)} %dynamic-slice_bitcast_fusion.3), channel_id=1, source_target_pairs={{0,8},{1,9},{2,10},{3,11},{4,12},{5,13},{6,14},{7,15},{8,0},{9,1},... | collective-permute-start | bytes 196616 | tf_op jit(solution)/shard_map/ppermute | solution.py:407
  710.4 6.9 collective-permute-start.15
  717.8 3.1 collective-permute-start.16

commit v5 on v4

--- a/solution.py
+++ b/solution.py
@@ -34,7 +34,6 @@
     for c in range(NC)
 ]
 Z_SWAP = [(w, w ^ 8) for w in range(WIDE)]
-LAST_TO_FIRST = [((SECTIONS - 1) * WIDE + w, w ^ 8) for w in range(WIDE)]
 CORE_SWAP = [(w, w ^ 1) for w in range(WIDE)]
 CORE_UP = [(w, w + 1) for w in range(0, WIDE, 2)]
 
@@ -57,14 +56,33 @@
     return weight.reshape(NG, NX, CHIP, HD).transpose(1, 0, 2, 3).reshape(NX, NG * CHIP, HD)
 
 
-def relayout_kv(w_key, w_value, core, after):
+def moved(w, stride, step):
+    at = w // stride % 4
+    return w + ((at + step) % 4 - at) * stride
+
+
+def from_ring(piece, at, stride):
+    blocks = [piece(at)]
+    for step in range(1, 4):
+        pairs = [(w, moved(w, stride, step)) for w in range(WIDE)]
+        blocks.append(lax.ppermute(piece((at + step) % 4), "wide", pairs))
+    return jnp.concatenate(blocks, axis=0)
+
+
+def in_order(blocks, at):
+    return jnp.concatenate(
+        [lax.dynamic_slice_in_dim(blocks, (at + 4 - i) % 4, 1, 0) for i in range(4)], axis=0
+    )
+
+
+def relayout_kv(w_key, w_value, core, x):
     both = jnp.stack([w_key.T, w_value.T])
     width = both.shape[1]
     both = both.reshape(2, width, NG, NX, CHIP).transpose(3, 0, 1, 2, 4)
-    mine = exchange(after(both.reshape(NX, 2 * width, NG * CHIP)), OVER_X)
-    other = swap_cores(mine)
-    mine = mine.reshape(NX, 2, 1, width, NG * CHIP)
-    other = other.reshape(NX, 2, 1, width, NG * CHIP)
+    both = both.reshape(NX, 2 * width, NG * CHIP)
+    mine = from_ring(lambda i: lax.dynamic_slice_in_dim(both, i, 1, 0), x, NC)
+    other = in_order(swap_cores(mine), x).reshape(NX, 2, 1, width, NG * CHIP)
+    mine = in_order(mine, x).reshape(NX, 2, 1, width, NG * CHIP)
     full = by_core(core, mine, other, 2)
     return full.transpose(1, 0, 2, 3, 4).reshape(2 * HD, NG * CHIP)
 
@@ -231,19 +249,23 @@
     count = context.shape[0]
     halves = NG // count
     rows = NG * CHIP
-    block = pl.BlockSpec((1, rows, HD), lambda i: (i, 0, 0))
+    block = pl.BlockSpec((1, rows, HD), lambda i, info: (i, 0, 0))
     return pl.pallas_call(
         functools.partial(output_kernel, halves),
-        grid=(NY,),
-        in_specs=[
-            pl.BlockSpec(memory_space=pltpu.SMEM),
-            pl.BlockSpec((count, HALF, CHIP), lambda i: (0, 0, 0)),
-            block,
-            block,
-        ],
-        out_specs=pl.BlockSpec((1, HALF, halves * CHIP), lambda i: (i, 0, 0)),
+        grid_spec=pltpu.PrefetchScalarGridSpec(
+            num_scalar_prefetch=1,
+            grid=(NY,),
+            in_specs=[
+                pl.BlockSpec((count, HALF, CHIP), lambda i, info: (0, 0, 0)),
+                block,
+                block,
+            ],
+            out_specs=pl.BlockSpec(
+                (1, HALF, halves * CHIP), lambda i, info: (lax.rem(info[3] + NY - i, NY), 0, 0)
+            ),
+            scratch_shapes=[pltpu.VMEM((HALF, count * CHIP), jnp.bfloat16)],
+        ),
         out_shape=jax.ShapeDtypeStruct((NY, HALF, halves * CHIP), jnp.bfloat16),
-        scratch_shapes=[pltpu.VMEM((HALF, count * CHIP), jnp.bfloat16)],
         compiler_params=pltpu.CompilerParams(vmem_limit_bytes=VMEM),
         name="output",
     )(info, context, *wo)
@@ -263,6 +285,10 @@
     return item_owner, item_rank
 
 
+def last_to_first(flip):
+    return [((SECTIONS - 1) * WIDE + w, w ^ flip) for w in range(WIDE)]
+
+
 def relay_pairs(first):
     same, cross = [], []
     for s in range(first, SECTIONS - 1, 2):
@@ -284,7 +310,12 @@
     halves = hidden_in.reshape(2, HALF, HD)
     kept = lax.dynamic_index_in_dim(halves, core, 0, keepdims=False)
     given = lax.dynamic_index_in_dim(halves, 1 - core, 0, keepdims=False)
-    start = by_core(core, kept, swap_cores(given), 1)
+    from_core = swap_cores(given)
+    flat = ("segment", "wide")
+    cross_own = lax.ppermute(kept, flat, last_to_first(8))
+    cross_other = lax.ppermute(given, flat, last_to_first(9))
+    start = by_core(core, kept, from_core, 1)
+    cross = by_core(core, cross_own, cross_other, 1)
 
     gain_x = lax.dynamic_index_in_dim(gain.reshape(NG, NX, CHIP), x, 1, keepdims=False)
     gain_x = gain_x.reshape(1, NG * CHIP)
@@ -295,24 +326,17 @@
     angle = position[:, None] * freq[None, :]
     cos = jnp.cos(angle)
     sin = jnp.where(lane[None, :] % 2 == 0, -1.0, 1.0) * jnp.sin(angle)
-    info = jnp.stack([core, length[0], z]).astype(jnp.int32)
+    info = jnp.stack([core, length[0], z, y]).astype(jnp.int32)
 
     def gather(pair):
         return exchange(jnp.broadcast_to(pair[None], (NY, HALF, NZ * CHIP)), OVER_Y)
 
-    cross = lax.ppermute(start, ("segment", "wide"), LAST_TO_FIRST)
     raw = w_out[0].reshape(NY, NZ * NX * CHIP, HD)
 
-    def prepare(before, out_rows):
-        rows = lax.optimization_barrier((x_blocks(w_query[0]), before))[0]
-        query = exchange(rows, OVER_X)
-        key_value = relayout_kv(
-            w_key[0],
-            w_value[0],
-            core,
-            lambda both: lax.optimization_barrier((both, query))[0],
-        )
-        out = exchange(lax.optimization_barrier((out_rows, key_value))[0], OVER_Y)
+    def prepare(out_rows):
+        query = exchange(x_blocks(w_query[0]), OVER_X)
+        key_value = relayout_kv(w_key[0], w_value[0], core, x)
+        out = from_ring(lambda i: lax.dynamic_slice_in_dim(out_rows, i, 1, 0), y, 16)
         return (query, swap_cores(query)), key_value, (out, swap_cores(out))
 
     def first_section(start, cross):
@@ -321,9 +345,9 @@
             jnp.concatenate([start, cross], axis=1),
             jnp.concatenate([cross, start], axis=1),
         )
-        gathered = gather(pair)
+        gathered = in_order(from_ring(lambda i: pair[None], y, 16), y)
         items = jnp.zeros((ITEMS_HERE,), jnp.int32)
-        return gathered, prepare(gathered, raw), (items, items)
+        return gathered, prepare(raw), (items, items)
 
     def later_section(start, cross):
         halves = raw.reshape(NY, NZ, NX * CHIP, HD)
@@ -332,7 +356,7 @@
         far = lax.ppermute(given, "wide", Z_SWAP)
         out_rows = jnp.concatenate([kept, far], axis=1)
         blank = jnp.zeros((NY, HALF, NZ * CHIP), jnp.bfloat16)
-        return blank, prepare(far, out_rows), ranks(placement, core)
+        return blank, prepare(out_rows), ranks(placement, core)
 
     gathered, (wq, wkv, wo), items = lax.cond(
         segment == 0, first_section, later_section, start, cross

time: 723 us -> 712 us (0.985)
  waiting for transfers between devices: 593 us -> 574 us
  starting transfers between devices: 65.2 us -> 83 us
  blocking collectives: 28.3 us -> 18.1 us
    all_to_all x5 -> x4, waiting for transfers between devices: 63.6 us -> 14.7 us  [exchange(): lax.all_to_all(value, 'wide', 0, 0, axis_index_groups=groups, tiled=True)]
    ppermute x1 -> x8, starting transfers between devices: 1.29 us -> 23.8 us  [the longest x6 21.3 us: from_ring(): blocks.append(lax.ppermute(piece((at + step) % 4), 'wide', pairs))]
    ppermute x1 -> x8, waiting for transfers between devices: 1.62 us -> 22.6 us  [the longest x6 21.6 us: from_ring(): blocks.append(lax.ppermute(piece((at + step) % 4), 'wide', pairs))]
    ppermute x2, waiting for transfers between devices: 418 us -> 434 us  [run(): return (lax.ppermute(value, axes, cross), lax.ppermute(value, axes, same))]
    all_to_all x3 -> x2, blocking collectives: 28.3 us -> 18.1 us  [exchange(): lax.all_to_all(value, 'wide', 0, 0, axis_index_groups=groups, tiled=True)]
    all_to_all x5 -> x4, starting transfers between devices: 28 us -> 23.4 us  [exchange(): lax.all_to_all(value, 'wide', 0, 0, axis_index_groups=groups, tiled=True)]
  transfers between devices with their start and end apart: 17 -> 23, of which waited for: 12 -> 15; matrix products, arithmetic and copies ran while one was open for 1% -> 1% of each run, Pallas kernels for 0% -> 0%
where the time goes in v5:
time: 712 us; the launch traced here: 710 us
  waiting for transfers between devices  574 us (81%)
  starting transfers between devices  83 us (12%)
  blocking collectives  18.1 us (3%)
  Pallas kernels  12.6 us (2%)
  local copies, waits for them, and re-layouts  11.1 us (2%)
  other arithmetic  8.27 us (1%)
    ppermute x2, waiting for transfers between devices, run(): return (lax.ppermute(value, axes, cross), lax.ppermute(value, axes, same))  434 us
    ppermute x1, waiting for transfers between devices, later_section(): far = lax.ppermute(given, 'wide', Z_SWAP)  82.4 us
    all_to_all x4, starting transfers between devices, exchange(): lax.all_to_all(value, 'wide', 0, 0, axis_index_groups=groups, tiled=True)  23.4 us
    ppermute x6, waiting for transfers between devices, from_ring(): blocks.append(lax.ppermute(piece((at + step) % 4), 'wide', pairs))  21.6 us
    ppermute x6, starting transfers between devices, from_ring(): blocks.append(lax.ppermute(piece((at + step) % 4), 'wide', pairs))  21.3 us
    ppermute x6, starting transfers between devices, swap_cores(): return lax.ppermute(value, 'wide', CORE_SWAP)  20.4 us
    all_to_all x2, blocking collectives, exchange(): lax.all_to_all(value, 'wide', 0, 0, axis_index_groups=groups, tiled=True)  18.1 us
    all_to_all x4, waiting for transfers between devices, exchange(): lax.all_to_all(value, 'wide', 0, 0, axis_index_groups=groups, tiled=True)  14.7 us
  transfers between devices with their start and end apart: 23, of which 15 were waited for; matrix products, arithmetic and copies ran while one was open for 1% of the time, Pallas kernels for 0%

profile of v5, /device:TPU:481, one launch (start us, length us, event | category | flops | bytes accessed | tf_op | source)
XLA Modules:
  0.0 710.1 jit_solution(2577655259861017715)
XLA Ops:
  11.3 157.2 %conditional.7 = (bf16[4,128,512]{2,1,0:T(8,128)(2,1)S(1)}, bf16[4,2048,128]{2,1,0:T(8,128)(2,1)}, bf16[4,2048,128]{2,1,0:T(8,128)(2,1)}, bf16[256,2048]{1,0:T(8...) conditional(s32[]{:T(128)} %convert_element_type.97, ...), branch_computations={%region_0.4_spmd, %region_4.5_spmd} | conditional | flops 11503095 | bytes 79703888 | solution.py:361
  13.2 9.5 %collective-permute-start.9 = (bf16[4,1024,128]{2,1,0:T(8,128)(2,1)S(1)}, bf16[4,1024,128]{2,1,0:T(8,128)(2,1)S(1)}, u32[]{:S(2)}, u32[]{:S(2)}) collective-permute-start(bf16[4,1024,128]{2,1,0:T(8,128)(2,1)S(1)} %get-tuple-element.626), channel_id=1, source_target_pairs={{0,8},{1,9},{2,10},{3,11},{4,12},{5,13},{6,14},{7,15},{8,0},{9,1},... | collective-permute-start | bytes 3145736 | tf_op jit(solution)/shard_map/cond/branch_0_fun/ppermute | solution.py:356
  24.2 4.5 all-to-all-start
  28.8 82.4 %collective-permute-done.9 = bf16[4,1024,128]{2,1,0:T(8,128)(2,1)S(1)} collective-permute-done((bf16[4,1024,128]{2,1,0:T(8,128)(2,1)S(1)}, bf16[4,1024,128]{2,1,0:T(8,128)(2,1)S(1)}, u32[]{:S(2)}, u32[]{:S(2)}) %collective-permute-start.9) | collective-permute-done | bytes 1048608 | tf_op jit(solution)/shard_map/cond/branch_0_fun/ppermute | solution.py:356
  111.2 3.2 collective-permute-start.10
  114.5 4.5 collective-permute-start.11
  122.0 5.4 collective-permute-done.10
  127.4 12.3 %collective-permute-done.11 = bf16[1,2048,128]{2,1,0:T(8,128)(2,1)S(1)} collective-permute-done((bf16[1,2048,128]{2,1,0:T(8,128)(2,1)S(1)}, bf16[1,2048,128]{2,1,0:T(8,128)(2,1)S(1)}, u32[]{:S(2)}, u32[]{:S(2)}) %collective-permute-start.11) | collective-permute-done | bytes 524320 | tf_op jit(solution)/shard_map/cond/branch_0_fun/ppermute | solution.py:68
  142.6 3.5 collective-permute-start.13
  148.9 3.1 collective-permute-start.5
  152.0 4.4 collective-permute-start.6
  156.4 3.1 collective-permute-start.7
  162.2 4.1 collective-permute-start.8
  169.8 500.4 %while.25 = (s32[]{:T(128)}, bf16[4,128,512]{2,1,0:T(8,128)(2,1)S(1)}, bf16[128,512]{1,0:T(8,128)(2,1)}, bf16[128,256]{1,0:T(8,128)(2,1)}, s32[]{:T(128)}, /*ind...) while((s32[]{:T(128)}, ...), condition=%wide.region_16.17_spmd.clone.clone, body=%wide.region_5.16_spmd.clone.clone.sunk | while | flops 1015839 | bytes 11798915 | solution.py:426
  170.9 446.8 %conditional.16 = (bf16[4,128,512]{2,1,0:T(8,128)(2,1)S(1)}) conditional(s32[]{:T(128)} %convert_element_type.136, bf16[4,128,512]{2,1,0:T(8,128)(2,1)S(1)} %get-tuple-element.825, (s32[]{:T(128)}, s32[]{:T(128)}, bf16[128,512]{1,0:T(8,128)(2,1)}, bf16[4,128,512]{2,1,0:T(8,128)(2,1)S(1)}) %tuple.148), branch_computations={%region_10.10_spmd, %region_11.15_spmd} | conditional | flops 262160 | bytes 4194573 | solution.py:415
  171.0 436.4 %conditional.1 = (bf16[128,512]{1,0:T(8,128)(2,1)}, bf16[128,512]{1,0:T(8,128)(2,1)}) conditional(s32[]{:T(128)} %convert_element_type.83, bf16[128,512]{1,0:T(8,128)(2,1)} %get-tuple-element.426, bf16[128,512]{1,0:T(8,128)(2,1)} %get-tuple-element.426), branch_computations={%region_12.11_spmd, %region_13.12_spmd} | conditional | bytes 1048672 | solution.py:410
  173.6 433.7 %collective-permute-done.2 = bf16[128,512]{1,0:T(8,128)(2,1)} collective-permute-done((bf16[128,512]{1,0:T(8,128)(2,1)}, bf16[128,512]{1,0:T(8,128)(2,1)}, u32[]{:S(2)}, u32[]{:S(2)}) %collective-permute-start.2) | collective-permute-done | bytes 131104 | tf_op jit(solution)/shard_map/while/body/eval_jaxpr/cond/branch_1_fun/cond/branch_1_fun/ppermute | solution.py:399
  607.3 10.4 %conditional.2 = (bf16[4,128,512]{2,1,0:T(8,128)(2,1)S(1)}) conditional(s32[]{:T(128)} %convert_element_type.82, bf16[4,128,512]{2,1,0:T(8,128)(2,1)S(1)} %get-tuple-element.425, (bf16[128,512]{1,0:T(8,128)(2,1)}, bf16[128,512]{1,0:T(8,128)(2,1)}) %tuple.61), branch_computations={%region_14.13_spmd, %region_15.14_spmd} | conditional | flops 262144 | bytes 3145736 | solution.py:411
  608.4 9.3 %all_to_all.39 = bf16[4,128,512]{2,1,0:T(8,128)(2,1)S(1)} all-to-all(bf16[4,128,512]{2,1,0:T(8,128)(2,1)S(1)} %broadcast_in_dim.66), channel_id=1, replica_groups={{0,16,32,48},{1,17,33,49},{2,18,34,50},{3,19,35,51},{4,20,36,52},{5,21,..., dimensions={0} | all-to-all | bytes 1048576 | tf_op jit(solution)/shard_map/while/body/eval_jaxpr/cond/branch_1_fun/cond/branch_1_fun/all_to_all | solution.py:42
  617.9 52.3 %conditional.15 = ((bf16[128,512]{1,0:T(8,128)(2,1)}, bf16[128,256]{1,0:T(8,128)(2,1)})) conditional(s32[]{:T(128)} %convert_element_type.137, (bf16[128,512]{1,0:T(8,128)(2,1)}, bf16[128,256]{1,0:T(8,128)(2,1)}) %tuple.146, (s32[]{:T(128)}, s32[4]{0:T(128)S(1)}, bf16[4,128,512]{2,1,0:T(8,128)(2,1)S(1)}, f32[1,2048]{1,0:T(1,128)S(1)}, ...), branch_computations={%region_6.6_spmd, %region_7.9_spmd} | conditional | flops 737286 | bytes 7537398 | solution.py:407
  617.9 5.0 project.1
  622.9 3.5 all-to-all-start.7
  626.8 6.8 all-to-all-done.7.part_ref
  635.8 6.5 collective-permute-done.26.first_ref
  644.0 26.1 %conditional = (bf16[128,512]{1,0:T(8,128)(2,1)}) conditional(s32[]{:T(128)} %convert_element_type.78, (s32[]{:T(128)}, bf16[128,512]{1,0:T(8,128)(2,1)S(1)}, bf16[4,128,256]{2,1,0:T(8,128)(2,1)S(1)}, s32[4]{0:T(128)S(1)}, bf16[4,2048,128]{2,1,0:T(8,128)(2,1)}, /*index=5*/bf16[4,2048,128]{2,1,0:T(8,128)(2,1)}) %tuple.56, (s32[]{:T(128)}, ...), branch_computations={%region_8.7_spmd, %region_9.8_spmd} | conditional | flops 720897 | bytes 4980786 | solution.py:392
  644.1 8.8 %all_to_all.37.ctx_ref = bf16[4,128,256]{2,1,0:T(8,128)(2,1)S(1)} all-to-all(bf16[4,128,256]{2,1,0:T(8,128)(2,1)S(1)} %get-tuple-element.397), channel_id=1, replica_groups={{0,2,4,6},{1,3,5,7},{8,10,12,14},{9,11,13,15},{16,18,20,22},{17,19,21,2..., dimensions={0} | all-to-all | bytes 524288 | tf_op jit(solution)/shard_map/while/body/eval_jaxpr/cond/branch_1_fun/cond/branch_0_fun/all_to_all | solution.py:42
  652.8 5.0 output.2
  657.8 3.5 all-to-all-start.3
  661.3 7.9 %all-to-all-done.3 = bf16[4,128,512]{2,1,0:T(8,128)(2,1)S(1)} async-done(((bf16[4,128,512]{2,1,0:T(8,128)(2,1)}), bf16[4,128,512]{2,1,0:T(8,128)(2,1)S(1)}, u32[]{:S(2)}, u32[]{:S(2)}) %all-to-all-start.3) | async-done | bytes 524320 | tf_op jit(solution)/shard_map/while/body/eval_jaxpr/cond/branch_1_fun/cond/branch_0_fun/all_to_all | solution.py:42
  671.8 12.1 %all-to-all-start.8 = ((bf16[8,128,256]{2,1,0:T(8,128)(2,1)}), bf16[8,128,256]{2,1,0:T(8,128)(2,1)S(1)}, u32[]{:S(2)}, u32[]{:S(2)}) async-start(bf16[8,128,256]{2,1,0:T(8,128)(2,1)} %broadcast_in_dim.92), calls=%async_computation.8 | async-start | bytes 1048576 | tf_op jit(solution)/shard_map/all_to_all | solution.py:42
  686.9 11.8 %collective-permute-done.30 = bf16[128,256]{0,1:T(8,128)(2,1)S(1)} collective-permute-done((bf16[128,256]{0,1:T(8,128)(2,1)S(1)}, bf16[128,256]{0,1:T(8,128)(2,1)S(1)}, u32[]{:S(2)}, u32[]{:S(2)}) %collective-permute-start.30) | collective-permute-done | bytes 65568 | tf_op jit(solution)/shard_map/ppermute | solution.py:431
  698.8 6.1 collective-permute-start.31
  (118 shorter events, 47.4 us)
Async XLA Ops:
  1.4 6.8 collective-permute-start.27
  4.0 6.3 collective-permute-start.29
  8.9 2.3 collective-permute-start.28
  11.3 11.4 %copy-start = (bf16[1,8192,128]{2,1,0:T(8,128)(2,1)S(1)}, bf16[1,8192,128]{2,1,0:T(8,128)(2,1)}, u32[]{:S(2)}) copy-start(bf16[1,8192,128]{2,1,0:T(8,128)(2,1)} %get-tuple-element.375) | copy-start | bytes 6291460 | tf_op jit(solution)/shard_map/cond
  13.2 97.9 %collective-permute-start.9 = (bf16[4,1024,128]{2,1,0:T(8,128)(2,1)S(1)}, bf16[4,1024,128]{2,1,0:T(8,128)(2,1)S(1)}, u32[]{:S(2)}, u32[]{:S(2)}) collective-permute-start(bf16[4,1024,128]{2,1,0:T(8,128)(2,1)S(1)} %get-tuple-element.626), channel_id=1, source_target_pairs={{0,8},{1,9},{2,10},{3,11},{4,12},{5,13},{6,14},{7,15},{8,0},{9,1},... | collective-permute-start | bytes 3145736 | tf_op jit(solution)/shard_map/cond/branch_0_fun/ppermute | solution.py:356
  24.2 121.8 %all-to-all-start = ((bf16[4,2048,128]{2,1,0:T(8,128)(2,1)}), bf16[4,2048,128]{2,1,0:T(8,128)(2,1)}, u32[]{:S(2)}, u32[]{:S(2)}) async-start(bf16[4,2048,128]{2,1,0:T(8,128)(2,1)} %bitcast.2), calls=%async_computation | async-start | bytes 4194304 | tf_op jit(solution)/shard_map/cond/branch_0_fun/all_to_all | solution.py:42
  111.2 16.1 %collective-permute-start.10 = (bf16[1,2048,128]{2,1,0:T(8,128)(2,1)S(1)}, bf16[1,2048,128]{2,1,0:T(8,128)(2,1)S(1)}, u32[]{:S(2)}, u32[]{:S(2)}) collective-permute-start(bf16[1,2048,128]{2,1,0:T(8,128)(2,1)S(1)} %get-tuple-element.623), channel_id=1, source_target_pairs={{0,16},{1,17},{2,18},{3,19},{4,20},{5,21},{6,22},{7,23},{8,24},{9,... | collective-permute-start | bytes 1572872 | tf_op jit(solution)/shard_map/cond/branch_0_fun/ppermute | solution.py:68
  114.5 25.2 %collective-permute-start.11 = (bf16[1,2048,128]{2,1,0:T(8,128)(2,1)S(1)}, bf16[1,2048,128]{2,1,0:T(8,128)(2,1)S(1)}, u32[]{:S(2)}, u32[]{:S(2)}) collective-permute-start(bf16[1,2048,128]{2,1,0:T(8,128)(2,1)S(1)} %get-tuple-element.624), channel_id=1, source_target_pairs={{0,32},{1,33},{2,34},{3,35},{4,36},{5,37},{6,38},{7,39},{8,40},{9,... | collective-permute-start | bytes 1572872 | tf_op jit(solution)/shard_map/cond/branch_0_fun/ppermute | solution.py:68
  119.0 22.0 %collective-permute-start.12 = (bf16[1,2048,128]{2,1,0:T(8,128)(2,1)S(1)}, bf16[1,2048,128]{2,1,0:T(8,128)(2,1)S(1)}, u32[]{:S(2)}, u32[]{:S(2)}) collective-permute-start(bf16[1,2048,128]{2,1,0:T(8,128)(2,1)S(1)} %get-tuple-element.625), channel_id=1, source_target_pairs={{0,48},{1,49},{2,50},{3,51},{4,52},{5,53},{6,54},{7,55},{8,56},{9,... | collective-permute-start | bytes 1572872 | tf_op jit(solution)/shard_map/cond/branch_0_fun/ppermute | solution.py:68
  141.0 7.1 copy-start.2
  141.0 7.3 %copy-start.4 = (bf16[1,8192,16]{1,2,0:T(8,128)(2,1)S(1)}, bf16[1,8192,16]{1,2,0:T(8,128)(2,1)}, u32[]{:S(2)}) copy-start(bf16[1,8192,16]{1,2,0:T(8,128)(2,1)} %get-tuple-element.378) | copy-start | bytes 786436 | tf_op jit(solution)/shard_map/cond
  142.6 25.6 %collective-permute-start.13 = (bf16[4,2048,128]{2,1,0:T(8,128)(2,1)}, bf16[4,2048,128]{2,1,0:T(8,128)(2,1)}, u32[]{:S(2)}, u32[]{:S(2)}) collective-permute-start(bf16[4,2048,128]{2,1,0:T(8,128)(2,1)} %pad_maximum_fusion), channel_id=1, source_target_pairs={{0,1},{1,0},{2,3},{3,2},{4,5},{5,4},{6,7},{7,6},{8,9},{9,8},{10,11... | collective-permute-start | bytes 6291464 | tf_op jit(solution)/shard_map/cond/branch_0_fun/ppermute | solution.py:46
  146.1 22.2 %collective-permute-start.4 = (bf16[4,2048,128]{2,1,0:T(8,128)(2,1)}, bf16[4,2048,128]{2,1,0:T(8,128)(2,1)}, u32[]{:S(2)}, u32[]{:S(2)}) collective-permute-start(bf16[4,2048,128]{2,1,0:T(8,128)(2,1)} %all-to-all-done), channel_id=1, source_target_pairs={{0,1},{1,0},{2,3},{3,2},{4,5},{5,4},{6,7},{7,6},{8,9},{9,8},{10,11... | collective-permute-start | bytes 6291464 | tf_op jit(solution)/shard_map/cond/branch_0_fun/ppermute | solution.py:46
  148.5 17.8 %copy-start.7 = (s32[256,1]{0,1:T(1,128)S(1)}, s32[256,1]{0,1:T(1,128)}, u32[]{:S(2)}) copy-start(s32[256,1]{0,1:T(1,128)} %get-tuple-element.383) | copy-start | bytes 3076 | tf_op jit(solution)/shard_map/cond
  148.9 10.6 %collective-permute-start.5 = (bf16[1,32,2048]{2,1,0:T(8,128)(2,1)S(1)}, bf16[1,32,2048]{2,1,0:T(8,128)(2,1)S(1)}, u32[]{:S(2)}, u32[]{:S(2)}) collective-permute-start(bf16[1,32,2048]{2,1,0:T(8,128)(2,1)S(1)} %get-tuple-element.641), channel_id=1, source_target_pairs={{0,2},{1,3},{2,4},{3,5},{4,6},{5,7},{6,0},{7,1},{8,10},{9,11},{10,... | collective-permute-start | bytes 393224 | tf_op jit(solution)/shard_map/cond/branch_0_fun/ppermute | solution.py:68
  152.0 8.4 %collective-permute-start.6 = (bf16[1,32,2048]{2,1,0:T(8,128)(2,1)S(1)}, bf16[1,32,2048]{2,1,0:T(8,128)(2,1)S(1)}, u32[]{:S(2)}, u32[]{:S(2)}) collective-permute-start(bf16[1,32,2048]{2,1,0:T(8,128)(2,1)S(1)} %get-tuple-element.640), channel_id=1, source_target_pairs={{0,4},{1,5},{2,6},{3,7},{4,0},{5,1},{6,2},{7,3},{8,12},{9,13},{10,... | collective-permute-start | bytes 393224 | tf_op jit(solution)/shard_map/cond/branch_0_fun/ppermute | solution.py:68
  156.4 5.7 collective-permute-start.7
  162.2 5.6 collective-permute-start.8
  169.8 517.1 %copy-start.6 = (s32[256,1]{0,1:T(1,128)S(1)}, s32[256,1]{0,1:T(1,128)}, u32[]{:S(2)}) copy-start(s32[256,1]{0,1:T(1,128)} %param.31) | copy-start | bytes 3076
  171.0 436.3 %collective-permute-start.2 = (bf16[128,512]{1,0:T(8,128)(2,1)}, bf16[128,512]{1,0:T(8,128)(2,1)}, u32[]{:S(2)}, u32[]{:S(2)}) collective-permute-start(bf16[128,512]{1,0:T(8,128)(2,1)} %param.8), channel_id=1, source_target_pairs={{0,72},{1,73},{2,74},{3,75},{4,76},{5,77},{6,78},{7,79},{8,64},{9,... | collective-permute-start | bytes 393224 | tf_op jit(solution)/shard_map/while/body/eval_jaxpr/cond/branch_1_fun/cond/branch_1_fun/ppermute | solution.py:399
  172.3 435.0 %collective-permute-start.3 = (bf16[128,512]{1,0:T(8,128)(2,1)}, bf16[128,512]{1,0:T(8,128)(2,1)}, u32[]{:S(2)}, u32[]{:S(2)}) collective-permute-start(bf16[128,512]{1,0:T(8,128)(2,1)} %param.8), channel_id=1, source_target_pairs={{0,64},{1,65},{2,66},{3,67},{4,68},{5,69},{6,70},{7,71},{8,72},{9,... | collective-permute-start | bytes 393224 | tf_op jit(solution)/shard_map/while/body/eval_jaxpr/cond/branch_1_fun/cond/branch_1_fun/ppermute | solution.py:399
  622.9 10.7 %all-to-all-start.7 = ((bf16[4,144,512]{2,1,0:T(8,128)(2,1)}), bf16[4,144,512]{2,1,0:T(8,128)(2,1)S(1)}, u32[]{:S(2)}, u32[]{:S(2)}) async-start(bf16[4,144,512]{2,1,0:T(8,128)(2,1)} %project.1), calls=%async_computation.7 | async-start | bytes 1179648 | tf_op jit(solution)/shard_map/while/body/eval_jaxpr/cond/branch_1_fun/all_to_all | solution.py:42
  634.5 7.8 %collective-permute-start.26 = (bf16[128,256]{1,0:T(8,128)(2,1)}, bf16[128,256]{1,0:T(8,128)(2,1)S(1)}, u32[]{:S(2)}, u32[]{:S(2)}) collective-permute-start(bf16[128,256]{1,0:T(8,128)(2,1)} %get-tuple-element.788.own_ref), channel_id=1, source_target_pairs={{0,1},{2,3},{4,5},{6,7},{8,9},{10,11},{12,13},{14,15},{16,17},{18,... | collective-permute-start | bytes 196616 | tf_op jit(solution)/shard_map/while/body/eval_jaxpr/cond/branch_1_fun/ppermute | solution.py:389
  657.8 11.4 %all-to-all-start.3 = ((bf16[4,128,512]{2,1,0:T(8,128)(2,1)}), bf16[4,128,512]{2,1,0:T(8,128)(2,1)S(1)}, u32[]{:S(2)}, u32[]{:S(2)}) async-start(bf16[4,128,512]{2,1,0:T(8,128)(2,1)} %output.2), calls=%async_computation.3 | async-start | bytes 1048576 | tf_op jit(solution)/shard_map/while/body/eval_jaxpr/cond/branch_1_fun/cond/branch_0_fun/all_to_all | solution.py:42
  671.8 33.9 %all-to-all-start.8 = ((bf16[8,128,256]{2,1,0:T(8,128)(2,1)}), bf16[8,128,256]{2,1,0:T(8,128)(2,1)S(1)}, u32[]{:S(2)}, u32[]{:S(2)}) async-start(bf16[8,128,256]{2,1,0:T(8,128)(2,1)} %broadcast_in_dim.92), calls=%async_computation.8 | async-start | bytes 1048576 | tf_op jit(solution)/shard_map/all_to_all | solution.py:42
  684.9 13.7 %collective-permute-start.30 = (bf16[128,256]{0,1:T(8,128)(2,1)S(1)}, bf16[128,256]{0,1:T(8,128)(2,1)S(1)}, u32[]{:S(2)}, u32[]{:S(2)}) collective-permute-start(bf16[128,256]{0,1:T(8,128)(2,1)S(1)} %dynamic-slice_bitcast_fusion.3), channel_id=1, source_target_pairs={{0,8},{1,9},{2,10},{3,11},{4,12},{5,13},{6,14},{7,15},{8,0},{9,1},... | collective-permute-start | bytes 196616 | tf_op jit(solution)/shard_map/ppermute | solution.py:431
  698.8 6.9 collective-permute-start.31
  706.2 3.1 collective-permute-start.32

commit v6 on v5

--- a/solution.py
+++ b/solution.py
@@ -75,12 +75,16 @@
     )
 
 
-def relayout_kv(w_key, w_value, core, x):
+def kv_blocks(w_key, w_value, x):
     both = jnp.stack([w_key.T, w_value.T])
     width = both.shape[1]
     both = both.reshape(2, width, NG, NX, CHIP).transpose(3, 0, 1, 2, 4)
     both = both.reshape(NX, 2 * width, NG * CHIP)
-    mine = from_ring(lambda i: lax.dynamic_slice_in_dim(both, i, 1, 0), x, NC)
+    return from_ring(lambda i: lax.dynamic_slice_in_dim(both, i, 1, 0), x, NC)
+
+
+def relayout_kv(mine, core, x):
+    width = mine.shape[1] // 2
     other = in_order(swap_cores(mine), x).reshape(NX, 2, 1, width, NG * CHIP)
     mine = in_order(mine, x).reshape(NX, 2, 1, width, NG * CHIP)
     full = by_core(core, mine, other, 2)
@@ -95,59 +99,73 @@
     return pl.ds(pl.multiple_of(block * HD, HD), size * HD)
 
 
+def fetch(own_ref, other_ref, weights, sems):
+    copies = []
+    for i in range(weights.shape[1]):
+        pair = []
+        for k, ref in enumerate((own_ref, other_ref)):
+            copy = pltpu.make_async_copy(ref.at[i], weights.at[k, i], sems.at[k, i])
+            copy.start()
+            pair.append(copy)
+        copies.append(pair)
+    return copies
+
+
 def project_kernel(
-    info_ref, h_ref, gain_ref, own_ref, other_ref, wkv_ref, out_ref, normed, kv, squares
+    info_ref, h_ref, gain_ref, wkv_ref, own_ref, other_ref, out_ref, normed, weights, sems
 ):
-    @pl.when(pl.program_id(0) == 0)
-    def _():
-        total = jnp.zeros((HALF, 1), jnp.float32)
-        for y in range(NY):
-            part = h_ref[y].astype(jnp.float32)
-            cols = slice(y * NZ * CHIP, (y + 1) * NZ * CHIP)
-            normed[:, cols] = (part * gain_ref[:, cols]).astype(jnp.bfloat16)
-            total = total + jnp.sum(part * part, axis=1, keepdims=True)
-        row = jnp.sum(jnp.where(eye(HALF), total, 0.0), axis=0, keepdims=True)
-        high = row.astype(jnp.bfloat16).astype(jnp.float32)
-        upper = lax.broadcasted_iota(jnp.int32, (16, HALF), 0) < 8
-        squares[...] = jnp.where(upper, high, row - high)
-        kv[...] = lax.dot_general(
-            normed[...], wkv_ref[...], (((1,), (1,)), ((), ())), preferred_element_type=jnp.float32
-        )
-
-    weight = jnp.concatenate([own_ref[0], other_ref[0]], axis=1)
-    query = jnp.dot(normed[...], weight, preferred_element_type=jnp.float32).astype(jnp.bfloat16)
+    copies = fetch(own_ref, other_ref, weights, sems)
+    total = jnp.zeros((HALF, 1), jnp.float32)
+    for y in range(NY):
+        part = h_ref[y].astype(jnp.float32)
+        cols = slice(y * NZ * CHIP, (y + 1) * NZ * CHIP)
+        normed[:, cols] = (part * gain_ref[:, cols]).astype(jnp.bfloat16)
+        total = total + jnp.sum(part * part, axis=1, keepdims=True)
+    row = jnp.sum(jnp.where(eye(HALF), total, 0.0), axis=0, keepdims=True)
+    high = row.astype(jnp.bfloat16).astype(jnp.float32)
+    upper = lax.broadcasted_iota(jnp.int32, (16, HALF), 0) < 8
+    squares = jnp.where(upper, high, row - high).astype(jnp.bfloat16)
+    kv = lax.dot_general(
+        normed[...], wkv_ref[...], (((1,), (1,)), ((), ())), preferred_element_type=jnp.float32
+    ).astype(jnp.bfloat16)
     core = info_ref[0]
-    out_ref[0, :HALF, aligned(core)] = query[:, :HD]
-    out_ref[0, :HALF, aligned(1 - core)] = query[:, HD:]
-    out_ref[0, :HALF, CHIP:] = kv[...].astype(jnp.bfloat16)
-    out_ref[0, HALF:, :] = jnp.zeros((16, 2 * CHIP), jnp.bfloat16)
-    out_ref[0, HALF:, :HALF] = squares[...].astype(jnp.bfloat16)
+    for i in range(NX):
+        out_ref[i, :HALF, CHIP:] = kv
+        out_ref[i, HALF:, :] = jnp.zeros((16, 2 * CHIP), jnp.bfloat16)
+        out_ref[i, HALF:, :HALF] = squares
+        for copy in copies[i]:
+            copy.wait()
+        weight = jnp.concatenate([weights[0, i], weights[1, i]], axis=1)
+        query = jnp.dot(normed[...], weight, preferred_element_type=jnp.float32)
+        query = query.astype(jnp.bfloat16)
+        out_ref[i, :HALF, aligned(core)] = query[:, :HD]
+        out_ref[i, :HALF, aligned(1 - core)] = query[:, HD:]
+
+
+def weight_scratch():
+    rows = NG * CHIP
+    return [pltpu.VMEM((2, NX, rows, HD), jnp.bfloat16), pltpu.SemaphoreType.DMA((2, NX))]
 
 
 def project(info, gathered, gain, wq, wkv):
     rows = NG * CHIP
-    block = pl.BlockSpec((1, rows, HD), lambda i: (i, 0, 0))
+    vmem = pl.BlockSpec(memory_space=pltpu.VMEM)
     return pl.pallas_call(
         project_kernel,
-        grid=(NX,),
         in_specs=[
             pl.BlockSpec(memory_space=pltpu.SMEM),
-            pl.BlockSpec((NY, HALF, NZ * CHIP), lambda i: (0, 0, 0)),
-            pl.BlockSpec((1, rows), lambda i: (0, 0)),
-            block,
-            block,
-            pl.BlockSpec((2 * HD, rows), lambda i: (0, 0)),
+            vmem,
+            vmem,
+            vmem,
+            pl.BlockSpec(memory_space=pl.ANY),
+            pl.BlockSpec(memory_space=pl.ANY),
         ],
-        out_specs=pl.BlockSpec((1, HALF + 16, 2 * CHIP), lambda i: (i, 0, 0)),
+        out_specs=vmem,
         out_shape=jax.ShapeDtypeStruct((NX, HALF + 16, 2 * CHIP), jnp.bfloat16),
-        scratch_shapes=[
-            pltpu.VMEM((HALF, rows), jnp.bfloat16),
-            pltpu.VMEM((HALF, CHIP), jnp.float32),
-            pltpu.VMEM((16, HALF), jnp.float32),
-        ],
+        scratch_shapes=[pltpu.VMEM((HALF, rows), jnp.bfloat16)] + weight_scratch(),
         compiler_params=pltpu.CompilerParams(vmem_limit_bytes=VMEM),
         name="project",
-    )(info, gathered, gain, *wq, wkv)
+    )(info, gathered, gain, wkv, *wq)
 
 
 def turn_kernel(features, part_ref, cos_ref, sin_ref, q_ref, kv_ref):
@@ -226,46 +244,43 @@
     )(info, query, own, first)
 
 
-def output_kernel(halves, info_ref, ctx_ref, own_ref, other_ref, out_ref, rows):
+def output_kernel(
+    halves, info_ref, ctx_ref, own_ref, other_ref, out_ref, rows, weights, sems
+):
+    copies = fetch(own_ref, other_ref, weights, sems)
     depth = rows.shape[1]
-
-    @pl.when(pl.program_id(0) == 0)
-    def _():
-        for i in range(depth // CHIP):
-            rows[:, i * CHIP : (i + 1) * CHIP] = ctx_ref[i]
-
-    core, z = info_ref[0], info_ref[2]
-    for part in range(halves):
-        cut = slice(part * depth, (part + 1) * depth)
-        weight = jnp.concatenate([own_ref[0, cut], other_ref[0, cut]], axis=1)
-        total = jnp.dot(rows[...], weight, preferred_element_type=jnp.float32)
-        total = total.astype(jnp.bfloat16)
-        first = (z if part == 0 else 1 - z) * NC if halves > 1 else 0
-        out_ref[0, :, aligned(first + core)] = total[:, :HD]
-        out_ref[0, :, aligned(first + 1 - core)] = total[:, HD:]
+    for i in range(depth // CHIP):
+        rows[:, i * CHIP : (i + 1) * CHIP] = ctx_ref[i]
+    core, z, y = info_ref[0], info_ref[2], info_ref[3]
+    for i in range(NY):
+        for copy in copies[i]:
+            copy.wait()
+        source = lax.rem(y + NY - i, NY)
+        for part in range(halves):
+            cut = slice(part * depth, (part + 1) * depth)
+            weight = jnp.concatenate([weights[0, i, cut], weights[1, i, cut]], axis=1)
+            total = jnp.dot(rows[...], weight, preferred_element_type=jnp.float32)
+            total = total.astype(jnp.bfloat16)
+            first = (z if part == 0 else 1 - z) * NC if halves > 1 else 0
+            out_ref[source, :, aligned(first + core)] = total[:, :HD]
+            out_ref[source, :, aligned(first + 1 - core)] = total[:, HD:]
 
 
 def output(info, context, wo):
     count = context.shape[0]
     halves = NG // count
-    rows = NG * CHIP
-    block = pl.BlockSpec((1, rows, HD), lambda i, info: (i, 0, 0))
+    vmem = pl.BlockSpec(memory_space=pltpu.VMEM)
     return pl.pallas_call(
         functools.partial(output_kernel, halves),
-        grid_spec=pltpu.PrefetchScalarGridSpec(
-            num_scalar_prefetch=1,
-            grid=(NY,),
-            in_specs=[
-                pl.BlockSpec((count, HALF, CHIP), lambda i, info: (0, 0, 0)),
-                block,
-                block,
-            ],
-            out_specs=pl.BlockSpec(
-                (1, HALF, halves * CHIP), lambda i, info: (lax.rem(info[3] + NY - i, NY), 0, 0)
-            ),
-            scratch_shapes=[pltpu.VMEM((HALF, count * CHIP), jnp.bfloat16)],
-        ),
+        in_specs=[
+            pl.BlockSpec(memory_space=pltpu.SMEM),
+            vmem,
+            pl.BlockSpec(memory_space=pl.ANY),
+            pl.BlockSpec(memory_space=pl.ANY),
+        ],
+        out_specs=vmem,
         out_shape=jax.ShapeDtypeStruct((NY, HALF, halves * CHIP), jnp.bfloat16),
+        scratch_shapes=[pltpu.VMEM((HALF, count * CHIP), jnp.bfloat16)] + weight_scratch(),
         compiler_params=pltpu.CompilerParams(vmem_limit_bytes=VMEM),
         name="output",
     )(info, context, *wo)
@@ -333,9 +348,11 @@
 
     raw = w_out[0].reshape(NY, NZ * NX * CHIP, HD)
 
-    def prepare(out_rows):
+    def prepare(out_rows, before):
         query = exchange(x_blocks(w_query[0]), OVER_X)
-        key_value = relayout_kv(w_key[0], w_value[0], core, x)
+        mine = kv_blocks(w_key[0], w_value[0], x)
+        out_rows = lax.optimization_barrier((out_rows, mine, before))[0]
+        key_value = relayout_kv(mine, core, x)
         out = from_ring(lambda i: lax.dynamic_slice_in_dim(out_rows, i, 1, 0), y, 16)
         return (query, swap_cores(query)), key_value, (out, swap_cores(out))
 
@@ -347,7 +364,7 @@
         )
         gathered = in_order(from_ring(lambda i: pair[None], y, 16), y)
         items = jnp.zeros((ITEMS_HERE,), jnp.int32)
-        return gathered, prepare(raw), (items, items)
+        return gathered, prepare(raw, gathered), (items, items)
 
     def later_section(start, cross):
         halves = raw.reshape(NY, NZ, NX * CHIP, HD)
@@ -356,7 +373,7 @@
         far = lax.ppermute(given, "wide", Z_SWAP)
         out_rows = jnp.concatenate([kept, far], axis=1)
         blank = jnp.zeros((NY, HALF, NZ * CHIP), jnp.bfloat16)
-        return blank, prepare(out_rows), ranks(placement, core)
+        return blank, prepare(out_rows, start), ranks(placement, core)
 
     gathered, (wq, wkv, wo), items = lax.cond(
         segment == 0, first_section, later_section, start, cross

time: 712 us -> 717 us (level)
  other arithmetic: 8.27 us -> 18.4 us
  waiting for transfers between devices: 574 us -> 565 us
    ppermute x1, waiting for transfers between devices: 82.4 us -> 63 us  [later_section(): far = lax.ppermute(given, 'wide', Z_SWAP)]
    ppermute x2, waiting for transfers between devices: 434 us -> 445 us  [run(): return (lax.ppermute(value, axes, cross), lax.ppermute(value, axes, same))]
  transfers between devices with their start and end apart: 23 -> 23, of which waited for: 15 -> 13; matrix products, arithmetic and copies ran while one was open for 1% -> 3% of each run, Pallas kernels for 0% -> 0%
where the time goes in v6:
time: 717 us; the launch traced here: 716 us
  waiting for transfers between devices  565 us (79%)
  starting transfers between devices  81.3 us (11%)
  other arithmetic  18.4 us (3%)
  blocking collectives  18.1 us (3%)
  local copies, waits for them, and re-layouts  17.5 us (2%)
  Pallas kernels  11.4 us (2%)
    ppermute x2, waiting for transfers between devices, run(): return (lax.ppermute(value, axes, cross), lax.ppermute(value, axes, same))  445 us
    ppermute x1, waiting for transfers between devices, later_section(): far = lax.ppermute(given, 'wide', Z_SWAP)  63 us
    all_to_all x4, starting transfers between devices, exchange(): lax.all_to_all(value, 'wide', 0, 0, axis_index_groups=groups, tiled=True)  23.5 us
    ppermute x6, starting transfers between devices, from_ring(): blocks.append(lax.ppermute(piece((at + step) % 4), 'wide', pairs))  21.2 us
    ppermute x6, waiting for transfers between devices, from_ring(): blocks.append(lax.ppermute(piece((at + step) % 4), 'wide', pairs))  19 us
    ppermute x6, starting transfers between devices, swap_cores(): return lax.ppermute(value, 'wide', CORE_SWAP)  18.7 us
    all_to_all x2, blocking collectives, exchange(): lax.all_to_all(value, 'wide', 0, 0, axis_index_groups=groups, tiled=True)  18.1 us
    all_to_all x4, waiting for transfers between devices, exchange(): lax.all_to_all(value, 'wide', 0, 0, axis_index_groups=groups, tiled=True)  14.7 us
  transfers between devices with their start and end apart: 23, of which 13 were waited for; matrix products, arithmetic and copies ran while one was open for 3% of the time, Pallas kernels for 0%

profile of v6, /device:TPU:481, one launch (start us, length us, event | category | flops | bytes accessed | tf_op | source)
XLA Modules:
  0.0 715.7 jit_solution(13219019531337911090)
XLA Ops:
  12.3 145.6 %conditional.7 = (bf16[4,128,512]{2,1,0:T(8,128)(2,1)S(1)}, bf16[4,2048,128]{2,1,0:T(8,128)(2,1)}, bf16[4,2048,128]{2,1,0:T(8,128)(2,1)}, bf16[256,2048]{1,0:T(8...) conditional(s32[]{:T(128)} %convert_element_type.97, ...), branch_computations={%region_0.4_spmd, %region_4.5_spmd} | conditional | flops 11503095 | bytes 82849584 | solution.py:378
  15.1 9.5 %collective-permute-start.9 = (bf16[4,1024,128]{2,1,0:T(8,128)(2,1)}, bf16[4,1024,128]{2,1,0:T(8,128)(2,1)}, u32[]{:S(2)}, u32[]{:S(2)}) collective-permute-start(bf16[4,1024,128]{2,1,0:T(8,128)(2,1)} %get-tuple-element.630), channel_id=1, source_target_pairs={{0,8},{1,9},{2,10},{3,11},{4,12},{5,13},{6,14},{7,15},{8,0},{9,1},... | collective-permute-start | bytes 3145736 | tf_op jit(solution)/shard_map/cond/branch_0_fun/ppermute | solution.py:373
  32.7 3.1 collective-permute-start.5
  35.8 4.4 collective-permute-start.6
  40.2 3.1 collective-permute-start.7
  44.7 4.5 all-to-all-start
  50.3 63.0 %collective-permute-done.9 = bf16[4,1024,128]{2,1,0:T(8,128)(2,1)} collective-permute-done((bf16[4,1024,128]{2,1,0:T(8,128)(2,1)}, bf16[4,1024,128]{2,1,0:T(8,128)(2,1)}, u32[]{:S(2)}, u32[]{:S(2)}) %collective-permute-start.9) | collective-permute-done | bytes 1048608 | tf_op jit(solution)/shard_map/cond/branch_0_fun/ppermute | solution.py:373
  114.9 3.2 collective-permute-start.10
  118.1 4.5 collective-permute-start.11
  122.7 3.0 collective-permute-start.12
  125.6 5.4 collective-permute-done.10
  131.0 12.3 %collective-permute-done.11 = bf16[1,2048,128]{2,1,0:T(8,128)(2,1)S(1)} collective-permute-done((bf16[1,2048,128]{2,1,0:T(8,128)(2,1)S(1)}, bf16[1,2048,128]{2,1,0:T(8,128)(2,1)S(1)}, u32[]{:S(2)}, u32[]{:S(2)}) %collective-permute-start.11) | collective-permute-done | bytes 524320 | tf_op jit(solution)/shard_map/cond/branch_0_fun/ppermute | solution.py:68
  146.3 3.5 collective-permute-start.13
  159.2 515.9 %while.25 = (s32[]{:T(128)}, bf16[4,128,512]{2,1,0:T(8,128)(2,1)S(1)}, bf16[128,512]{1,0:T(8,128)(2,1)}, bf16[128,256]{1,0:T(8,128)(2,1)}, s32[]{:T(128)}, /*ind...) while((s32[]{:T(128)}, ...), condition=%wide.region_16.17_spmd.clone.clone, body=%wide.region_5.16_spmd.clone.clone.sunk | while | flops 1015839 | bytes 11800991 | solution.py:443
  164.8 458.5 %conditional.16 = (bf16[4,128,512]{2,1,0:T(8,128)(2,1)S(1)}) conditional(s32[]{:T(128)} %convert_element_type.136, bf16[4,128,512]{2,1,0:T(8,128)(2,1)S(1)} %get-tuple-element.828, (s32[]{:T(128)}, s32[]{:T(128)}, bf16[128,512]{1,0:T(8,128)(2,1)}, bf16[4,128,512]{2,1,0:T(8,128)(2,1)S(1)}) %tuple.151), branch_computations={%region_10.10_spmd, %region_11.15_spmd} | conditional | flops 262160 | bytes 4194573 | solution.py:432
  164.8 448.0 %conditional.1 = (bf16[128,512]{1,0:T(8,128)(2,1)}, bf16[128,512]{1,0:T(8,128)(2,1)}) conditional(s32[]{:T(128)} %convert_element_type.83, bf16[128,512]{1,0:T(8,128)(2,1)} %get-tuple-element.429, bf16[128,512]{1,0:T(8,128)(2,1)} %get-tuple-element.429), branch_computations={%region_12.11_spmd, %region_13.12_spmd} | conditional | bytes 1048672 | solution.py:427
  167.4 445.4 %collective-permute-done.2 = bf16[128,512]{1,0:T(8,128)(2,1)} collective-permute-done((bf16[128,512]{1,0:T(8,128)(2,1)}, bf16[128,512]{1,0:T(8,128)(2,1)}, u32[]{:S(2)}, u32[]{:S(2)}) %collective-permute-start.2) | collective-permute-done | bytes 131104 | tf_op jit(solution)/shard_map/while/body/eval_jaxpr/cond/branch_1_fun/cond/branch_1_fun/ppermute | solution.py:416
  612.8 10.4 %conditional.2 = (bf16[4,128,512]{2,1,0:T(8,128)(2,1)S(1)}) conditional(s32[]{:T(128)} %convert_element_type.82, bf16[4,128,512]{2,1,0:T(8,128)(2,1)S(1)} %get-tuple-element.428, (bf16[128,512]{1,0:T(8,128)(2,1)}, bf16[128,512]{1,0:T(8,128)(2,1)}) %tuple.64), branch_computations={%region_14.13_spmd, %region_15.14_spmd} | conditional | flops 262144 | bytes 3145736 | solution.py:428
  613.9 9.3 %all_to_all.39 = bf16[4,128,512]{2,1,0:T(8,128)(2,1)S(1)} all-to-all(bf16[4,128,512]{2,1,0:T(8,128)(2,1)S(1)} %broadcast_in_dim.66), channel_id=1, replica_groups={{0,16,32,48},{1,17,33,49},{2,18,34,50},{3,19,35,51},{4,20,36,52},{5,21,..., dimensions={0} | all-to-all | bytes 1048576 | tf_op jit(solution)/shard_map/while/body/eval_jaxpr/cond/branch_1_fun/cond/branch_1_fun/all_to_all | solution.py:42
  624.0 51.1 %conditional.15 = ((bf16[128,512]{1,0:T(8,128)(2,1)}, bf16[128,256]{1,0:T(8,128)(2,1)})) conditional(s32[]{:T(128)} %convert_element_type.137, (bf16[128,512]{1,0:T(8,128)(2,1)}, bf16[128,256]{1,0:T(8,128)(2,1)}) %tuple.149, (s32[]{:T(128)}, s32[4]{0:T(128)S(1)}, bf16[4,128,512]{2,1,0:T(8,128)(2,1)S(1)}, f32[1,2048]{1,0:T(1,128)S(1)}, ...), branch_computations={%region_6.6_spmd, %region_7.9_spmd} | conditional | flops 737286 | bytes 7539474 | solution.py:424
  624.0 4.9 project.1
  628.9 3.5 all-to-all-start.7
  632.9 6.8 all-to-all-done.7.part_ref
  641.9 6.5 collective-permute-done.26.first_ref
  650.1 25.0 %conditional = (bf16[128,512]{1,0:T(8,128)(2,1)}) conditional(s32[]{:T(128)} %convert_element_type.78, (s32[]{:T(128)}, bf16[128,512]{1,0:T(8,128)(2,1)S(1)}, bf16[4,128,256]{2,1,0:T(8,128)(2,1)S(1)}, s32[4]{0:T(128)S(1)}, bf16[4,2048,128]{2,1,0:T(8,128)(2,1)}, /*index=5*/bf16[4,2048,128]{2,1,0:T(8,128)(2,1)}) %tuple.59, (s32[]{:T(128)}, ...), branch_computations={%region_8.7_spmd, %region_9.8_spmd} | conditional | flops 720897 | bytes 4980786 | solution.py:409
  650.1 8.8 %all_to_all.37.ctx_ref = bf16[4,128,256]{2,1,0:T(8,128)(2,1)S(1)} all-to-all(bf16[4,128,256]{2,1,0:T(8,128)(2,1)S(1)} %get-tuple-element.400), channel_id=1, replica_groups={{0,2,4,6},{1,3,5,7},{8,10,12,14},{9,11,13,15},{16,18,20,22},{17,19,21,2..., dimensions={0} | all-to-all | bytes 524288 | tf_op jit(solution)/shard_map/while/body/eval_jaxpr/cond/branch_1_fun/cond/branch_0_fun/all_to_all | solution.py:42
  658.9 3.9 output.2
  662.8 3.5 all-to-all-start.3
  666.3 7.9 %all-to-all-done.3 = bf16[4,128,512]{2,1,0:T(8,128)(2,1)S(1)} async-done(((bf16[4,128,512]{2,1,0:T(8,128)(2,1)}), bf16[4,128,512]{2,1,0:T(8,128)(2,1)S(1)}, u32[]{:S(2)}, u32[]{:S(2)}) %all-to-all-start.3) | async-done | bytes 524320 | tf_op jit(solution)/shard_map/while/body/eval_jaxpr/cond/branch_1_fun/cond/branch_0_fun/all_to_all | solution.py:42
  676.8 12.1 %all-to-all-start.8 = ((bf16[8,128,256]{2,1,0:T(8,128)(2,1)}), bf16[8,128,256]{2,1,0:T(8,128)(2,1)S(1)}, u32[]{:S(2)}, u32[]{:S(2)}) async-start(bf16[8,128,256]{2,1,0:T(8,128)(2,1)} %broadcast_in_dim.92), calls=%async_computation.8 | async-start | bytes 1048576 | tf_op jit(solution)/shard_map/all_to_all | solution.py:42
  691.9 11.8 %collective-permute-done.30 = bf16[128,256]{0,1:T(8,128)(2,1)S(1)} collective-permute-done((bf16[128,256]{0,1:T(8,128)(2,1)S(1)}, bf16[128,256]{0,1:T(8,128)(2,1)S(1)}, u32[]{:S(2)}, u32[]{:S(2)}) %collective-permute-start.30) | collective-permute-done | bytes 65568 | tf_op jit(solution)/shard_map/ppermute | solution.py:448
  703.8 6.1 collective-permute-start.31
  (123 shorter events, 63.0 us)
Async XLA Ops:
  1.4 7.8 %collective-permute-start.27 = (bf16[128,128]{1,0:T(8,128)(2,1)S(1)}, bf16[128,128]{1,0:T(8,128)(2,1)S(1)}, u32[]{:S(2)}, u32[]{:S(2)}) collective-permute-start(bf16[128,128]{1,0:T(8,128)(2,1)S(1)} %dynamic-slice_bitcast_fusion.4), channel_id=1, source_target_pairs={{0,1},{1,0},{2,3},{3,2},{4,5},{5,4},{6,7},{7,6},{8,9},{9,8},{10,11... | collective-permute-start | bytes 98312 | tf_op jit(solution)/shard_map/ppermute | solution.py:46
  4.0 7.4 %collective-permute-start.29 = (bf16[128,128]{1,0:T(8,128)(2,1)S(1)}, bf16[128,128]{1,0:T(8,128)(2,1)S(1)}, u32[]{:S(2)}, u32[]{:S(2)}) collective-permute-start(bf16[128,128]{1,0:T(8,128)(2,1)S(1)} %dynamic-slice_bitcast_fusion.4), channel_id=1, source_target_pairs={{448,9},{449,8},{450,11},{451,10},{452,13},{453,12},{454,15},{455,... | collective-permute-start | bytes 98312 | tf_op jit(solution)/shard_map/ppermute | solution.py:331
  10.0 2.3 collective-permute-start.28
  12.4 12.3 %copy-start.3 = (bf16[1,8192,16]{1,2,0:T(8,128)(2,1)S(1)}, bf16[1,8192,16]{1,2,0:T(8,128)(2,1)}, u32[]{:S(2)}) copy-start(bf16[1,8192,16]{1,2,0:T(8,128)(2,1)} %get-tuple-element.378) | copy-start | bytes 786436 | tf_op jit(solution)/shard_map/cond
  15.1 98.3 %collective-permute-start.9 = (bf16[4,1024,128]{2,1,0:T(8,128)(2,1)}, bf16[4,1024,128]{2,1,0:T(8,128)(2,1)}, u32[]{:S(2)}, u32[]{:S(2)}) collective-permute-start(bf16[4,1024,128]{2,1,0:T(8,128)(2,1)} %get-tuple-element.630), channel_id=1, source_target_pairs={{0,8},{1,9},{2,10},{3,11},{4,12},{5,13},{6,14},{7,15},{8,0},{9,1},... | collective-permute-start | bytes 3145736 | tf_op jit(solution)/shard_map/cond/branch_0_fun/ppermute | solution.py:373
  25.6 17.6 %copy-start = (bf16[1,8192,128]{2,1,0:T(8,128)(2,1)S(1)}, bf16[1,8192,128]{2,1,0:T(8,128)(2,1)}, u32[]{:S(2)}) copy-start(bf16[1,8192,128]{2,1,0:T(8,128)(2,1)} %get-tuple-element.376) | copy-start | bytes 6291460 | tf_op jit(solution)/shard_map/cond
  32.7 16.6 %collective-permute-start.5 = (bf16[1,32,2048]{2,1,0:T(8,128)(2,1)}, bf16[1,32,2048]{2,1,0:T(8,128)(2,1)S(1)}, u32[]{:S(2)}, u32[]{:S(2)}) collective-permute-start(bf16[1,32,2048]{2,1,0:T(8,128)(2,1)} %get-tuple-element.644), channel_id=1, source_target_pairs={{0,2},{1,3},{2,4},{3,5},{4,6},{5,7},{6,0},{7,1},{8,10},{9,11},{10,... | collective-permute-start | bytes 393224 | tf_op jit(solution)/shard_map/cond/branch_0_fun/ppermute | solution.py:68
  35.8 13.5 %collective-permute-start.6 = (bf16[1,32,2048]{2,1,0:T(8,128)(2,1)}, bf16[1,32,2048]{2,1,0:T(8,128)(2,1)}, u32[]{:S(2)}, u32[]{:S(2)}) collective-permute-start(bf16[1,32,2048]{2,1,0:T(8,128)(2,1)} %get-tuple-element.643), channel_id=1, source_target_pairs={{0,4},{1,5},{2,6},{3,7},{4,0},{5,1},{6,2},{7,3},{8,12},{9,13},{10,... | collective-permute-start | bytes 393224 | tf_op jit(solution)/shard_map/cond/branch_0_fun/ppermute | solution.py:68
  40.2 9.1 %collective-permute-start.7 = (bf16[1,32,2048]{2,1,0:T(8,128)(2,1)S(1)}, bf16[1,32,2048]{2,1,0:T(8,128)(2,1)}, u32[]{:S(2)}, u32[]{:S(2)}) collective-permute-start(bf16[1,32,2048]{2,1,0:T(8,128)(2,1)S(1)} %get-tuple-element.642), channel_id=1, source_target_pairs={{0,6},{1,7},{2,0},{3,1},{4,2},{5,3},{6,4},{7,5},{8,14},{9,15},{10,... | collective-permute-start | bytes 393224 | tf_op jit(solution)/shard_map/cond/branch_0_fun/ppermute | solution.py:68
  44.7 105.0 %all-to-all-start = ((bf16[4,2048,128]{2,1,0:T(8,128)(2,1)}), bf16[4,2048,128]{2,1,0:T(8,128)(2,1)}, u32[]{:S(2)}, u32[]{:S(2)}) async-start(bf16[4,2048,128]{2,1,0:T(8,128)(2,1)} %bitcast.102), calls=%async_computation | async-start | bytes 4194304 | tf_op jit(solution)/shard_map/cond/branch_0_fun/all_to_all | solution.py:42
  114.9 16.1 %collective-permute-start.10 = (bf16[1,2048,128]{2,1,0:T(8,128)(2,1)S(1)}, bf16[1,2048,128]{2,1,0:T(8,128)(2,1)S(1)}, u32[]{:S(2)}, u32[]{:S(2)}) collective-permute-start(bf16[1,2048,128]{2,1,0:T(8,128)(2,1)S(1)} %get-tuple-element.628), channel_id=1, source_target_pairs={{0,16},{1,17},{2,18},{3,19},{4,20},{5,21},{6,22},{7,23},{8,24},{9,... | collective-permute-start | bytes 1572872 | tf_op jit(solution)/shard_map/cond/branch_0_fun/ppermute | solution.py:68
  118.1 25.2 %collective-permute-start.11 = (bf16[1,2048,128]{2,1,0:T(8,128)(2,1)S(1)}, bf16[1,2048,128]{2,1,0:T(8,128)(2,1)S(1)}, u32[]{:S(2)}, u32[]{:S(2)}) collective-permute-start(bf16[1,2048,128]{2,1,0:T(8,128)(2,1)S(1)} %get-tuple-element.627), channel_id=1, source_target_pairs={{0,32},{1,33},{2,34},{3,35},{4,36},{5,37},{6,38},{7,39},{8,40},{9,... | collective-permute-start | bytes 1572872 | tf_op jit(solution)/shard_map/cond/branch_0_fun/ppermute | solution.py:68
  122.7 22.0 %collective-permute-start.12 = (bf16[1,2048,128]{2,1,0:T(8,128)(2,1)S(1)}, bf16[1,2048,128]{2,1,0:T(8,128)(2,1)S(1)}, u32[]{:S(2)}, u32[]{:S(2)}) collective-permute-start(bf16[1,2048,128]{2,1,0:T(8,128)(2,1)S(1)} %get-tuple-element.626), channel_id=1, source_target_pairs={{0,48},{1,49},{2,50},{3,51},{4,52},{5,53},{6,54},{7,55},{8,56},{9,... | collective-permute-start | bytes 1572872 | tf_op jit(solution)/shard_map/cond/branch_0_fun/ppermute | solution.py:68
  144.6 9.5 %copy-start.5 = (s32[256,1]{0,1:T(1,128)S(1)}, s32[256,1]{0,1:T(1,128)}, u32[]{:S(2)}) copy-start(s32[256,1]{0,1:T(1,128)} %get-tuple-element.385) | copy-start | bytes 3076 | tf_op jit(solution)/shard_map/cond
  146.3 11.4 %collective-permute-start.13 = (bf16[4,2048,128]{2,1,0:T(8,128)(2,1)}, bf16[4,2048,128]{2,1,0:T(8,128)(2,1)}, u32[]{:S(2)}, u32[]{:S(2)}) collective-permute-start(bf16[4,2048,128]{2,1,0:T(8,128)(2,1)} %pad_maximum_fusion.1), channel_id=1, source_target_pairs={{0,1},{1,0},{2,3},{3,2},{4,5},{5,4},{6,7},{7,6},{8,9},{9,8},{10,11... | collective-permute-start | bytes 6291464 | tf_op jit(solution)/shard_map/cond/branch_0_fun/ppermute | solution.py:46
  149.7 7.9 %collective-permute-start.4 = (bf16[4,2048,128]{2,1,0:T(8,128)(2,1)}, bf16[4,2048,128]{2,1,0:T(8,128)(2,1)}, u32[]{:S(2)}, u32[]{:S(2)}) collective-permute-start(bf16[4,2048,128]{2,1,0:T(8,128)(2,1)} %all-to-all-done), channel_id=1, source_target_pairs={{0,1},{1,0},{2,3},{3,2},{4,5},{5,4},{6,7},{7,6},{8,9},{9,8},{10,11... | collective-permute-start | bytes 6291464 | tf_op jit(solution)/shard_map/cond/branch_0_fun/ppermute | solution.py:46
  151.7 5.6 collective-permute-start.8
  157.9 1.3 copy-start.7
  159.2 532.6 %copy-start.4 = (s32[256,1]{0,1:T(1,128)S(1)}, s32[256,1]{0,1:T(1,128)}, u32[]{:S(2)}) copy-start(s32[256,1]{0,1:T(1,128)} %param.31) | copy-start | bytes 3076
  164.8 448.0 %collective-permute-start.2 = (bf16[128,512]{1,0:T(8,128)(2,1)}, bf16[128,512]{1,0:T(8,128)(2,1)}, u32[]{:S(2)}, u32[]{:S(2)}) collective-permute-start(bf16[128,512]{1,0:T(8,128)(2,1)} %param.8), channel_id=1, source_target_pairs={{0,72},{1,73},{2,74},{3,75},{4,76},{5,77},{6,78},{7,79},{8,64},{9,... | collective-permute-start | bytes 393224 | tf_op jit(solution)/shard_map/while/body/eval_jaxpr/cond/branch_1_fun/cond/branch_1_fun/ppermute | solution.py:416
  166.1 446.7 %collective-permute-start.3 = (bf16[128,512]{1,0:T(8,128)(2,1)}, bf16[128,512]{1,0:T(8,128)(2,1)}, u32[]{:S(2)}, u32[]{:S(2)}) collective-permute-start(bf16[128,512]{1,0:T(8,128)(2,1)} %param.8), channel_id=1, source_target_pairs={{0,64},{1,65},{2,66},{3,67},{4,68},{5,69},{6,70},{7,71},{8,72},{9,... | collective-permute-start | bytes 393224 | tf_op jit(solution)/shard_map/while/body/eval_jaxpr/cond/branch_1_fun/cond/branch_1_fun/ppermute | solution.py:416
  624.0 8.7 %copy-start.6 = (f32[128]{0:T(128)S(1)}, f32[128]{0:T(128)}, u32[]{:S(2)}) copy-start(f32[128]{0:T(128)} %get-tuple-element.581) | copy-start | bytes 1540 | tf_op jit(solution)/shard_map/while/body/eval_jaxpr/cond
  628.9 10.7 %all-to-all-start.7 = ((bf16[4,144,512]{2,1,0:T(8,128)(2,1)}), bf16[4,144,512]{2,1,0:T(8,128)(2,1)S(1)}, u32[]{:S(2)}, u32[]{:S(2)}) async-start(bf16[4,144,512]{2,1,0:T(8,128)(2,1)} %project.1), calls=%async_computation.7 | async-start | bytes 1179648 | tf_op jit(solution)/shard_map/while/body/eval_jaxpr/cond/branch_1_fun/all_to_all | solution.py:42
  640.6 7.8 %collective-permute-start.26 = (bf16[128,256]{1,0:T(8,128)(2,1)}, bf16[128,256]{1,0:T(8,128)(2,1)S(1)}, u32[]{:S(2)}, u32[]{:S(2)}) collective-permute-start(bf16[128,256]{1,0:T(8,128)(2,1)} %get-tuple-element.791.own_ref), channel_id=1, source_target_pairs={{0,1},{2,3},{4,5},{6,7},{8,9},{10,11},{12,13},{14,15},{16,17},{18,... | collective-permute-start | bytes 196616 | tf_op jit(solution)/shard_map/while/body/eval_jaxpr/cond/branch_1_fun/ppermute | solution.py:406
  662.8 11.4 %all-to-all-start.3 = ((bf16[4,128,512]{2,1,0:T(8,128)(2,1)}), bf16[4,128,512]{2,1,0:T(8,128)(2,1)S(1)}, u32[]{:S(2)}, u32[]{:S(2)}) async-start(bf16[4,128,512]{2,1,0:T(8,128)(2,1)} %output.2), calls=%async_computation.3 | async-start | bytes 1048576 | tf_op jit(solution)/shard_map/while/body/eval_jaxpr/cond/branch_1_fun/cond/branch_0_fun/all_to_all | solution.py:42
  676.8 33.9 %all-to-all-start.8 = ((bf16[8,128,256]{2,1,0:T(8,128)(2,1)}), bf16[8,128,256]{2,1,0:T(8,128)(2,1)S(1)}, u32[]{:S(2)}, u32[]{:S(2)}) async-start(bf16[8,128,256]{2,1,0:T(8,128)(2,1)} %broadcast_in_dim.92), calls=%async_computation.8 | async-start | bytes 1048576 | tf_op jit(solution)/shard_map/all_to_all | solution.py:42
  689.9 13.7 %collective-permute-start.30 = (bf16[128,256]{0,1:T(8,128)(2,1)S(1)}, bf16[128,256]{0,1:T(8,128)(2,1)S(1)}, u32[]{:S(2)}, u32[]{:S(2)}) collective-permute-start(bf16[128,256]{0,1:T(8,128)(2,1)S(1)} %dynamic-slice_bitcast_fusion.3), channel_id=1, source_target_pairs={{0,8},{1,9},{2,10},{3,11},{4,12},{5,13},{6,14},{7,15},{8,0},{9,1},... | collective-permute-start | bytes 196616 | tf_op jit(solution)/shard_map/ppermute | solution.py:448
  691.9 23.0 %copy-start.8 = (s32[128]{0:T(128)S(1)}, s32[128]{0:T(128)}, u32[]{:S(2)}) copy-start(s32[128]{0:T(128)} %get-tuple-element.477) | copy-start | bytes 1540
  703.8 6.9 collective-permute-start.31
  711.8 3.1 collective-permute-start.32

commit v7 on v6

--- a/solution.py
+++ b/solution.py
@@ -23,9 +23,6 @@
 VMEM = 16 * 1024 * 1024
 
 OVER_X = [[g * 8 + x * 2 + c for x in range(NX)] for g in range(NG) for c in range(NC)]
-OVER_XZ = [
-    [y * 16 + m * 2 + c for m in range(NZ * NX)] for y in range(NY) for c in range(NC)
-]
 OVER_G = [[g * 8 + x * 2 + c for g in range(NG)] for x in range(NX) for c in range(NC)]
 OVER_Y = [
     [(y * 2 + z) * 8 + x * 2 + c for y in range(NY)]
@@ -66,7 +63,7 @@
     for step in range(1, 4):
         pairs = [(w, moved(w, stride, step)) for w in range(WIDE)]
         blocks.append(lax.ppermute(piece((at + step) % 4), "wide", pairs))
-    return jnp.concatenate(blocks, axis=0)
+    return blocks
 
 
 def in_order(blocks, at):
@@ -75,12 +72,14 @@
     )
 
 
-def kv_blocks(w_key, w_value, x):
+def kv_blocks(w_key, w_value, x, after):
     both = jnp.stack([w_key.T, w_value.T])
     width = both.shape[1]
     both = both.reshape(2, width, NG, NX, CHIP).transpose(3, 0, 1, 2, 4)
     both = both.reshape(NX, 2 * width, NG * CHIP)
-    return from_ring(lambda i: lax.dynamic_slice_in_dim(both, i, 1, 0), x, NC)
+    both = lax.optimization_barrier((both, after))[0]
+    blocks = from_ring(lambda i: lax.dynamic_slice_in_dim(both, i, 1, 0), x, NC)
+    return jnp.concatenate(blocks, axis=0)
 
 
 def relayout_kv(mine, core, x):
@@ -244,9 +243,7 @@
     )(info, query, own, first)
 
 
-def output_kernel(
-    halves, info_ref, ctx_ref, own_ref, other_ref, out_ref, rows, weights, sems
-):
+def output_kernel(info_ref, ctx_ref, own_ref, other_ref, out_ref, rows, weights, sems):
     copies = fetch(own_ref, other_ref, weights, sems)
     depth = rows.shape[1]
     for i in range(depth // CHIP):
@@ -256,22 +253,20 @@
         for copy in copies[i]:
             copy.wait()
         source = lax.rem(y + NY - i, NY)
-        for part in range(halves):
+        for part in range(NZ):
             cut = slice(part * depth, (part + 1) * depth)
             weight = jnp.concatenate([weights[0, i, cut], weights[1, i, cut]], axis=1)
             total = jnp.dot(rows[...], weight, preferred_element_type=jnp.float32)
             total = total.astype(jnp.bfloat16)
-            first = (z if part == 0 else 1 - z) * NC if halves > 1 else 0
+            first = (z if part == 0 else 1 - z) * NC
             out_ref[source, :, aligned(first + core)] = total[:, :HD]
             out_ref[source, :, aligned(first + 1 - core)] = total[:, HD:]
 
 
 def output(info, context, wo):
-    count = context.shape[0]
-    halves = NG // count
     vmem = pl.BlockSpec(memory_space=pltpu.VMEM)
     return pl.pallas_call(
-        functools.partial(output_kernel, halves),
+        output_kernel,
         in_specs=[
             pl.BlockSpec(memory_space=pltpu.SMEM),
             vmem,
@@ -279,8 +274,8 @@
             pl.BlockSpec(memory_space=pl.ANY),
         ],
         out_specs=vmem,
-        out_shape=jax.ShapeDtypeStruct((NY, HALF, halves * CHIP), jnp.bfloat16),
-        scratch_shapes=[pltpu.VMEM((HALF, count * CHIP), jnp.bfloat16)] + weight_scratch(),
+        out_shape=jax.ShapeDtypeStruct((NY, HALF, NZ * CHIP), jnp.bfloat16),
+        scratch_shapes=[pltpu.VMEM((HALF, NX * CHIP), jnp.bfloat16)] + weight_scratch(),
         compiler_params=pltpu.CompilerParams(vmem_limit_bytes=VMEM),
         name="output",
     )(info, context, *wo)
@@ -348,36 +343,42 @@
 
     raw = w_out[0].reshape(NY, NZ * NX * CHIP, HD)
 
-    def prepare(out_rows, before):
-        query = exchange(x_blocks(w_query[0]), OVER_X)
-        mine = kv_blocks(w_key[0], w_value[0], x)
-        out_rows = lax.optimization_barrier((out_rows, mine, before))[0]
+    halves = raw.reshape(NY, NZ, NX * CHIP, HD)
+
+    def prepare(before, late):
+        kept = lax.dynamic_index_in_dim(halves, z, 1, keepdims=False)
+        given = lax.dynamic_index_in_dim(halves, 1 - z, 1, keepdims=False)
+        rows = x_blocks(w_query[0])
+        query = exchange(rows, OVER_X)
+        mine = kv_blocks(w_key[0], w_value[0], x, query)
+        if late:
+            given = lax.optimization_barrier((given, query, mine))[0]
+        far = lax.ppermute(given, "wide", Z_SWAP)
         key_value = relayout_kv(mine, core, x)
-        out = from_ring(lambda i: lax.dynamic_slice_in_dim(out_rows, i, 1, 0), y, 16)
+        out_rows = jnp.concatenate([kept, far], axis=1)
+        out_rows = lax.optimization_barrier((out_rows, before))[0]
+        blocks = from_ring(lambda i: lax.dynamic_slice_in_dim(out_rows, i, 1, 0), y, 16)
+        out = jnp.concatenate(lax.optimization_barrier((blocks, mine))[0], axis=0)
         return (query, swap_cores(query)), key_value, (out, swap_cores(out))
 
-    def first_section(start, cross):
+    def early_section(start, cross):
         pair = jnp.where(
             z == 0,
             jnp.concatenate([start, cross], axis=1),
             jnp.concatenate([cross, start], axis=1),
         )
-        gathered = in_order(from_ring(lambda i: pair[None], y, 16), y)
+        gathered = in_order(jnp.concatenate(from_ring(lambda i: pair[None], y, 16)), y)
         items = jnp.zeros((ITEMS_HERE,), jnp.int32)
-        return gathered, prepare(raw, gathered), (items, items)
-
-    def later_section(start, cross):
-        halves = raw.reshape(NY, NZ, NX * CHIP, HD)
-        kept = lax.dynamic_index_in_dim(halves, z, 1, keepdims=False)
-        given = lax.dynamic_index_in_dim(halves, 1 - z, 1, keepdims=False)
-        far = lax.ppermute(given, "wide", Z_SWAP)
-        out_rows = jnp.concatenate([kept, far], axis=1)
+        return gathered, prepare(gathered, False), (items, items)
+
+    def late_section(start, cross):
         blank = jnp.zeros((NY, HALF, NZ * CHIP), jnp.bfloat16)
-        return blank, prepare(out_rows, start), ranks(placement, core)
+        return blank, prepare(start, True), ranks(placement, core)
 
     gathered, (wq, wkv, wo), items = lax.cond(
-        segment == 0, first_section, later_section, start, cross
+        segment <= 1, early_section, late_section, start, cross
     )
+    cos, sin = lax.optimization_barrier((cos, sin))
 
     def later_gather(same, cross):
         return gather((same.astype(jnp.float32) + cross.astype(jnp.float32)).astype(jnp.bfloat16))
@@ -385,16 +386,6 @@
     def summed(parts, own):
         parts = parts.astype(jnp.float32)
         return own.astype(jnp.float32) + (parts[0] + parts[1] + parts[2] + parts[3])
-
-    def whole_out(context, own):
-        context = jnp.broadcast_to(context[:1], (NG, HALF, CHIP))
-        parts = exchange(output(info, exchange(context, OVER_XZ), wo), OVER_Y)
-        own = jnp.where(z == 0, own[:, :CHIP], own[:, CHIP:])
-        result = summed(parts, own).astype(jnp.bfloat16)
-        zero = jnp.zeros_like(result)
-        return jnp.concatenate(
-            [jnp.where(z == 0, result, zero), jnp.where(z == 0, zero, result)], axis=1
-        )
 
     def half_out(context, own):
         parts = exchange(output(info, exchange(context, OVER_X), wo), OVER_Y)
@@ -406,7 +397,7 @@
         first = lax.ppermute(kv, "wide", CORE_UP)
         context = attend(info, query, kv, first)
         own = lax.dynamic_index_in_dim(gathered, y, 0, keepdims=False)
-        return lax.cond(segment == 0, whole_out, half_out, context, own), kv
+        return half_out(context, own), kv
 
     def send(pairs):
         same, cross = pairs
@@ -453,7 +444,7 @@
     outputs = by_core(core, kept, swap_cores(given), 0)
 
     item_owner, item_rank = lax.cond(
-        segment == 0, lambda: ranks(placement, core), lambda: items
+        segment <= 1, lambda: ranks(placement, core), lambda: items
     )
     blocks = HALF // BLOCK
     slots = 2 * placement.shape[0] // WIDE

time: 717 us -> 646 us (0.901)
  waiting for transfers between devices: 565 us -> 508 us
  other arithmetic: 18.4 us -> 6.71 us
  blocking collectives: 18.1 us -> 27.8 us
    ppermute x2, waiting for transfers between devices: 445 us -> 366 us  [run(): return (lax.ppermute(value, axes, cross), lax.ppermute(value, axes, same))]
    all_to_all x4 -> x3, waiting for transfers between devices: 14.7 us -> 32.9 us  [exchange(): lax.all_to_all(value, 'wide', 0, 0, axis_index_groups=groups, tiled=True)]
    all_to_all x2 -> x3, blocking collectives: 18.1 us -> 27.8 us  [exchange(): lax.all_to_all(value, 'wide', 0, 0, axis_index_groups=groups, tiled=True)]
    all_to_all x4 -> x3, starting transfers between devices: 23.5 us -> 20.1 us  [exchange(): lax.all_to_all(value, 'wide', 0, 0, axis_index_groups=groups, tiled=True)]
  transfers between devices with their start and end apart: 23 -> 22, of which waited for: 13 -> 15; matrix products, arithmetic and copies ran while one was open for 3% -> 2% of each run, Pallas kernels for 0% -> 0%
where the time goes in v7:
time: 646 us; the launch traced here: 644 us
  waiting for transfers between devices  508 us (79%)
  starting transfers between devices  75.8 us (12%)
  blocking collectives  27.8 us (4%)
  local copies, waits for them, and re-layouts  12.9 us (2%)
  Pallas kernels  9.12 us (1%)
  other arithmetic  6.71 us (1%)
    ppermute x2, waiting for transfers between devices, run(): return (lax.ppermute(value, axes, cross), lax.ppermute(value, axes, same))  366 us
    ppermute x1, waiting for transfers between devices, prepare(): far = lax.ppermute(given, 'wide', Z_SWAP)  68.9 us
    all_to_all x3, waiting for transfers between devices, exchange(): lax.all_to_all(value, 'wide', 0, 0, axis_index_groups=groups, tiled=True)  32.9 us
    all_to_all x3, blocking collectives, exchange(): lax.all_to_all(value, 'wide', 0, 0, axis_index_groups=groups, tiled=True)  27.8 us
    all_to_all x3, starting transfers between devices, exchange(): lax.all_to_all(value, 'wide', 0, 0, axis_index_groups=groups, tiled=True)  20.1 us
    ppermute x6, starting transfers between devices, swap_cores(): return lax.ppermute(value, 'wide', CORE_SWAP)  19.8 us
    ppermute x6, waiting for transfers between devices, from_ring(): blocks.append(lax.ppermute(piece((at + step) % 4), 'wide', pairs))  19.2 us
    ppermute x6, starting transfers between devices, from_ring(): blocks.append(lax.ppermute(piece((at + step) % 4), 'wide', pairs))  19.1 us
  transfers between devices with their start and end apart: 22, of which 15 were waited for; matrix products, arithmetic and copies ran while one was open for 2% of the time, Pallas kernels for 0%

profile of v7, /device:TPU:481, one launch (start us, length us, event | category | flops | bytes accessed | tf_op | source)
XLA Modules:
  0.0 644.5 jit_solution(11547158367370677460)
XLA Ops:
  1.4 2.6 collective-permute-start.28
  12.2 166.6 %conditional.6 = (bf16[4,128,512]{2,1,0:T(8,128)(2,1)S(1)}, bf16[4,2048,128]{2,1,0:T(8,128)(2,1)}, bf16[4,2048,128]{2,1,0:T(8,128)(2,1)}, bf16[256,2048]{1,0:T(8...) conditional(s32[]{:T(128)} %convert_element_type.84, ...), branch_computations={%region_0.4_spmd, %region_4.5_spmd} | conditional | flops 10027141 | bytes 88870032 | solution.py:378
  12.2 3.1 copy.38
  15.4 4.6 all-to-all-start
  20.8 25.0 %all-to-all-done = bf16[4,2048,128]{2,1,0:T(8,128)(2,1)} async-done(((bf16[4,2048,128]{2,1,0:T(8,128)(2,1)}), bf16[4,2048,128]{2,1,0:T(8,128)(2,1)}, u32[]{:S(2)}, u32[]{:S(2)}) %all-to-all-start) | async-done | bytes 2097184 | tf_op jit(solution)/shard_map/cond/branch_0_fun/all_to_all | solution.py:39
  48.1 3.7 collective-permute-start.6
  55.6 3.6 collective-permute-done.7
  59.3 8.4 %collective-permute-start.9 = (bf16[4,1024,128]{2,1,0:T(8,128)(2,1)}, bf16[4,1024,128]{2,1,0:T(8,128)(2,1)S(1)}, u32[]{:S(2)}, u32[]{:S(2)}) collective-permute-start(bf16[4,1024,128]{2,1,0:T(8,128)(2,1)} %get-tuple-element.354), channel_id=1, source_target_pairs={{0,8},{1,9},{2,10},{3,11},{4,12},{5,13},{6,14},{7,15},{8,0},{9,1},... | collective-permute-start | bytes 3145736 | tf_op jit(solution)/shard_map/cond/branch_0_fun/ppermute | solution.py:356
  67.8 68.9 %collective-permute-done.9 = bf16[4,1024,128]{2,1,0:T(8,128)(2,1)S(1)} collective-permute-done((bf16[4,1024,128]{2,1,0:T(8,128)(2,1)}, bf16[4,1024,128]{2,1,0:T(8,128)(2,1)S(1)}, u32[]{:S(2)}, u32[]{:S(2)}) %collective-permute-start.9) | collective-permute-done | bytes 1048608 | tf_op jit(solution)/shard_map/cond/branch_0_fun/ppermute | solution.py:356
  137.0 3.2 collective-permute-start.10
  140.2 4.5 collective-permute-start.11
  144.8 3.0 collective-permute-start.12
  147.8 3.5 collective-permute-start.4
  153.0 12.3 %collective-permute-done.11 = bf16[1,2048,128]{2,1,0:T(8,128)(2,1)S(1)} collective-permute-done((bf16[1,2048,128]{2,1,0:T(8,128)(2,1)S(1)}, bf16[1,2048,128]{2,1,0:T(8,128)(2,1)S(1)}, u32[]{:S(2)}, u32[]{:S(2)}) %collective-permute-start.11) | collective-permute-done | bytes 524320 | tf_op jit(solution)/shard_map/cond/branch_0_fun/ppermute | solution.py:65
  170.2 3.5 collective-permute-start.13
  179.4 426.2 %while.23 = (s32[]{:T(128)}, bf16[4,128,512]{2,1,0:T(8,128)(2,1)S(1)}, bf16[128,512]{1,0:T(8,128)(2,1)S(1)}, bf16[128,256]{1,0:T(8,128)(2,1)S(1)}, s32[]{:T(128)...) while((s32[]{:T(128)}, ...), condition=%wide.region_14.15_spmd, body=%wide.region_5.14_spmd.sunk | while | flops 983069 | bytes 11141949 | solution.py:434
  179.7 378.8 %conditional.11 = (bf16[4,128,512]{2,1,0:T(8,128)(2,1)S(1)}) conditional(s32[]{:T(128)} %convert_element_type.116, bf16[4,128,512]{2,1,0:T(8,128)(2,1)S(1)} %get-tuple-element.696, (s32[]{:T(128)}, s32[]{:T(128)}, bf16[128,512]{1,0:T(8,128)(2,1)S(1)}, bf16[4,128,512]{2,1,0:T(8,128)(2,1)S(1)}) %tuple.140), branch_computations={%region_8.8_spmd, %region_9.13_spmd} | conditional | flops 262160 | bytes 4194573 | solution.py:423
  179.8 368.4 %conditional = (bf16[128,512]{1,0:T(8,128)(2,1)}, bf16[128,512]{1,0:T(8,128)(2,1)}) conditional(s32[]{:T(128)} %convert_element_type.70, bf16[128,512]{1,0:T(8,128)(2,1)S(1)} %get-tuple-element.396, bf16[128,512]{1,0:T(8,128)(2,1)S(1)} %get-tuple-element.396), branch_computations={%region_10.9_spmd, %region_11.10_spmd} | conditional | bytes 1048672 | solution.py:418
  182.4 365.8 %collective-permute-done.2 = bf16[128,512]{1,0:T(8,128)(2,1)} collective-permute-done((bf16[128,512]{1,0:T(8,128)(2,1)S(1)}, bf16[128,512]{1,0:T(8,128)(2,1)}, u32[]{:S(2)}, u32[]{:S(2)}) %collective-permute-start.2) | collective-permute-done | bytes 131104 | tf_op jit(solution)/shard_map/while/body/eval_jaxpr/cond/branch_1_fun/cond/branch_1_fun/ppermute | solution.py:407
  548.1 10.4 %conditional.1 = (bf16[4,128,512]{2,1,0:T(8,128)(2,1)S(1)}) conditional(s32[]{:T(128)} %convert_element_type.69, bf16[4,128,512]{2,1,0:T(8,128)(2,1)S(1)} %get-tuple-element.395, (bf16[128,512]{1,0:T(8,128)(2,1)}, bf16[128,512]{1,0:T(8,128)(2,1)}) %tuple.62), branch_computations={%region_12.11_spmd, %region_13.12_spmd} | conditional | flops 262144 | bytes 3145736 | solution.py:419
  549.2 9.3 %all_to_all.31 = bf16[4,128,512]{2,1,0:T(8,128)(2,1)S(1)} all-to-all(bf16[4,128,512]{2,1,0:T(8,128)(2,1)S(1)} %broadcast_in_dim.60), channel_id=1, replica_groups={{0,16,32,48},{1,17,33,49},{2,18,34,50},{3,19,35,51},{4,20,36,52},{5,21,..., dimensions={0} | all-to-all | bytes 1048576 | tf_op jit(solution)/shard_map/while/body/eval_jaxpr/cond/branch_1_fun/cond/branch_1_fun/all_to_all | solution.py:39
  558.6 47.0 %conditional.10 = ((bf16[128,512]{1,0:T(8,128)(2,1)S(1)}, bf16[128,256]{1,0:T(8,128)(2,1)S(1)})) conditional(s32[]{:T(128)} %convert_element_type.117, (bf16[128,512]{1,0:T(8,128)(2,1)S(1)}, bf16[128,256]{1,0:T(8,128)(2,1)S(1)}) %tuple.138, (s32[]{:T(128)}, s32[]{:T(128)}, bf16[4,128,512]{2,1,0:T(8,128)(2,1)S(1)}, s32[4]{0:T(128)S(1)}, ...), branch_computations={%region_6.6_spmd, %region_7.7_spmd} | conditional | flops 720900 | bytes 6947016 | solution.py:415
  558.6 3.6 project.1
  562.2 9.7 %all_to_all.29.part_ref = bf16[4,144,512]{2,1,0:T(8,128)(2,1)S(1)} all-to-all(bf16[4,144,512]{2,1,0:T(8,128)(2,1)S(1)} %project.1), channel_id=1, replica_groups={{0,2,4,6},{1,3,5,7},{8,10,12,14},{9,11,13,15},{16,18,20,22},{17,19,21,2..., dimensions={0} | all-to-all | bytes 1179648 | tf_op jit(solution)/shard_map/while/body/eval_jaxpr/cond/branch_1_fun/all_to_all | solution.py:39
  573.4 6.3 collective-permute-done.27.first_ref
  581.2 8.8 %all_to_all.30.ctx_ref = bf16[4,128,256]{2,1,0:T(8,128)(2,1)S(1)} all-to-all(bf16[4,128,256]{2,1,0:T(8,128)(2,1)S(1)} %attend.1), channel_id=1, replica_groups={{0,2,4,6},{1,3,5,7},{8,10,12,14},{9,11,13,15},{16,18,20,22},{17,19,21,2..., dimensions={0} | all-to-all | bytes 524288 | tf_op jit(solution)/shard_map/while/body/eval_jaxpr/cond/branch_1_fun/all_to_all | solution.py:39
  589.9 3.9 output.1
  593.9 3.5 all-to-all-start.4
  597.4 7.9 %all-to-all-done.4 = bf16[4,128,512]{2,1,0:T(8,128)(2,1)S(1)} async-done(((bf16[4,128,512]{2,1,0:T(8,128)(2,1)}), bf16[4,128,512]{2,1,0:T(8,128)(2,1)S(1)}, u32[]{:S(2)}, u32[]{:S(2)}) %all-to-all-start.4) | async-done | bytes 524320 | tf_op jit(solution)/shard_map/while/body/eval_jaxpr/cond/branch_1_fun/all_to_all | solution.py:39
  606.5 12.1 %all-to-all-start.6 = ((bf16[8,128,256]{2,1,0:T(8,128)(2,1)}), bf16[8,128,256]{2,1,0:T(8,128)(2,1)S(1)}, u32[]{:S(2)}, u32[]{:S(2)}) async-start(bf16[8,128,256]{2,1,0:T(8,128)(2,1)} %broadcast_in_dim.89), calls=%async_computation.6 | async-start | bytes 1048576 | tf_op jit(solution)/shard_map/all_to_all | solution.py:39
  620.6 11.8 %collective-permute-done.31 = bf16[128,256]{0,1:T(8,128)(2,1)S(1)} collective-permute-done((bf16[128,256]{0,1:T(8,128)(2,1)S(1)}, bf16[128,256]{0,1:T(8,128)(2,1)S(1)}, u32[]{:S(2)}, u32[]{:S(2)}) %collective-permute-start.31) | collective-permute-done | bytes 65568 | tf_op jit(solution)/shard_map/ppermute | solution.py:439
  632.5 6.1 collective-permute-start.32
  (118 shorter events, 43.2 us)
Async XLA Ops:
  1.4 7.1 %collective-permute-start.28 = (bf16[128,128]{1,0:T(8,128)(2,1)S(1)}, bf16[128,128]{1,0:T(8,128)(2,1)S(1)}, u32[]{:S(2)}, u32[]{:S(2)}) collective-permute-start(bf16[128,128]{1,0:T(8,128)(2,1)S(1)} %dynamic-slice_bitcast_fusion.5), channel_id=1, source_target_pairs={{0,1},{1,0},{2,3},{3,2},{4,5},{5,4},{6,7},{7,6},{8,9},{9,8},{10,11... | collective-permute-start | bytes 98312 | tf_op jit(solution)/shard_map/ppermute | solution.py:43
  4.0 7.2 %collective-permute-start.30 = (bf16[128,128]{1,0:T(8,128)(2,1)S(1)}, bf16[128,128]{1,0:T(8,128)(2,1)S(1)}, u32[]{:S(2)}, u32[]{:S(2)}) collective-permute-start(bf16[128,128]{1,0:T(8,128)(2,1)S(1)} %dynamic-slice_bitcast_fusion.5), channel_id=1, source_target_pairs={{448,9},{449,8},{450,11},{451,10},{452,13},{453,12},{454,15},{455,... | collective-permute-start | bytes 98312 | tf_op jit(solution)/shard_map/ppermute | solution.py:326
  9.3 2.3 collective-permute-start.29
  15.4 4.7 copy-start.4
  15.4 4.9 copy-start.6
  15.4 30.5 %all-to-all-start = ((bf16[4,2048,128]{2,1,0:T(8,128)(2,1)}), bf16[4,2048,128]{2,1,0:T(8,128)(2,1)}, u32[]{:S(2)}, u32[]{:S(2)}) async-start(bf16[4,2048,128]{2,1,0:T(8,128)(2,1)} %bitcast.2), calls=%async_computation | async-start | bytes 4194304 | tf_op jit(solution)/shard_map/cond/branch_0_fun/all_to_all | solution.py:39
  20.3 34.1 %copy-start = (bf16[4,2,1024,128]{3,2,1,0:T(8,128)(2,1)S(1)}, bf16[4,2,1024,128]{3,2,1,0:T(8,128)(2,1)}, u32[]{:S(2)}) copy-start(bf16[4,2,1024,128]{3,2,1,0:T(8,128)(2,1)} %get-tuple-element.352) | copy-start | bytes 6291460 | tf_op jit(solution)/shard_map/cond
  45.9 9.6 %collective-permute-start.5 = (bf16[1,32,2048]{2,1,0:T(8,128)(2,1)S(1)}, bf16[1,32,2048]{2,1,0:T(8,128)(2,1)S(1)}, u32[]{:S(2)}, u32[]{:S(2)}) collective-permute-start(bf16[1,32,2048]{2,1,0:T(8,128)(2,1)S(1)} %get-tuple-element.515), channel_id=1, source_target_pairs={{0,2},{1,3},{2,4},{3,5},{4,6},{5,7},{6,0},{7,1},{8,10},{9,11},{10,... | collective-permute-start | bytes 393224 | tf_op jit(solution)/shard_map/cond/branch_0_fun/ppermute | solution.py:65
  48.1 7.5 %collective-permute-start.6 = (bf16[1,32,2048]{2,1,0:T(8,128)(2,1)S(1)}, bf16[1,32,2048]{2,1,0:T(8,128)(2,1)S(1)}, u32[]{:S(2)}, u32[]{:S(2)}) collective-permute-start(bf16[1,32,2048]{2,1,0:T(8,128)(2,1)S(1)} %get-tuple-element.514), channel_id=1, source_target_pairs={{0,4},{1,5},{2,6},{3,7},{4,0},{5,1},{6,2},{7,3},{8,12},{9,13},{10,... | collective-permute-start | bytes 393224 | tf_op jit(solution)/shard_map/cond/branch_0_fun/ppermute | solution.py:65
  51.8 7.4 %collective-permute-start.7 = (bf16[1,32,2048]{2,1,0:T(8,128)(2,1)S(1)}, bf16[1,32,2048]{2,1,0:T(8,128)(2,1)S(1)}, u32[]{:S(2)}, u32[]{:S(2)}) collective-permute-start(bf16[1,32,2048]{2,1,0:T(8,128)(2,1)S(1)} %get-tuple-element.513), channel_id=1, source_target_pairs={{0,6},{1,7},{2,0},{3,1},{4,2},{5,3},{6,4},{7,5},{8,14},{9,15},{10,... | collective-permute-start | bytes 393224 | tf_op jit(solution)/shard_map/cond/branch_0_fun/ppermute | solution.py:65
  59.3 77.5 %collective-permute-start.9 = (bf16[4,1024,128]{2,1,0:T(8,128)(2,1)}, bf16[4,1024,128]{2,1,0:T(8,128)(2,1)S(1)}, u32[]{:S(2)}, u32[]{:S(2)}) collective-permute-start(bf16[4,1024,128]{2,1,0:T(8,128)(2,1)} %get-tuple-element.354), channel_id=1, source_target_pairs={{0,8},{1,9},{2,10},{3,11},{4,12},{5,13},{6,14},{7,15},{8,0},{9,1},... | collective-permute-start | bytes 3145736 | tf_op jit(solution)/shard_map/cond/branch_0_fun/ppermute | solution.py:356
  137.0 15.9 %collective-permute-start.10 = (bf16[1,2048,128]{2,1,0:T(8,128)(2,1)S(1)}, bf16[1,2048,128]{2,1,0:T(8,128)(2,1)S(1)}, u32[]{:S(2)}, u32[]{:S(2)}) collective-permute-start(bf16[1,2048,128]{2,1,0:T(8,128)(2,1)S(1)} %get-tuple-element.498), channel_id=1, source_target_pairs={{0,16},{1,17},{2,18},{3,19},{4,20},{5,21},{6,22},{7,23},{8,24},{9,... | collective-permute-start | bytes 1572872 | tf_op jit(solution)/shard_map/cond/branch_0_fun/ppermute | solution.py:65
  140.2 25.1 %collective-permute-start.11 = (bf16[1,2048,128]{2,1,0:T(8,128)(2,1)S(1)}, bf16[1,2048,128]{2,1,0:T(8,128)(2,1)S(1)}, u32[]{:S(2)}, u32[]{:S(2)}) collective-permute-start(bf16[1,2048,128]{2,1,0:T(8,128)(2,1)S(1)} %get-tuple-element.497), channel_id=1, source_target_pairs={{0,32},{1,33},{2,34},{3,35},{4,36},{5,37},{6,38},{7,39},{8,40},{9,... | collective-permute-start | bytes 1572872 | tf_op jit(solution)/shard_map/cond/branch_0_fun/ppermute | solution.py:65
  144.8 22.0 %collective-permute-start.12 = (bf16[1,2048,128]{2,1,0:T(8,128)(2,1)S(1)}, bf16[1,2048,128]{2,1,0:T(8,128)(2,1)S(1)}, u32[]{:S(2)}, u32[]{:S(2)}) collective-permute-start(bf16[1,2048,128]{2,1,0:T(8,128)(2,1)S(1)} %get-tuple-element.496), channel_id=1, source_target_pairs={{0,48},{1,49},{2,50},{3,51},{4,52},{5,53},{6,54},{7,55},{8,56},{9,... | collective-permute-start | bytes 1572872 | tf_op jit(solution)/shard_map/cond/branch_0_fun/ppermute | solution.py:65
  147.8 30.8 %collective-permute-start.4 = (bf16[4,2048,128]{2,1,0:T(8,128)(2,1)}, bf16[4,2048,128]{2,1,0:T(8,128)(2,1)}, u32[]{:S(2)}, u32[]{:S(2)}) collective-permute-start(bf16[4,2048,128]{2,1,0:T(8,128)(2,1)} %all-to-all-done), channel_id=1, source_target_pairs={{0,1},{1,0},{2,3},{3,2},{4,5},{5,4},{6,7},{7,6},{8,9},{9,8},{10,11... | collective-permute-start | bytes 6291464 | tf_op jit(solution)/shard_map/cond/branch_0_fun/ppermute | solution.py:43
  166.7 8.9 %copy-start.11 = (s32[256,1]{0,1:T(1,128)S(1)}, s32[256,1]{0,1:T(1,128)}, u32[]{:S(2)}) copy-start(s32[256,1]{0,1:T(1,128)} %get-tuple-element.360) | copy-start | bytes 3076 | tf_op jit(solution)/shard_map/cond
  170.2 8.4 %collective-permute-start.13 = (bf16[4,2048,128]{2,1,0:T(8,128)(2,1)}, bf16[4,2048,128]{2,1,0:T(8,128)(2,1)}, u32[]{:S(2)}, u32[]{:S(2)}) collective-permute-start(bf16[4,2048,128]{2,1,0:T(8,128)(2,1)} %constant_dynamic-update-slice_fusion), channel_id=1, source_target_pairs={{0,1},{1,0},{2,3},{3,2},{4,5},{5,4},{6,7},{7,6},{8,9},{9,8},{10,11... | collective-permute-start | bytes 6291464 | tf_op jit(solution)/shard_map/cond/branch_0_fun/ppermute | solution.py:43
  173.7 4.5 collective-permute-start.8
  178.8 0.6 copy-start.12
  179.4 441.2 %copy-start.10 = (s32[256,1]{0,1:T(1,128)S(1)}, s32[256,1]{0,1:T(1,128)}, u32[]{:S(2)}) copy-start(s32[256,1]{0,1:T(1,128)} %param.29) | copy-start | bytes 3076
  179.8 368.4 %collective-permute-start.2 = (bf16[128,512]{1,0:T(8,128)(2,1)S(1)}, bf16[128,512]{1,0:T(8,128)(2,1)}, u32[]{:S(2)}, u32[]{:S(2)}) collective-permute-start(bf16[128,512]{1,0:T(8,128)(2,1)S(1)} %param.6), channel_id=1, source_target_pairs={{0,72},{1,73},{2,74},{3,75},{4,76},{5,77},{6,78},{7,79},{8,64},{9,... | collective-permute-start | bytes 393224 | tf_op jit(solution)/shard_map/while/body/eval_jaxpr/cond/branch_1_fun/cond/branch_1_fun/ppermute | solution.py:407
  181.1 367.1 %collective-permute-start.3 = (bf16[128,512]{1,0:T(8,128)(2,1)S(1)}, bf16[128,512]{1,0:T(8,128)(2,1)}, u32[]{:S(2)}, u32[]{:S(2)}) collective-permute-start(bf16[128,512]{1,0:T(8,128)(2,1)S(1)} %param.6), channel_id=1, source_target_pairs={{0,64},{1,65},{2,66},{3,67},{4,68},{5,69},{6,70},{7,71},{8,72},{9,... | collective-permute-start | bytes 393224 | tf_op jit(solution)/shard_map/while/body/eval_jaxpr/cond/branch_1_fun/cond/branch_1_fun/ppermute | solution.py:407
  572.1 21.8 %copy-start.2 = (bf16[128,256]{1,0:T(8,128)(2,1)}, bf16[128,256]{1,0:T(8,128)(2,1)S(1)}, u32[]{:S(2)}) copy-start(bf16[128,256]{1,0:T(8,128)(2,1)S(1)} %get-tuple-element.660.own_ref) | copy-start | bytes 196612 | tf_op jit(solution)/shard_map/while/body/eval_jaxpr/cond
  572.1 7.7 %collective-permute-start.27 = (bf16[128,256]{1,0:T(8,128)(2,1)S(1)}, bf16[128,256]{1,0:T(8,128)(2,1)S(1)}, u32[]{:S(2)}, u32[]{:S(2)}) collective-permute-start(bf16[128,256]{1,0:T(8,128)(2,1)S(1)} %get-tuple-element.660.own_ref), channel_id=1, source_target_pairs={{0,1},{2,3},{4,5},{6,7},{8,9},{10,11},{12,13},{14,15},{16,17},{18,... | collective-permute-start | bytes 196616 | tf_op jit(solution)/shard_map/while/body/eval_jaxpr/cond/branch_1_fun/ppermute | solution.py:397
  593.9 11.4 %all-to-all-start.4 = ((bf16[4,128,512]{2,1,0:T(8,128)(2,1)}), bf16[4,128,512]{2,1,0:T(8,128)(2,1)S(1)}, u32[]{:S(2)}, u32[]{:S(2)}) async-start(bf16[4,128,512]{2,1,0:T(8,128)(2,1)} %output.1), calls=%async_computation.4 | async-start | bytes 1048576 | tf_op jit(solution)/shard_map/while/body/eval_jaxpr/cond/branch_1_fun/all_to_all | solution.py:39
  597.4 8.2 %copy-start.3 = (bf16[128,256]{1,0:T(8,128)(2,1)S(1)}, bf16[128,256]{1,0:T(8,128)(2,1)}, u32[]{:S(2)}) copy-start(bf16[128,256]{1,0:T(8,128)(2,1)} %copy-done.2) | copy-start | bytes 196612 | tf_op jit(solution)/shard_map/while/body/eval_jaxpr/cond
  606.5 33.0 %all-to-all-start.6 = ((bf16[8,128,256]{2,1,0:T(8,128)(2,1)}), bf16[8,128,256]{2,1,0:T(8,128)(2,1)S(1)}, u32[]{:S(2)}, u32[]{:S(2)}) async-start(bf16[8,128,256]{2,1,0:T(8,128)(2,1)} %broadcast_in_dim.89), calls=%async_computation.6 | async-start | bytes 1048576 | tf_op jit(solution)/shard_map/all_to_all | solution.py:39
  618.7 13.7 %collective-permute-start.31 = (bf16[128,256]{0,1:T(8,128)(2,1)S(1)}, bf16[128,256]{0,1:T(8,128)(2,1)S(1)}, u32[]{:S(2)}, u32[]{:S(2)}) collective-permute-start(bf16[128,256]{0,1:T(8,128)(2,1)S(1)} %dynamic-slice_bitcast_fusion.4), channel_id=1, source_target_pairs={{0,8},{1,9},{2,10},{3,11},{4,12},{5,13},{6,14},{7,15},{8,0},{9,1},... | collective-permute-start | bytes 196616 | tf_op jit(solution)/shard_map/ppermute | solution.py:439
  620.6 23.1 %copy-start.13 = (s32[128]{0:T(128)S(1)}, s32[128]{0:T(128)}, u32[]{:S(2)}) copy-start(s32[128]{0:T(128)} %get-tuple-element.448) | copy-start | bytes 1540
  632.5 6.9 %collective-permute-start.32 = (bf16[128,128]{1,0:T(8,128)(2,1)S(1)}, bf16[128,128]{1,0:T(8,128)(2,1)S(1)}, u32[]{:S(2)}, u32[]{:S(2)}) collective-permute-start(bf16[128,128]{1,0:T(8,128)(2,1)S(1)} %bitcast.106), channel_id=1, source_target_pairs={{0,1},{1,0},{2,3},{3,2},{4,5},{5,4},{6,7},{7,6},{8,9},{9,8},{10,11... | collective-permute-start | bytes 98312 | tf_op jit(solution)/shard_map/ppermute | solution.py:43
  640.6 3.1 collective-permute-start.33

commit v8 on v7

--- a/solution.py
+++ b/solution.py
@@ -72,22 +72,19 @@
     )
 
 
-def kv_blocks(w_key, w_value, x, after):
+def kv_blocks(w_key, w_value):
     both = jnp.stack([w_key.T, w_value.T])
     width = both.shape[1]
     both = both.reshape(2, width, NG, NX, CHIP).transpose(3, 0, 1, 2, 4)
-    both = both.reshape(NX, 2 * width, NG * CHIP)
-    both = lax.optimization_barrier((both, after))[0]
-    blocks = from_ring(lambda i: lax.dynamic_slice_in_dim(both, i, 1, 0), x, NC)
-    return jnp.concatenate(blocks, axis=0)
-
-
-def relayout_kv(mine, core, x):
-    width = mine.shape[1] // 2
-    other = in_order(swap_cores(mine), x).reshape(NX, 2, 1, width, NG * CHIP)
-    mine = in_order(mine, x).reshape(NX, 2, 1, width, NG * CHIP)
+    return both.reshape(NX, 2 * width * NG * NC, HD)
+
+
+def whole_head(mine, other, core):
+    rows = NG * CHIP
+    mine = mine.reshape(NX, 2, 1, -1, rows)
+    other = other.reshape(NX, 2, 1, -1, rows)
     full = by_core(core, mine, other, 2)
-    return full.transpose(1, 0, 2, 3, 4).reshape(2 * HD, NG * CHIP)
+    return full.transpose(1, 0, 2, 3, 4).reshape(2 * HD, rows)
 
 
 def eye(n):
@@ -103,7 +100,8 @@
     for i in range(weights.shape[1]):
         pair = []
         for k, ref in enumerate((own_ref, other_ref)):
-            copy = pltpu.make_async_copy(ref.at[i], weights.at[k, i], sems.at[k, i])
+            source = ref.at[i, pl.ds(0, weights.shape[2])]
+            copy = pltpu.make_async_copy(source, weights.at[k, i], sems.at[k, i])
             copy.start()
             pair.append(copy)
         copies.append(pair)
@@ -348,18 +346,19 @@
     def prepare(before, late):
         kept = lax.dynamic_index_in_dim(halves, z, 1, keepdims=False)
         given = lax.dynamic_index_in_dim(halves, 1 - z, 1, keepdims=False)
-        rows = x_blocks(w_query[0])
-        query = exchange(rows, OVER_X)
-        mine = kv_blocks(w_key[0], w_value[0], x, query)
+        rows = jnp.concatenate([x_blocks(w_query[0]), kv_blocks(w_key[0], w_value[0])], axis=1)
+        mine = exchange(rows, OVER_X)
+        other = swap_cores(mine)
         if late:
-            given = lax.optimization_barrier((given, query, mine))[0]
+            given = lax.optimization_barrier((given, mine))[0]
         far = lax.ppermute(given, "wide", Z_SWAP)
-        key_value = relayout_kv(mine, core, x)
+        depth = NG * CHIP
+        key_value = whole_head(mine[:, depth:], other[:, depth:], core)
         out_rows = jnp.concatenate([kept, far], axis=1)
         out_rows = lax.optimization_barrier((out_rows, before))[0]
         blocks = from_ring(lambda i: lax.dynamic_slice_in_dim(out_rows, i, 1, 0), y, 16)
-        out = jnp.concatenate(lax.optimization_barrier((blocks, mine))[0], axis=0)
-        return (query, swap_cores(query)), key_value, (out, swap_cores(out))
+        out = jnp.concatenate(blocks, axis=0)
+        return (mine, other), key_value, (out, swap_cores(out))
 
     def early_section(start, cross):
         pair = jnp.where(

time: 646 us -> 680 us (1.053)
  waiting for transfers between devices: 508 us -> 541 us
  starting transfers between devices: 75.8 us -> 66.4 us
  other arithmetic: 6.71 us -> 15 us
    ppermute x2, waiting for transfers between devices: 366 us -> 399 us  [run(): return (lax.ppermute(value, axes, cross), lax.ppermute(value, axes, same))]
    ppermute x6 -> x3, starting transfers between devices: 19.1 us -> 10.7 us  [from_ring(): blocks.append(lax.ppermute(piece((at + step) % 4), 'wide', pairs))]
    ppermute x6 -> x5, starting transfers between devices: 19.8 us -> 18.7 us  [swap_cores(): return lax.ppermute(value, 'wide', CORE_SWAP)]
    ppermute x6 -> x3, waiting for transfers between devices: 19.2 us -> 19 us  [from_ring(): blocks.append(lax.ppermute(piece((at + step) % 4), 'wide', pairs))]
  transfers between devices with their start and end apart: 22 -> 18, of which waited for: 15 -> 12; matrix products, arithmetic and copies ran while one was open for 2% -> 3% of each run, Pallas kernels for 0% -> 0%
where the time goes in v8:
time: 680 us; the launch traced here: 678 us
  waiting for transfers between devices  541 us (80%)
  starting transfers between devices  66.4 us (10%)
  blocking collectives  27.8 us (4%)
  local copies, waits for them, and re-layouts  15.7 us (2%)
  other arithmetic  15 us (2%)
  Pallas kernels  9.83 us (1%)
    ppermute x2, waiting for transfers between devices, run(): return (lax.ppermute(value, axes, cross), lax.ppermute(value, axes, same))  399 us
    ppermute x1, waiting for transfers between devices, prepare(): far = lax.ppermute(given, 'wide', Z_SWAP)  66.5 us
    all_to_all x3, waiting for transfers between devices, exchange(): lax.all_to_all(value, 'wide', 0, 0, axis_index_groups=groups, tiled=True)  36 us
    all_to_all x3, blocking collectives, exchange(): lax.all_to_all(value, 'wide', 0, 0, axis_index_groups=groups, tiled=True)  27.8 us
    all_to_all x3, starting transfers between devices, exchange(): lax.all_to_all(value, 'wide', 0, 0, axis_index_groups=groups, tiled=True)  19.5 us
    ppermute x3, waiting for transfers between devices, from_ring(): blocks.append(lax.ppermute(piece((at + step) % 4), 'wide', pairs))  19 us
    ppermute x5, starting transfers between devices, swap_cores(): return lax.ppermute(value, 'wide', CORE_SWAP)  18.7 us
  transfers between devices with their start and end apart: 18, of which 12 were waited for; matrix products, arithmetic and copies ran while one was open for 3% of the time, Pallas kernels for 0%

profile of v8, /device:TPU:481, one launch (start us, length us, event | category | flops | bytes accessed | tf_op | source)
XLA Modules:
  0.0 678.1 jit_solution(11236043329060876929)
XLA Ops:
  1.4 2.6 collective-permute-start.20
  11.6 165.4 %conditional.6 = (bf16[4,128,512]{2,1,0:T(8,128)(2,1)}, bf16[4,2560,128]{2,1,0:T(8,128)(2,1)S(1)}, bf16[4,2560,128]{2,1,0:T(8,128)(2,1)}, bf16[256,2048]{1,0:T(8...) conditional(s32[]{:T(128)} %convert_element_type.84, ...), branch_computations={%region_0.4_spmd, %region_4.5_spmd} | conditional | flops 16056391 | bytes 108267872 | solution.py:377
  17.5 4.0 all-to-all-start
  21.5 3.1 dynamic-slice_bitcast_fusion.1
  24.6 28.1 %all-to-all-done = bf16[4,2560,128]{2,1,0:T(8,128)(2,1)S(1)} async-done(((bf16[4,2560,128]{2,1,0:T(8,128)(2,1)}), bf16[4,2560,128]{2,1,0:T(8,128)(2,1)S(1)}, u32[]{:S(2)}, u32[]{:S(2)}) %all-to-all-start) | async-done | bytes 2621472 | tf_op jit(solution)/shard_map/cond/branch_0_fun/all_to_all | solution.py:39
  52.6 9.1 %collective-permute-start.5 = (bf16[4,1024,128]{2,1,0:T(8,128)(2,1)}, bf16[4,1024,128]{2,1,0:T(8,128)(2,1)}, u32[]{:S(2)}, u32[]{:S(2)}) collective-permute-start(bf16[4,1024,128]{2,1,0:T(8,128)(2,1)} %get-tuple-element.348), channel_id=1, source_target_pairs={{0,8},{1,9},{2,10},{3,11},{4,12},{5,13},{6,14},{7,15},{8,0},{9,1},... | collective-permute-start | bytes 3145736 | tf_op jit(solution)/shard_map/cond/branch_0_fun/ppermute | solution.py:354
  61.8 4.4 collective-permute-start.4
  66.2 66.5 %collective-permute-done.5 = bf16[4,1024,128]{2,1,0:T(8,128)(2,1)} collective-permute-done((bf16[4,1024,128]{2,1,0:T(8,128)(2,1)}, bf16[4,1024,128]{2,1,0:T(8,128)(2,1)}, u32[]{:S(2)}, u32[]{:S(2)}) %collective-permute-start.5) | collective-permute-done | bytes 1048608 | tf_op jit(solution)/shard_map/cond/branch_0_fun/ppermute | solution.py:354
  134.5 3.2 collective-permute-start.6
  137.7 4.5 collective-permute-start.7
  142.2 3.0 collective-permute-start.8
  145.2 5.5 collective-permute-done.6
  150.7 12.3 %collective-permute-done.7 = bf16[1,2048,128]{2,1,0:T(8,128)(2,1)S(1)} collective-permute-done((bf16[1,2048,128]{2,1,0:T(8,128)(2,1)S(1)}, bf16[1,2048,128]{2,1,0:T(8,128)(2,1)S(1)}, u32[]{:S(2)}, u32[]{:S(2)}) %collective-permute-start.7) | collective-permute-done | bytes 524320 | tf_op jit(solution)/shard_map/cond/branch_0_fun/ppermute | solution.py:65
  165.8 3.5 collective-permute-start.9
  177.9 462.0 %while.23 = (s32[]{:T(128)}, bf16[4,128,512]{2,1,0:T(8,128)(2,1)}, bf16[128,512]{1,0:T(8,128)(2,1)S(1)}, bf16[128,256]{1,0:T(8,128)(2,1)S(1)}, s32[]{:T(128)}, /...) while((s32[]{:T(128)}, bf16[4,128,512]{2,1,0:T(8,128)(2,1)}, ...), condition=%wide.region_14.15_spmd, body=%wide.region_5.14_spmd.sunk | while | flops 983069 | bytes 11141949 | solution.py:433
  178.2 413.1 %conditional.11 = (bf16[4,128,512]{2,1,0:T(8,128)(2,1)}) conditional(s32[]{:T(128)} %convert_element_type.116, bf16[4,128,512]{2,1,0:T(8,128)(2,1)} %get-tuple-element.656, (s32[]{:T(128)}, s32[]{:T(128)}, bf16[128,512]{1,0:T(8,128)(2,1)S(1)}, bf16[4,128,512]{2,1,0:T(8,128)(2,1)}) %tuple.118), branch_computations={%region_8.8_spmd, %region_9.13_spmd} | conditional | flops 262160 | bytes 4194573 | solution.py:422
  178.3 401.9 %conditional = (bf16[128,512]{1,0:T(8,128)(2,1)}, bf16[128,512]{1,0:T(8,128)(2,1)}) conditional(s32[]{:T(128)} %convert_element_type.70, bf16[128,512]{1,0:T(8,128)(2,1)S(1)} %get-tuple-element.380, bf16[128,512]{1,0:T(8,128)(2,1)S(1)} %get-tuple-element.380), branch_computations={%region_10.9_spmd, %region_11.10_spmd} | conditional | bytes 1048672 | solution.py:417
  180.9 399.2 %collective-permute-done.2 = bf16[128,512]{1,0:T(8,128)(2,1)} collective-permute-done((bf16[128,512]{1,0:T(8,128)(2,1)S(1)}, bf16[128,512]{1,0:T(8,128)(2,1)}, u32[]{:S(2)}, u32[]{:S(2)}) %collective-permute-start.2) | collective-permute-done | bytes 131104 | tf_op jit(solution)/shard_map/while/body/eval_jaxpr/cond/branch_1_fun/cond/branch_1_fun/ppermute | solution.py:406
  580.1 11.2 %conditional.1 = (bf16[4,128,512]{2,1,0:T(8,128)(2,1)}) conditional(s32[]{:T(128)} %convert_element_type.69, bf16[4,128,512]{2,1,0:T(8,128)(2,1)} %get-tuple-element.379, (bf16[128,512]{1,0:T(8,128)(2,1)}, bf16[128,512]{1,0:T(8,128)(2,1)}) %tuple.58), branch_computations={%region_12.11_spmd, %region_13.12_spmd} | conditional | flops 262144 | bytes 3145736 | solution.py:418
  581.2 9.3 %all_to_all.31 = bf16[4,128,512]{2,1,0:T(8,128)(2,1)S(1)} all-to-all(bf16[4,128,512]{2,1,0:T(8,128)(2,1)S(1)} %broadcast_in_dim.60), channel_id=1, replica_groups={{0,16,32,48},{1,17,33,49},{2,18,34,50},{3,19,35,51},{4,20,36,52},{5,21,..., dimensions={0} | all-to-all | bytes 1048576 | tf_op jit(solution)/shard_map/while/body/eval_jaxpr/cond/branch_1_fun/cond/branch_1_fun/all_to_all | solution.py:39
  591.3 48.6 %conditional.10 = ((bf16[128,512]{1,0:T(8,128)(2,1)S(1)}, bf16[128,256]{1,0:T(8,128)(2,1)S(1)})) conditional(s32[]{:T(128)} %convert_element_type.117, (bf16[128,512]{1,0:T(8,128)(2,1)S(1)}, bf16[128,256]{1,0:T(8,128)(2,1)S(1)}) %tuple.116, (s32[]{:T(128)}, s32[]{:T(128)}, bf16[4,128,512]{2,1,0:T(8,128)(2,1)}, s32[4]{0:T(128)S(1)}, ...), branch_computations={%region_6.6_spmd, %region_7.7_spmd} | conditional | flops 720900 | bytes 6947016 | solution.py:414
  591.3 4.3 project.1
  595.6 9.7 %all_to_all.29.part_ref = bf16[4,144,512]{2,1,0:T(8,128)(2,1)S(1)} all-to-all(bf16[4,144,512]{2,1,0:T(8,128)(2,1)S(1)} %project.1), channel_id=1, replica_groups={{0,2,4,6},{1,3,5,7},{8,10,12,14},{9,11,13,15},{16,18,20,22},{17,19,21,2..., dimensions={0} | all-to-all | bytes 1179648 | tf_op jit(solution)/shard_map/while/body/eval_jaxpr/cond/branch_1_fun/all_to_all | solution.py:39
  606.8 6.3 collective-permute-done.19.first_ref
  614.6 8.8 %all_to_all.30.ctx_ref = bf16[4,128,256]{2,1,0:T(8,128)(2,1)S(1)} all-to-all(bf16[4,128,256]{2,1,0:T(8,128)(2,1)S(1)} %attend.1), channel_id=1, replica_groups={{0,2,4,6},{1,3,5,7},{8,10,12,14},{9,11,13,15},{16,18,20,22},{17,19,21,2..., dimensions={0} | all-to-all | bytes 524288 | tf_op jit(solution)/shard_map/while/body/eval_jaxpr/cond/branch_1_fun/all_to_all | solution.py:39
  623.4 3.9 output.1
  627.3 3.5 all-to-all-start.4
  630.8 7.9 %all-to-all-done.4 = bf16[4,128,512]{2,1,0:T(8,128)(2,1)S(1)} async-done(((bf16[4,128,512]{2,1,0:T(8,128)(2,1)}), bf16[4,128,512]{2,1,0:T(8,128)(2,1)S(1)}, u32[]{:S(2)}, u32[]{:S(2)}) %all-to-all-start.4) | async-done | bytes 524320 | tf_op jit(solution)/shard_map/while/body/eval_jaxpr/cond/branch_1_fun/all_to_all | solution.py:39
  640.8 12.1 %all-to-all-start.6 = ((bf16[8,128,256]{2,1,0:T(8,128)(2,1)}), bf16[8,128,256]{2,1,0:T(8,128)(2,1)S(1)}, u32[]{:S(2)}, u32[]{:S(2)}) async-start(bf16[8,128,256]{2,1,0:T(8,128)(2,1)} %broadcast_in_dim.89), calls=%async_computation.6 | async-start | bytes 1048576 | tf_op jit(solution)/shard_map/all_to_all | solution.py:39
  654.9 11.8 %collective-permute-done.23 = bf16[128,256]{0,1:T(8,128)(2,1)S(1)} collective-permute-done((bf16[128,256]{0,1:T(8,128)(2,1)S(1)}, bf16[128,256]{0,1:T(8,128)(2,1)S(1)}, u32[]{:S(2)}, u32[]{:S(2)}) %collective-permute-start.23) | collective-permute-done | bytes 65568 | tf_op jit(solution)/shard_map/ppermute | solution.py:438
  666.9 6.1 collective-permute-start.24
  674.2 2.3 collective-permute-start.25
  (102 shorter events, 41.2 us)
Async XLA Ops:
  1.4 7.1 %collective-permute-start.20 = (bf16[128,128]{1,0:T(8,128)(2,1)S(1)}, bf16[128,128]{1,0:T(8,128)(2,1)S(1)}, u32[]{:S(2)}, u32[]{:S(2)}) collective-permute-start(bf16[128,128]{1,0:T(8,128)(2,1)S(1)} %dynamic-slice_bitcast_fusion.5), channel_id=1, source_target_pairs={{0,1},{1,0},{2,3},{3,2},{4,5},{5,4},{6,7},{7,6},{8,9},{9,8},{10,11... | collective-permute-start | bytes 98312 | tf_op jit(solution)/shard_map/ppermute | solution.py:43
  4.0 6.6 collective-permute-start.22
  9.3 2.3 collective-permute-start.21
  11.6 1.9 copy-start.6
  11.6 2.8 copy-start.8
  17.5 35.1 %all-to-all-start = ((bf16[4,2560,128]{2,1,0:T(8,128)(2,1)}), bf16[4,2560,128]{2,1,0:T(8,128)(2,1)S(1)}, u32[]{:S(2)}, u32[]{:S(2)}) async-start(bf16[4,2560,128]{2,1,0:T(8,128)(2,1)} %pad_maximum_fusion), calls=%async_computation | async-start | bytes 5242880 | tf_op jit(solution)/shard_map/cond/branch_0_fun/all_to_all | solution.py:39
  52.6 80.0 %collective-permute-start.5 = (bf16[4,1024,128]{2,1,0:T(8,128)(2,1)}, bf16[4,1024,128]{2,1,0:T(8,128)(2,1)}, u32[]{:S(2)}, u32[]{:S(2)}) collective-permute-start(bf16[4,1024,128]{2,1,0:T(8,128)(2,1)} %get-tuple-element.348), channel_id=1, source_target_pairs={{0,8},{1,9},{2,10},{3,11},{4,12},{5,13},{6,14},{7,15},{8,0},{9,1},... | collective-permute-start | bytes 3145736 | tf_op jit(solution)/shard_map/cond/branch_0_fun/ppermute | solution.py:354
  61.8 107.9 %collective-permute-start.4 = (bf16[4,2560,128]{2,1,0:T(8,128)(2,1)S(1)}, bf16[4,2560,128]{2,1,0:T(8,128)(2,1)}, u32[]{:S(2)}, u32[]{:S(2)}) collective-permute-start(bf16[4,2560,128]{2,1,0:T(8,128)(2,1)S(1)} %all-to-all-done), channel_id=1, source_target_pairs={{0,1},{1,0},{2,3},{3,2},{4,5},{5,4},{6,7},{7,6},{8,9},{9,8},{10,11... | collective-permute-start | bytes 7864328 | tf_op jit(solution)/shard_map/cond/branch_0_fun/ppermute | solution.py:43
  134.5 16.2 %collective-permute-start.6 = (bf16[1,2048,128]{2,1,0:T(8,128)(2,1)S(1)}, bf16[1,2048,128]{2,1,0:T(8,128)(2,1)S(1)}, u32[]{:S(2)}, u32[]{:S(2)}) collective-permute-start(bf16[1,2048,128]{2,1,0:T(8,128)(2,1)S(1)} %get-tuple-element.485), channel_id=1, source_target_pairs={{0,16},{1,17},{2,18},{3,19},{4,20},{5,21},{6,22},{7,23},{8,24},{9,... | collective-permute-start | bytes 1572872 | tf_op jit(solution)/shard_map/cond/branch_0_fun/ppermute | solution.py:65
  137.7 25.3 %collective-permute-start.7 = (bf16[1,2048,128]{2,1,0:T(8,128)(2,1)S(1)}, bf16[1,2048,128]{2,1,0:T(8,128)(2,1)S(1)}, u32[]{:S(2)}, u32[]{:S(2)}) collective-permute-start(bf16[1,2048,128]{2,1,0:T(8,128)(2,1)S(1)} %get-tuple-element.484), channel_id=1, source_target_pairs={{0,32},{1,33},{2,34},{3,35},{4,36},{5,37},{6,38},{7,39},{8,40},{9,... | collective-permute-start | bytes 1572872 | tf_op jit(solution)/shard_map/cond/branch_0_fun/ppermute | solution.py:65
  142.2 22.0 %collective-permute-start.8 = (bf16[1,2048,128]{2,1,0:T(8,128)(2,1)S(1)}, bf16[1,2048,128]{2,1,0:T(8,128)(2,1)S(1)}, u32[]{:S(2)}, u32[]{:S(2)}) collective-permute-start(bf16[1,2048,128]{2,1,0:T(8,128)(2,1)S(1)} %get-tuple-element.483), channel_id=1, source_target_pairs={{0,48},{1,49},{2,50},{3,51},{4,52},{5,53},{6,54},{7,55},{8,56},{9,... | collective-permute-start | bytes 1572872 | tf_op jit(solution)/shard_map/cond/branch_0_fun/ppermute | solution.py:65
  164.2 5.1 copy-start.11
  165.8 10.3 %collective-permute-start.9 = (bf16[4,2048,128]{2,1,0:T(8,128)(2,1)}, bf16[4,2048,128]{2,1,0:T(8,128)(2,1)}, u32[]{:S(2)}, u32[]{:S(2)}) collective-permute-start(bf16[4,2048,128]{2,1,0:T(8,128)(2,1)} %pad_maximum_fusion.2), channel_id=1, source_target_pairs={{0,1},{1,0},{2,3},{3,2},{4,5},{5,4},{6,7},{7,6},{8,9},{9,8},{10,11... | collective-permute-start | bytes 6291464 | tf_op jit(solution)/shard_map/cond/branch_0_fun/ppermute | solution.py:43
  176.9 1.0 copy-start.2
  177.9 477.0 %copy-start.10 = (s32[256,1]{0,1:T(1,128)S(1)}, s32[256,1]{0,1:T(1,128)}, u32[]{:S(2)}) copy-start(s32[256,1]{0,1:T(1,128)} %param.29) | copy-start | bytes 3076
  178.3 401.8 %collective-permute-start.2 = (bf16[128,512]{1,0:T(8,128)(2,1)S(1)}, bf16[128,512]{1,0:T(8,128)(2,1)}, u32[]{:S(2)}, u32[]{:S(2)}) collective-permute-start(bf16[128,512]{1,0:T(8,128)(2,1)S(1)} %param.6), channel_id=1, source_target_pairs={{0,72},{1,73},{2,74},{3,75},{4,76},{5,77},{6,78},{7,79},{8,64},{9,... | collective-permute-start | bytes 393224 | tf_op jit(solution)/shard_map/while/body/eval_jaxpr/cond/branch_1_fun/cond/branch_1_fun/ppermute | solution.py:406
  179.6 400.5 %collective-permute-start.3 = (bf16[128,512]{1,0:T(8,128)(2,1)S(1)}, bf16[128,512]{1,0:T(8,128)(2,1)}, u32[]{:S(2)}, u32[]{:S(2)}) collective-permute-start(bf16[128,512]{1,0:T(8,128)(2,1)S(1)} %param.6), channel_id=1, source_target_pairs={{0,64},{1,65},{2,66},{3,67},{4,68},{5,69},{6,70},{7,71},{8,72},{9,... | collective-permute-start | bytes 393224 | tf_op jit(solution)/shard_map/while/body/eval_jaxpr/cond/branch_1_fun/cond/branch_1_fun/ppermute | solution.py:406
  605.5 21.8 %copy-start.4 = (bf16[128,256]{1,0:T(8,128)(2,1)}, bf16[128,256]{1,0:T(8,128)(2,1)S(1)}, u32[]{:S(2)}) copy-start(bf16[128,256]{1,0:T(8,128)(2,1)S(1)} %get-tuple-element.620.own_ref) | copy-start | bytes 196612 | tf_op jit(solution)/shard_map/while/body/eval_jaxpr/cond
  605.5 7.6 %collective-permute-start.19 = (bf16[128,256]{1,0:T(8,128)(2,1)S(1)}, bf16[128,256]{1,0:T(8,128)(2,1)S(1)}, u32[]{:S(2)}, u32[]{:S(2)}) collective-permute-start(bf16[128,256]{1,0:T(8,128)(2,1)S(1)} %get-tuple-element.620.own_ref), channel_id=1, source_target_pairs={{0,1},{2,3},{4,5},{6,7},{8,9},{10,11},{12,13},{14,15},{16,17},{18,... | collective-permute-start | bytes 196616 | tf_op jit(solution)/shard_map/while/body/eval_jaxpr/cond/branch_1_fun/ppermute | solution.py:396
  627.3 11.4 %all-to-all-start.4 = ((bf16[4,128,512]{2,1,0:T(8,128)(2,1)}), bf16[4,128,512]{2,1,0:T(8,128)(2,1)S(1)}, u32[]{:S(2)}, u32[]{:S(2)}) async-start(bf16[4,128,512]{2,1,0:T(8,128)(2,1)} %output.1), calls=%async_computation.4 | async-start | bytes 1048576 | tf_op jit(solution)/shard_map/while/body/eval_jaxpr/cond/branch_1_fun/all_to_all | solution.py:39
  630.8 9.1 %copy-start.5 = (bf16[128,256]{1,0:T(8,128)(2,1)S(1)}, bf16[128,256]{1,0:T(8,128)(2,1)}, u32[]{:S(2)}) copy-start(bf16[128,256]{1,0:T(8,128)(2,1)} %copy-done.4) | copy-start | bytes 196612 | tf_op jit(solution)/shard_map/while/body/eval_jaxpr/cond
  640.8 33.0 %all-to-all-start.6 = ((bf16[8,128,256]{2,1,0:T(8,128)(2,1)}), bf16[8,128,256]{2,1,0:T(8,128)(2,1)S(1)}, u32[]{:S(2)}, u32[]{:S(2)}) async-start(bf16[8,128,256]{2,1,0:T(8,128)(2,1)} %broadcast_in_dim.89), calls=%async_computation.6 | async-start | bytes 1048576 | tf_op jit(solution)/shard_map/all_to_all | solution.py:39
  653.0 13.7 %collective-permute-start.23 = (bf16[128,256]{0,1:T(8,128)(2,1)S(1)}, bf16[128,256]{0,1:T(8,128)(2,1)S(1)}, u32[]{:S(2)}, u32[]{:S(2)}) collective-permute-start(bf16[128,256]{0,1:T(8,128)(2,1)S(1)} %dynamic-slice_bitcast_fusion.4), channel_id=1, source_target_pairs={{0,8},{1,9},{2,10},{3,11},{4,12},{5,13},{6,14},{7,15},{8,0},{9,1},... | collective-permute-start | bytes 196616 | tf_op jit(solution)/shard_map/ppermute | solution.py:438
  666.9 6.9 %collective-permute-start.24 = (bf16[128,128]{1,0:T(8,128)(2,1)S(1)}, bf16[128,128]{1,0:T(8,128)(2,1)S(1)}, u32[]{:S(2)}, u32[]{:S(2)}) collective-permute-start(bf16[128,128]{1,0:T(8,128)(2,1)S(1)} %bitcast.100), channel_id=1, source_target_pairs={{0,1},{1,0},{2,3},{3,2},{4,5},{5,4},{6,7},{7,6},{8,9},{9,8},{10,11... | collective-permute-start | bytes 98312 | tf_op jit(solution)/shard_map/ppermute | solution.py:43
  674.2 3.1 collective-permute-start.25

commit v9 on v7

--- a/solution.py
+++ b/solution.py
@@ -72,11 +72,14 @@
     )
 
 
-def kv_blocks(w_key, w_value, x, after):
+def kv_blocks(w_key, w_value):
     both = jnp.stack([w_key.T, w_value.T])
     width = both.shape[1]
     both = both.reshape(2, width, NG, NX, CHIP).transpose(3, 0, 1, 2, 4)
-    both = both.reshape(NX, 2 * width, NG * CHIP)
+    return both.reshape(NX, 2 * width, NG * CHIP)
+
+
+def kv_over_x(both, x, after):
     both = lax.optimization_barrier((both, after))[0]
     blocks = from_ring(lambda i: lax.dynamic_slice_in_dim(both, i, 1, 0), x, NC)
     return jnp.concatenate(blocks, axis=0)
@@ -165,6 +168,21 @@
         compiler_params=pltpu.CompilerParams(vmem_limit_bytes=VMEM),
         name="project",
     )(info, gathered, gain, wkv, *wq)
+
+
+def join_kernel(same_ref, cross_ref, out_ref):
+    pair = same_ref[...].astype(jnp.float32) + cross_ref[...].astype(jnp.float32)
+    for y in range(NY):
+        out_ref[y] = pair.astype(jnp.bfloat16)
+
+
+def join(same, cross):
+    return pl.pallas_call(
+        join_kernel,
+        out_shape=jax.ShapeDtypeStruct((NY,) + same.shape, jnp.bfloat16),
+        compiler_params=pltpu.CompilerParams(vmem_limit_bytes=VMEM),
+        name="join",
+    )(same, cross)
 
 
 def turn_kernel(features, part_ref, cos_ref, sin_ref, q_ref, kv_ref):
@@ -327,9 +345,6 @@
     start = by_core(core, kept, from_core, 1)
     cross = by_core(core, cross_own, cross_other, 1)
 
-    gain_x = lax.dynamic_index_in_dim(gain.reshape(NG, NX, CHIP), x, 1, keepdims=False)
-    gain_x = gain_x.reshape(1, NG * CHIP)
-
     lane = jnp.arange(HD, dtype=jnp.int32)
     freq = jnp.power(ROPE_BASE, -2.0 * (lane // 2).astype(jnp.float32) / HD)
     position = (core * HALF + jnp.arange(HALF, dtype=jnp.int32)).astype(jnp.float32)
@@ -338,28 +353,31 @@
     sin = jnp.where(lane[None, :] % 2 == 0, -1.0, 1.0) * jnp.sin(angle)
     info = jnp.stack([core, length[0], z, y]).astype(jnp.int32)
 
-    def gather(pair):
-        return exchange(jnp.broadcast_to(pair[None], (NY, HALF, NZ * CHIP)), OVER_Y)
-
     raw = w_out[0].reshape(NY, NZ * NX * CHIP, HD)
 
     halves = raw.reshape(NY, NZ, NX * CHIP, HD)
 
+    kept_rows = lax.dynamic_index_in_dim(halves, z, 1, keepdims=False)
+    given_rows = lax.dynamic_index_in_dim(halves, 1 - z, 1, keepdims=False)
+    blocks_x = x_blocks(w_query[0])
+    both = kv_blocks(w_key[0], w_value[0])
+    blocks_x, both, given_rows = lax.optimization_barrier((blocks_x, both, given_rows))
+
     def prepare(before, late):
-        kept = lax.dynamic_index_in_dim(halves, z, 1, keepdims=False)
-        given = lax.dynamic_index_in_dim(halves, 1 - z, 1, keepdims=False)
-        rows = x_blocks(w_query[0])
-        query = exchange(rows, OVER_X)
-        mine = kv_blocks(w_key[0], w_value[0], x, query)
+        kept, given = kept_rows, given_rows
+        query = exchange(blocks_x, OVER_X)
+        mine = kv_over_x(both, x, query)
         if late:
             given = lax.optimization_barrier((given, query, mine))[0]
         far = lax.ppermute(given, "wide", Z_SWAP)
+        rows_gain = lax.dynamic_index_in_dim(gain.reshape(NG, NX, CHIP), x, 1, keepdims=False)
         key_value = relayout_kv(mine, core, x)
         out_rows = jnp.concatenate([kept, far], axis=1)
         out_rows = lax.optimization_barrier((out_rows, before))[0]
         blocks = from_ring(lambda i: lax.dynamic_slice_in_dim(out_rows, i, 1, 0), y, 16)
         out = jnp.concatenate(lax.optimization_barrier((blocks, mine))[0], axis=0)
-        return (query, swap_cores(query)), key_value, (out, swap_cores(out))
+        gains = rows_gain.reshape(1, NG * CHIP)
+        return (query, swap_cores(query)), key_value, (out, swap_cores(out)), gains
 
     def early_section(start, cross):
         pair = jnp.where(
@@ -375,13 +393,13 @@
         blank = jnp.zeros((NY, HALF, NZ * CHIP), jnp.bfloat16)
         return blank, prepare(start, True), ranks(placement, core)
 
-    gathered, (wq, wkv, wo), items = lax.cond(
+    gathered, (wq, wkv, wo, gain_x), items = lax.cond(
         segment <= 1, early_section, late_section, start, cross
     )
     cos, sin = lax.optimization_barrier((cos, sin))
 
     def later_gather(same, cross):
-        return gather((same.astype(jnp.float32) + cross.astype(jnp.float32)).astype(jnp.bfloat16))
+        return exchange(join(same, cross), OVER_Y)
 
     def summed(parts, own):
         parts = parts.astype(jnp.float32)

time: 646 us -> 647 us (level)
  no operation moved by 1% of the time
where the time goes in v9:
time: 647 us; the launch traced here: 646 us
  waiting for transfers between devices  509 us (79%)
  starting transfers between devices  76 us (12%)
  blocking collectives  27.8 us (4%)
  local copies, waits for them, and re-layouts  14.4 us (2%)
  Pallas kernels  10.1 us (2%)
    ppermute x2, waiting for transfers between devices, run(): return (lax.ppermute(value, axes, cross), lax.ppermute(value, axes, same))  365 us
    ppermute x1, waiting for transfers between devices, prepare(): far = lax.ppermute(given, 'wide', Z_SWAP)  68.6 us
    all_to_all x3, waiting for transfers between devices, exchange(): lax.all_to_all(value, 'wide', 0, 0, axis_index_groups=groups, tiled=True)  33.8 us
    all_to_all x3, blocking collectives, exchange(): lax.all_to_all(value, 'wide', 0, 0, axis_index_groups=groups, tiled=True)  27.8 us
    ppermute x6, waiting for transfers between devices, from_ring(): blocks.append(lax.ppermute(piece((at + step) % 4), 'wide', pairs))  20.4 us
    all_to_all x3, starting transfers between devices, exchange(): lax.all_to_all(value, 'wide', 0, 0, axis_index_groups=groups, tiled=True)  20 us
    ppermute x6, starting transfers between devices, swap_cores(): return lax.ppermute(value, 'wide', CORE_SWAP)  19.8 us
    ppermute x6, starting transfers between devices, from_ring(): blocks.append(lax.ppermute(piece((at + step) % 4), 'wide', pairs))  19.1 us
  transfers between devices with their start and end apart: 22, of which 15 were waited for; matrix products, arithmetic and copies ran while one was open for 2% of the time, Pallas kernels for 0%

profile of v9, /device:TPU:481, one launch (start us, length us, event | category | flops | bytes accessed | tf_op | source)
XLA Modules:
  0.0 645.7 jit_solution(10774047939749559144)
XLA Ops:
  1.6 2.6 collective-permute-start.28
  11.5 3.3 copy.58
  18.2 164.1 %conditional.6 = (bf16[4,128,512]{2,1,0:T(8,128)(2,1)S(1)}, bf16[4,2048,128]{2,1,0:T(8,128)(2,1)}, bf16[4,2048,128]{2,1,0:T(8,128)(2,1)}, bf16[256,2048]{1,0:T(8...) conditional(s32[]{:T(128)} %convert_element_type.75, ...), branch_computations={%region_0.4_spmd, %region_4.5_spmd} | conditional | flops 9764990 | bytes 65424336 | solution.py:396
  18.2 4.5 all-to-all-start.4
  22.8 25.8 %all-to-all-done.4 = bf16[4,2048,128]{2,1,0:T(8,128)(2,1)} async-done(((bf16[4,2048,128]{2,1,0:T(8,128)(2,1)}), bf16[4,2048,128]{2,1,0:T(8,128)(2,1)}, u32[]{:S(2)}, u32[]{:S(2)}) %all-to-all-start.4) | async-done | bytes 2097184 | tf_op jit(solution)/shard_map/cond/branch_0_fun/all_to_all | solution.py:39
  50.8 3.7 collective-permute-start.7
  58.4 3.6 collective-permute-done.8
  62.0 8.1 %collective-permute-start.10 = (bf16[4,1024,128]{2,1,0:T(8,128)(2,1)S(1)}, bf16[4,1024,128]{2,1,0:T(8,128)(2,1)}, u32[]{:S(2)}, u32[]{:S(2)}) collective-permute-start(bf16[4,1024,128]{2,1,0:T(8,128)(2,1)S(1)} %get-tuple-element.355), channel_id=1, source_target_pairs={{0,8},{1,9},{2,10},{3,11},{4,12},{5,13},{6,14},{7,15},{8,0},{9,1},... | collective-permute-start | bytes 3145736 | tf_op jit(solution)/shard_map/cond/branch_0_fun/ppermute | solution.py:372
  70.2 68.6 %collective-permute-done.10 = bf16[4,1024,128]{2,1,0:T(8,128)(2,1)} collective-permute-done((bf16[4,1024,128]{2,1,0:T(8,128)(2,1)S(1)}, bf16[4,1024,128]{2,1,0:T(8,128)(2,1)}, u32[]{:S(2)}, u32[]{:S(2)}) %collective-permute-start.10) | collective-permute-done | bytes 1048608 | tf_op jit(solution)/shard_map/cond/branch_0_fun/ppermute | solution.py:372
  140.3 3.2 collective-permute-start.11
  143.5 4.5 collective-permute-start.12
  148.0 3.0 collective-permute-start.13
  151.0 3.5 collective-permute-start.5
  156.2 12.3 %collective-permute-done.12 = bf16[1,2048,128]{2,1,0:T(8,128)(2,1)S(1)} collective-permute-done((bf16[1,2048,128]{2,1,0:T(8,128)(2,1)S(1)}, bf16[1,2048,128]{2,1,0:T(8,128)(2,1)S(1)}, u32[]{:S(2)}, u32[]{:S(2)}) %collective-permute-start.12) | collective-permute-done | bytes 524320 | tf_op jit(solution)/shard_map/cond/branch_0_fun/ppermute | solution.py:65
  173.4 3.5 collective-permute-start.14
  182.4 425.1 %while.23 = (s32[]{:T(128)}, bf16[4,128,512]{2,1,0:T(8,128)(2,1)S(1)}, bf16[128,512]{1,0:T(8,128)(2,1)S(1)}, bf16[128,256]{1,0:T(8,128)(2,1)S(1)}, s32[]{:T(128)...) while((s32[]{:T(128)}, ...), condition=%wide.region_14.15_spmd, body=%wide.region_5.14_spmd.sunk | while | flops 720925 | bytes 10093373 | solution.py:452
  182.9 377.5 %conditional.11 = (bf16[4,128,512]{2,1,0:T(8,128)(2,1)S(1)}) conditional(s32[]{:T(128)} %convert_element_type.104, bf16[4,128,512]{2,1,0:T(8,128)(2,1)S(1)} %get-tuple-element.707, (s32[]{:T(128)}, s32[]{:T(128)}, bf16[128,512]{1,0:T(8,128)(2,1)S(1)}, bf16[4,128,512]{2,1,0:T(8,128)(2,1)S(1)}) %tuple.141), branch_computations={%region_8.8_spmd, %region_9.13_spmd} | conditional | flops 16 | bytes 3145997 | solution.py:441
  182.9 367.1 %conditional = (bf16[128,512]{1,0:T(8,128)(2,1)}, bf16[128,512]{1,0:T(8,128)(2,1)}) conditional(s32[]{:T(128)} %convert_element_type.61, bf16[128,512]{1,0:T(8,128)(2,1)S(1)} %get-tuple-element.399, bf16[128,512]{1,0:T(8,128)(2,1)S(1)} %get-tuple-element.399), branch_computations={%region_10.9_spmd, %region_11.10_spmd} | conditional | bytes 1048672 | solution.py:436
  185.5 364.5 %collective-permute-done.2 = bf16[128,512]{1,0:T(8,128)(2,1)} collective-permute-done((bf16[128,512]{1,0:T(8,128)(2,1)S(1)}, bf16[128,512]{1,0:T(8,128)(2,1)}, u32[]{:S(2)}, u32[]{:S(2)}) %collective-permute-start.2) | collective-permute-done | bytes 131104 | tf_op jit(solution)/shard_map/while/body/eval_jaxpr/cond/branch_1_fun/cond/branch_1_fun/ppermute | solution.py:425
  550.1 10.4 %conditional.1 = (bf16[4,128,512]{2,1,0:T(8,128)(2,1)S(1)}) conditional(s32[]{:T(128)} %convert_element_type.60, bf16[4,128,512]{2,1,0:T(8,128)(2,1)S(1)} %get-tuple-element.398, (bf16[128,512]{1,0:T(8,128)(2,1)}, bf16[128,512]{1,0:T(8,128)(2,1)}) %tuple.62), branch_computations={%region_12.11_spmd, %region_13.12_spmd} | conditional | bytes 2097160 | solution.py:437
  551.1 9.3 %all_to_all.31 = bf16[4,128,512]{2,1,0:T(8,128)(2,1)S(1)} all-to-all(bf16[4,128,512]{2,1,0:T(8,128)(2,1)S(1)} %join.1), channel_id=1, replica_groups={{0,16,32,48},{1,17,33,49},{2,18,34,50},{3,19,35,51},{4,20,36,52},{5,21,..., dimensions={0} | all-to-all | bytes 1048576 | tf_op jit(solution)/shard_map/while/body/eval_jaxpr/cond/branch_1_fun/cond/branch_1_fun/all_to_all | solution.py:39
  560.5 47.0 %conditional.10 = ((bf16[128,512]{1,0:T(8,128)(2,1)S(1)}, bf16[128,256]{1,0:T(8,128)(2,1)S(1)})) conditional(s32[]{:T(128)} %convert_element_type.105, (bf16[128,512]{1,0:T(8,128)(2,1)S(1)}, bf16[128,256]{1,0:T(8,128)(2,1)S(1)}) %tuple.139, (s32[]{:T(128)}, s32[]{:T(128)}, bf16[4,128,512]{2,1,0:T(8,128)(2,1)S(1)}, s32[4]{0:T(128)S(1)}, ...), branch_computations={%region_6.6_spmd, %region_7.7_spmd} | conditional | flops 720900 | bytes 6947016 | solution.py:433
  560.5 3.6 project.1
  564.0 9.7 %all_to_all.29.part_ref = bf16[4,144,512]{2,1,0:T(8,128)(2,1)S(1)} all-to-all(bf16[4,144,512]{2,1,0:T(8,128)(2,1)S(1)} %project.1), channel_id=1, replica_groups={{0,2,4,6},{1,3,5,7},{8,10,12,14},{9,11,13,15},{16,18,20,22},{17,19,21,2..., dimensions={0} | all-to-all | bytes 1179648 | tf_op jit(solution)/shard_map/while/body/eval_jaxpr/cond/branch_1_fun/all_to_all | solution.py:39
  575.3 6.3 collective-permute-done.4.first_ref
  583.0 8.8 %all_to_all.30.ctx_ref = bf16[4,128,256]{2,1,0:T(8,128)(2,1)S(1)} all-to-all(bf16[4,128,256]{2,1,0:T(8,128)(2,1)S(1)} %attend.1), channel_id=1, replica_groups={{0,2,4,6},{1,3,5,7},{8,10,12,14},{9,11,13,15},{16,18,20,22},{17,19,21,2..., dimensions={0} | all-to-all | bytes 524288 | tf_op jit(solution)/shard_map/while/body/eval_jaxpr/cond/branch_1_fun/all_to_all | solution.py:39
  591.8 3.9 output.1
  595.7 3.5 all-to-all-start.3
  599.3 7.9 %all-to-all-done.3 = bf16[4,128,512]{2,1,0:T(8,128)(2,1)S(1)} async-done(((bf16[4,128,512]{2,1,0:T(8,128)(2,1)}), bf16[4,128,512]{2,1,0:T(8,128)(2,1)S(1)}, u32[]{:S(2)}, u32[]{:S(2)}) %all-to-all-start.3) | async-done | bytes 524320 | tf_op jit(solution)/shard_map/while/body/eval_jaxpr/cond/branch_1_fun/all_to_all | solution.py:39
  608.3 12.1 %all-to-all-start.6 = ((bf16[8,128,256]{2,1,0:T(8,128)(2,1)}), bf16[8,128,256]{2,1,0:T(8,128)(2,1)S(1)}, u32[]{:S(2)}, u32[]{:S(2)}) async-start(bf16[8,128,256]{2,1,0:T(8,128)(2,1)} %broadcast_in_dim.83), calls=%async_computation.6 | async-start | bytes 1048576 | tf_op jit(solution)/shard_map/all_to_all | solution.py:39
  622.5 11.8 %collective-permute-done.31 = bf16[128,256]{0,1:T(8,128)(2,1)S(1)} collective-permute-done((bf16[128,256]{0,1:T(8,128)(2,1)S(1)}, bf16[128,256]{0,1:T(8,128)(2,1)S(1)}, u32[]{:S(2)}, u32[]{:S(2)}) %collective-permute-start.31) | collective-permute-done | bytes 65568 | tf_op jit(solution)/shard_map/ppermute | solution.py:457
  634.4 6.1 collective-permute-start.32
  (115 shorter events, 45.6 us)
Async XLA Ops:
  0.6 9.3 %copy-start.2 = (bf16[1,8192,128]{2,1,0:T(8,128)(2,1)S(1)}, bf16[1,8192,128]{2,1,0:T(8,128)(2,1)}, u32[]{:S(2)}) copy-start(bf16[1,8192,128]{2,1,0:T(8,128)(2,1)} %param.27) | copy-start | bytes 6291460
  1.6 13.5 %collective-permute-start.28 = (bf16[128,128]{1,0:T(8,128)(2,1)S(1)}, bf16[128,128]{1,0:T(8,128)(2,1)S(1)}, u32[]{:S(2)}, u32[]{:S(2)}) collective-permute-start(bf16[128,128]{1,0:T(8,128)(2,1)S(1)} %dynamic-slice_bitcast_fusion.3), channel_id=1, source_target_pairs={{0,1},{1,0},{2,3},{3,2},{4,5},{5,4},{6,7},{7,6},{8,9},{9,8},{10,11... | collective-permute-start | bytes 98312 | tf_op jit(solution)/shard_map/ppermute | solution.py:43
  4.1 12.3 %collective-permute-start.30 = (bf16[128,128]{1,0:T(8,128)(2,1)S(1)}, bf16[128,128]{1,0:T(8,128)(2,1)}, u32[]{:S(2)}, u32[]{:S(2)}) collective-permute-start(bf16[128,128]{1,0:T(8,128)(2,1)S(1)} %dynamic-slice_bitcast_fusion.3), channel_id=1, source_target_pairs={{448,9},{449,8},{450,11},{451,10},{452,13},{453,12},{454,15},{455,... | collective-permute-start | bytes 98312 | tf_op jit(solution)/shard_map/ppermute | solution.py:344
  11.5 3.3 copy-start.3
  11.5 3.6 copy-start.6
  11.5 6.7 %copy-start.4 = (bf16[4,1024,128]{2,1,0:T(8,128)(2,1)S(1)}, bf16[4,1024,128]{2,1,0:T(8,128)(2,1)}, u32[]{:S(2)}) copy-start(bf16[4,1024,128]{2,1,0:T(8,128)(2,1)} %get-tuple-element.445) | copy-start | bytes 3145732
  11.5 6.7 %copy-start.5 = (f32[1,8192]{1,0:T(1,128)S(1)}, f32[1,8192]{1,0:T(1,128)}, u32[]{:S(2)}) copy-start(f32[1,8192]{1,0:T(1,128)} %param.23) | copy-start | bytes 98308
  11.5 6.7 %copy-start.7 = (s32[256,1]{0,1:T(1,128)S(1)}, s32[256,1]{0,1:T(1,128)}, u32[]{:S(2)}) copy-start(s32[256,1]{0,1:T(1,128)} %param.29) | copy-start | bytes 3076
  15.1 2.3 collective-permute-start.29
  18.2 30.4 %all-to-all-start.4 = ((bf16[4,2048,128]{2,1,0:T(8,128)(2,1)}), bf16[4,2048,128]{2,1,0:T(8,128)(2,1)}, u32[]{:S(2)}, u32[]{:S(2)}) async-start(bf16[4,2048,128]{2,1,0:T(8,128)(2,1)} %get-tuple-element.348), calls=%async_computation.4 | async-start | bytes 4194304 | tf_op jit(solution)/shard_map/cond/branch_0_fun/all_to_all | solution.py:39
  48.6 8.4 %collective-permute-start.6 = (bf16[1,32,2048]{2,1,0:T(8,128)(2,1)S(1)}, bf16[1,32,2048]{2,1,0:T(8,128)(2,1)S(1)}, u32[]{:S(2)}, u32[]{:S(2)}) collective-permute-start(bf16[1,32,2048]{2,1,0:T(8,128)(2,1)S(1)} %get-tuple-element.524), channel_id=1, source_target_pairs={{0,2},{1,3},{2,4},{3,5},{4,6},{5,7},{6,0},{7,1},{8,10},{9,11},{10,... | collective-permute-start | bytes 393224 | tf_op jit(solution)/shard_map/cond/branch_0_fun/ppermute | solution.py:65
  50.8 7.5 %collective-permute-start.7 = (bf16[1,32,2048]{2,1,0:T(8,128)(2,1)S(1)}, bf16[1,32,2048]{2,1,0:T(8,128)(2,1)S(1)}, u32[]{:S(2)}, u32[]{:S(2)}) collective-permute-start(bf16[1,32,2048]{2,1,0:T(8,128)(2,1)S(1)} %get-tuple-element.523), channel_id=1, source_target_pairs={{0,4},{1,5},{2,6},{3,7},{4,0},{5,1},{6,2},{7,3},{8,12},{9,13},{10,... | collective-permute-start | bytes 393224 | tf_op jit(solution)/shard_map/cond/branch_0_fun/ppermute | solution.py:65
  54.5 7.4 %collective-permute-start.8 = (bf16[1,32,2048]{2,1,0:T(8,128)(2,1)S(1)}, bf16[1,32,2048]{2,1,0:T(8,128)(2,1)S(1)}, u32[]{:S(2)}, u32[]{:S(2)}) collective-permute-start(bf16[1,32,2048]{2,1,0:T(8,128)(2,1)S(1)} %get-tuple-element.522), channel_id=1, source_target_pairs={{0,6},{1,7},{2,0},{3,1},{4,2},{5,3},{6,4},{7,5},{8,14},{9,15},{10,... | collective-permute-start | bytes 393224 | tf_op jit(solution)/shard_map/cond/branch_0_fun/ppermute | solution.py:65
  62.0 76.7 %collective-permute-start.10 = (bf16[4,1024,128]{2,1,0:T(8,128)(2,1)S(1)}, bf16[4,1024,128]{2,1,0:T(8,128)(2,1)}, u32[]{:S(2)}, u32[]{:S(2)}) collective-permute-start(bf16[4,1024,128]{2,1,0:T(8,128)(2,1)S(1)} %get-tuple-element.355), channel_id=1, source_target_pairs={{0,8},{1,9},{2,10},{3,11},{4,12},{5,13},{6,14},{7,15},{8,0},{9,1},... | collective-permute-start | bytes 3145736 | tf_op jit(solution)/shard_map/cond/branch_0_fun/ppermute | solution.py:372
  140.3 16.0 %collective-permute-start.11 = (bf16[1,2048,128]{2,1,0:T(8,128)(2,1)S(1)}, bf16[1,2048,128]{2,1,0:T(8,128)(2,1)S(1)}, u32[]{:S(2)}, u32[]{:S(2)}) collective-permute-start(bf16[1,2048,128]{2,1,0:T(8,128)(2,1)S(1)} %get-tuple-element.509), channel_id=1, source_target_pairs={{0,16},{1,17},{2,18},{3,19},{4,20},{5,21},{6,22},{7,23},{8,24},{9,... | collective-permute-start | bytes 1572872 | tf_op jit(solution)/shard_map/cond/branch_0_fun/ppermute | solution.py:65
  143.5 25.1 %collective-permute-start.12 = (bf16[1,2048,128]{2,1,0:T(8,128)(2,1)S(1)}, bf16[1,2048,128]{2,1,0:T(8,128)(2,1)S(1)}, u32[]{:S(2)}, u32[]{:S(2)}) collective-permute-start(bf16[1,2048,128]{2,1,0:T(8,128)(2,1)S(1)} %get-tuple-element.508), channel_id=1, source_target_pairs={{0,32},{1,33},{2,34},{3,35},{4,36},{5,37},{6,38},{7,39},{8,40},{9,... | collective-permute-start | bytes 1572872 | tf_op jit(solution)/shard_map/cond/branch_0_fun/ppermute | solution.py:65
  148.0 22.0 %collective-permute-start.13 = (bf16[1,2048,128]{2,1,0:T(8,128)(2,1)S(1)}, bf16[1,2048,128]{2,1,0:T(8,128)(2,1)S(1)}, u32[]{:S(2)}, u32[]{:S(2)}) collective-permute-start(bf16[1,2048,128]{2,1,0:T(8,128)(2,1)S(1)} %get-tuple-element.507), channel_id=1, source_target_pairs={{0,48},{1,49},{2,50},{3,51},{4,52},{5,53},{6,54},{7,55},{8,56},{9,... | collective-permute-start | bytes 1572872 | tf_op jit(solution)/shard_map/cond/branch_0_fun/ppermute | solution.py:65
  151.0 31.3 %collective-permute-start.5 = (bf16[4,2048,128]{2,1,0:T(8,128)(2,1)}, bf16[4,2048,128]{2,1,0:T(8,128)(2,1)}, u32[]{:S(2)}, u32[]{:S(2)}) collective-permute-start(bf16[4,2048,128]{2,1,0:T(8,128)(2,1)} %all-to-all-done.4), channel_id=1, source_target_pairs={{0,1},{1,0},{2,3},{3,2},{4,5},{5,4},{6,7},{7,6},{8,9},{9,8},{10,11... | collective-permute-start | bytes 6291464 | tf_op jit(solution)/shard_map/cond/branch_0_fun/ppermute | solution.py:43
  173.4 8.9 %collective-permute-start.14 = (bf16[4,2048,128]{2,1,0:T(8,128)(2,1)}, bf16[4,2048,128]{2,1,0:T(8,128)(2,1)}, u32[]{:S(2)}, u32[]{:S(2)}) collective-permute-start(bf16[4,2048,128]{2,1,0:T(8,128)(2,1)} %constant_dynamic-update-slice_fusion), channel_id=1, source_target_pairs={{0,1},{1,0},{2,3},{3,2},{4,5},{5,4},{6,7},{7,6},{8,9},{9,8},{10,11... | collective-permute-start | bytes 6291464 | tf_op jit(solution)/shard_map/cond/branch_0_fun/ppermute | solution.py:43
  178.1 3.8 collective-permute-start.9
  182.9 367.1 %collective-permute-start.2 = (bf16[128,512]{1,0:T(8,128)(2,1)S(1)}, bf16[128,512]{1,0:T(8,128)(2,1)}, u32[]{:S(2)}, u32[]{:S(2)}) collective-permute-start(bf16[128,512]{1,0:T(8,128)(2,1)S(1)} %param.6), channel_id=1, source_target_pairs={{0,72},{1,73},{2,74},{3,75},{4,76},{5,77},{6,78},{7,79},{8,64},{9,... | collective-permute-start | bytes 393224 | tf_op jit(solution)/shard_map/while/body/eval_jaxpr/cond/branch_1_fun/cond/branch_1_fun/ppermute | solution.py:425
  184.2 365.8 %collective-permute-start.3 = (bf16[128,512]{1,0:T(8,128)(2,1)S(1)}, bf16[128,512]{1,0:T(8,128)(2,1)}, u32[]{:S(2)}, u32[]{:S(2)}) collective-permute-start(bf16[128,512]{1,0:T(8,128)(2,1)S(1)} %param.6), channel_id=1, source_target_pairs={{0,64},{1,65},{2,66},{3,67},{4,68},{5,69},{6,70},{7,71},{8,72},{9,... | collective-permute-start | bytes 393224 | tf_op jit(solution)/shard_map/while/body/eval_jaxpr/cond/branch_1_fun/cond/branch_1_fun/ppermute | solution.py:425
  574.0 21.8 %copy-start = (bf16[128,256]{1,0:T(8,128)(2,1)}, bf16[128,256]{1,0:T(8,128)(2,1)S(1)}, u32[]{:S(2)}) copy-start(bf16[128,256]{1,0:T(8,128)(2,1)S(1)} %get-tuple-element.669.own_ref) | copy-start | bytes 196612 | tf_op jit(solution)/shard_map/while/body/eval_jaxpr/cond
  574.0 7.6 %collective-permute-start.4 = (bf16[128,256]{1,0:T(8,128)(2,1)S(1)}, bf16[128,256]{1,0:T(8,128)(2,1)S(1)}, u32[]{:S(2)}, u32[]{:S(2)}) collective-permute-start(bf16[128,256]{1,0:T(8,128)(2,1)S(1)} %get-tuple-element.669.own_ref), channel_id=1, source_target_pairs={{0,1},{2,3},{4,5},{6,7},{8,9},{10,11},{12,13},{14,15},{16,17},{18,... | collective-permute-start | bytes 196616 | tf_op jit(solution)/shard_map/while/body/eval_jaxpr/cond/branch_1_fun/ppermute | solution.py:415
  595.7 11.4 %all-to-all-start.3 = ((bf16[4,128,512]{2,1,0:T(8,128)(2,1)}), bf16[4,128,512]{2,1,0:T(8,128)(2,1)S(1)}, u32[]{:S(2)}, u32[]{:S(2)}) async-start(bf16[4,128,512]{2,1,0:T(8,128)(2,1)} %output.1), calls=%async_computation.3 | async-start | bytes 1048576 | tf_op jit(solution)/shard_map/while/body/eval_jaxpr/cond/branch_1_fun/all_to_all | solution.py:39
  599.2 8.2 %copy-start.1 = (bf16[128,256]{1,0:T(8,128)(2,1)S(1)}, bf16[128,256]{1,0:T(8,128)(2,1)}, u32[]{:S(2)}) copy-start(bf16[128,256]{1,0:T(8,128)(2,1)} %copy-done) | copy-start | bytes 196612 | tf_op jit(solution)/shard_map/while/body/eval_jaxpr/cond
  608.3 33.0 %all-to-all-start.6 = ((bf16[8,128,256]{2,1,0:T(8,128)(2,1)}), bf16[8,128,256]{2,1,0:T(8,128)(2,1)S(1)}, u32[]{:S(2)}, u32[]{:S(2)}) async-start(bf16[8,128,256]{2,1,0:T(8,128)(2,1)} %broadcast_in_dim.83), calls=%async_computation.6 | async-start | bytes 1048576 | tf_op jit(solution)/shard_map/all_to_all | solution.py:39
  620.5 13.7 %collective-permute-start.31 = (bf16[128,256]{0,1:T(8,128)(2,1)S(1)}, bf16[128,256]{0,1:T(8,128)(2,1)S(1)}, u32[]{:S(2)}, u32[]{:S(2)}) collective-permute-start(bf16[128,256]{0,1:T(8,128)(2,1)S(1)} %dynamic-slice_bitcast_fusion.2), channel_id=1, source_target_pairs={{0,8},{1,9},{2,10},{3,11},{4,12},{5,13},{6,14},{7,15},{8,0},{9,1},... | collective-permute-start | bytes 196616 | tf_op jit(solution)/shard_map/ppermute | solution.py:457
  634.4 6.9 %collective-permute-start.32 = (bf16[128,128]{1,0:T(8,128)(2,1)S(1)}, bf16[128,128]{1,0:T(8,128)(2,1)S(1)}, u32[]{:S(2)}, u32[]{:S(2)}) collective-permute-start(bf16[128,128]{1,0:T(8,128)(2,1)S(1)} %bitcast.90), channel_id=1, source_target_pairs={{0,1},{1,0},{2,3},{3,2},{4,5},{5,4},{6,7},{7,6},{8,9},{9,8},{10,11... | collective-permute-start | bytes 98312 | tf_op jit(solution)/shard_map/ppermute | solution.py:43
  641.8 3.1 collective-permute-start.33

commit v10 on v7

--- a/solution.py
+++ b/solution.py
@@ -434,9 +434,14 @@
     _, partial, kv = lax.fori_loop(0, SECTIONS, tick, (gathered, partial, kv))
 
     pair = partial.reshape(HALF, NZ, CHIP)
+    by_half = jnp.broadcast_to(pair.transpose(1, 0, 2)[None], (NY, NZ, HALF, CHIP))
+    sent = jnp.concatenate(
+        [jnp.broadcast_to(kv[None], (NG, HALF, CHIP)), by_half.reshape(NG, HALF, CHIP)], axis=2
+    )
+    got = exchange(sent, OVER_G)
+
     kept = lax.dynamic_index_in_dim(pair, z, 1, keepdims=False)
-    given = lax.dynamic_index_in_dim(pair, 1 - z, 1, keepdims=False)
-    other = lax.ppermute(given, "wide", Z_SWAP)
+    other = lax.dynamic_slice(got, (y * NZ + 1 - z, 0, CHIP), (1, HALF, CHIP))[0]
     own = (kept.astype(jnp.float32) + other.astype(jnp.float32)).astype(jnp.bfloat16)
     columns = own.reshape(HALF, NC, HD)
     kept = lax.dynamic_index_in_dim(columns, core, 1, keepdims=False)
@@ -450,8 +455,7 @@
     slots = 2 * placement.shape[0] // WIDE
     slot = jnp.arange(slots, dtype=jnp.int32)
 
-    sent = jnp.broadcast_to(kv[None], (NG, HALF, CHIP))
-    rows = exchange(sent, OVER_G).reshape(NG * blocks, BLOCK * CHIP)
+    rows = got[:, :, :CHIP].reshape(NG * blocks, BLOCK * CHIP)
 
     def chosen(owner):
         wanted = (item_owner[None, :] == owner) & (item_rank[None, :] == slot[:, None])

time: 646 us -> 648 us (level)
    ppermute x1 -> x0, waiting for transfers between devices: 11.8 us -> none  [shards(): other = lax.ppermute(given, 'wide', Z_SWAP)]
    all_to_all x3, waiting for transfers between devices: 32.9 us -> 44.7 us  [exchange(): lax.all_to_all(value, 'wide', 0, 0, axis_index_groups=groups, tiled=True)]
  transfers between devices with their start and end apart: 22 -> 21, of which waited for: 15 -> 14; matrix products, arithmetic and copies ran while one was open for 2% -> 2% of each run, Pallas kernels for 0% -> 0%
where the time goes in v10:
time: 648 us; the launch traced here: 641 us
  waiting for transfers between devices  507 us (78%)
  starting transfers between devices  73.4 us (11%)
  blocking collectives  27.8 us (4%)
  local copies, waits for them, and re-layouts  12 us (2%)
  Pallas kernels  9.11 us (1%)
  other arithmetic  7.81 us (1%)
    ppermute x2, waiting for transfers between devices, run(): return (lax.ppermute(value, axes, cross), lax.ppermute(value, axes, same))  365 us
    ppermute x1, waiting for transfers between devices, prepare(): far = lax.ppermute(given, 'wide', Z_SWAP)  68.9 us
    all_to_all x3, waiting for transfers between devices, exchange(): lax.all_to_all(value, 'wide', 0, 0, axis_index_groups=groups, tiled=True)  44.7 us
    all_to_all x3, blocking collectives, exchange(): lax.all_to_all(value, 'wide', 0, 0, axis_index_groups=groups, tiled=True)  27.8 us
    all_to_all x3, starting transfers between devices, exchange(): lax.all_to_all(value, 'wide', 0, 0, axis_index_groups=groups, tiled=True)  20.1 us
    ppermute x6, starting transfers between devices, swap_cores(): return lax.ppermute(value, 'wide', CORE_SWAP)  19.3 us
    ppermute x6, waiting for transfers between devices, from_ring(): blocks.append(lax.ppermute(piece((at + step) % 4), 'wide', pairs))  19.2 us
    ppermute x6, starting transfers between devices, from_ring(): blocks.append(lax.ppermute(piece((at + step) % 4), 'wide', pairs))  19.1 us
  transfers between devices with their start and end apart: 21, of which 14 were waited for; matrix products, arithmetic and copies ran while one was open for 2% of the time, Pallas kernels for 0%

profile of v10, /device:TPU:481, one launch (start us, length us, event | category | flops | bytes accessed | tf_op | source)
XLA Modules:
  0.0 640.8 jit_solution(8172073284178706615)
XLA Ops:
  1.4 2.6 collective-permute-start.28
  12.2 166.6 %conditional.6 = (bf16[4,128,512]{2,1,0:T(8,128)(2,1)S(1)}, bf16[4,2048,128]{2,1,0:T(8,128)(2,1)}, bf16[4,2048,128]{2,1,0:T(8,128)(2,1)}, bf16[256,2048]{1,0:T(8...) conditional(s32[]{:T(128)} %convert_element_type.90, ...), branch_computations={%region_0.4_spmd, %region_4.5_spmd} | conditional | flops 10027141 | bytes 88870032 | solution.py:378
  12.2 3.2 copy.40
  15.4 4.6 all-to-all-start
  20.8 25.0 %all-to-all-done = bf16[4,2048,128]{2,1,0:T(8,128)(2,1)} async-done(((bf16[4,2048,128]{2,1,0:T(8,128)(2,1)}), bf16[4,2048,128]{2,1,0:T(8,128)(2,1)}, u32[]{:S(2)}, u32[]{:S(2)}) %all-to-all-start) | async-done | bytes 2097184 | tf_op jit(solution)/shard_map/cond/branch_0_fun/all_to_all | solution.py:39
  48.1 3.7 collective-permute-start.6
  55.6 3.6 collective-permute-done.7
  59.3 8.4 %collective-permute-start.9 = (bf16[4,1024,128]{2,1,0:T(8,128)(2,1)}, bf16[4,1024,128]{2,1,0:T(8,128)(2,1)S(1)}, u32[]{:S(2)}, u32[]{:S(2)}) collective-permute-start(bf16[4,1024,128]{2,1,0:T(8,128)(2,1)} %get-tuple-element.354), channel_id=1, source_target_pairs={{0,8},{1,9},{2,10},{3,11},{4,12},{5,13},{6,14},{7,15},{8,0},{9,1},... | collective-permute-start | bytes 3145736 | tf_op jit(solution)/shard_map/cond/branch_0_fun/ppermute | solution.py:356
  67.8 68.9 %collective-permute-done.9 = bf16[4,1024,128]{2,1,0:T(8,128)(2,1)S(1)} collective-permute-done((bf16[4,1024,128]{2,1,0:T(8,128)(2,1)}, bf16[4,1024,128]{2,1,0:T(8,128)(2,1)S(1)}, u32[]{:S(2)}, u32[]{:S(2)}) %collective-permute-start.9) | collective-permute-done | bytes 1048608 | tf_op jit(solution)/shard_map/cond/branch_0_fun/ppermute | solution.py:356
  137.0 3.2 collective-permute-start.10
  140.2 4.5 collective-permute-start.11
  144.8 3.0 collective-permute-start.12
  147.8 3.5 collective-permute-start.4
  153.0 12.3 %collective-permute-done.11 = bf16[1,2048,128]{2,1,0:T(8,128)(2,1)S(1)} collective-permute-done((bf16[1,2048,128]{2,1,0:T(8,128)(2,1)S(1)}, bf16[1,2048,128]{2,1,0:T(8,128)(2,1)S(1)}, u32[]{:S(2)}, u32[]{:S(2)}) %collective-permute-start.11) | collective-permute-done | bytes 524320 | tf_op jit(solution)/shard_map/cond/branch_0_fun/ppermute | solution.py:65
  170.2 3.5 collective-permute-start.13
  178.9 426.1 %while.23 = (s32[]{:T(128)}, bf16[4,128,512]{2,1,0:T(8,128)(2,1)S(1)}, bf16[128,512]{1,0:T(8,128)(2,1)S(1)}, bf16[128,256]{1,0:T(8,128)(2,1)S(1)}, s32[]{:T(128)...) while((s32[]{:T(128)}, ...), condition=%wide.region_14.15_spmd, body=%wide.region_5.14_spmd.sunk | while | flops 983069 | bytes 11141949 | solution.py:434
  179.4 378.5 %conditional.11 = (bf16[4,128,512]{2,1,0:T(8,128)(2,1)S(1)}) conditional(s32[]{:T(128)} %convert_element_type.123, bf16[4,128,512]{2,1,0:T(8,128)(2,1)S(1)} %get-tuple-element.696, (s32[]{:T(128)}, s32[]{:T(128)}, bf16[128,512]{1,0:T(8,128)(2,1)S(1)}, bf16[4,128,512]{2,1,0:T(8,128)(2,1)S(1)}) %tuple.140), branch_computations={%region_8.8_spmd, %region_9.13_spmd} | conditional | flops 262160 | bytes 4194573 | solution.py:423
  179.4 368.1 %conditional = (bf16[128,512]{1,0:T(8,128)(2,1)}, bf16[128,512]{1,0:T(8,128)(2,1)}) conditional(s32[]{:T(128)} %convert_element_type.75, bf16[128,512]{1,0:T(8,128)(2,1)S(1)} %get-tuple-element.396, bf16[128,512]{1,0:T(8,128)(2,1)S(1)} %get-tuple-element.396), branch_computations={%region_10.9_spmd, %region_11.10_spmd} | conditional | bytes 1048672 | solution.py:418
  182.0 365.5 %collective-permute-done.2 = bf16[128,512]{1,0:T(8,128)(2,1)} collective-permute-done((bf16[128,512]{1,0:T(8,128)(2,1)S(1)}, bf16[128,512]{1,0:T(8,128)(2,1)}, u32[]{:S(2)}, u32[]{:S(2)}) %collective-permute-start.2) | collective-permute-done | bytes 131104 | tf_op jit(solution)/shard_map/while/body/eval_jaxpr/cond/branch_1_fun/cond/branch_1_fun/ppermute | solution.py:407
  547.5 10.4 %conditional.1 = (bf16[4,128,512]{2,1,0:T(8,128)(2,1)S(1)}) conditional(s32[]{:T(128)} %convert_element_type.74, bf16[4,128,512]{2,1,0:T(8,128)(2,1)S(1)} %get-tuple-element.395, (bf16[128,512]{1,0:T(8,128)(2,1)}, bf16[128,512]{1,0:T(8,128)(2,1)}) %tuple.62), branch_computations={%region_12.11_spmd, %region_13.12_spmd} | conditional | flops 262144 | bytes 3145736 | solution.py:419
  548.5 9.3 %all_to_all.31 = bf16[4,128,512]{2,1,0:T(8,128)(2,1)S(1)} all-to-all(bf16[4,128,512]{2,1,0:T(8,128)(2,1)S(1)} %broadcast_in_dim.61), channel_id=1, replica_groups={{0,16,32,48},{1,17,33,49},{2,18,34,50},{3,19,35,51},{4,20,36,52},{5,21,..., dimensions={0} | all-to-all | bytes 1048576 | tf_op jit(solution)/shard_map/while/body/eval_jaxpr/cond/branch_1_fun/cond/branch_1_fun/all_to_all | solution.py:39
  557.9 46.9 %conditional.10 = ((bf16[128,512]{1,0:T(8,128)(2,1)S(1)}, bf16[128,256]{1,0:T(8,128)(2,1)S(1)})) conditional(s32[]{:T(128)} %convert_element_type.124, (bf16[128,512]{1,0:T(8,128)(2,1)S(1)}, bf16[128,256]{1,0:T(8,128)(2,1)S(1)}) %tuple.138, (s32[]{:T(128)}, s32[]{:T(128)}, bf16[4,128,512]{2,1,0:T(8,128)(2,1)S(1)}, s32[4]{0:T(128)S(1)}, ...), branch_computations={%region_6.6_spmd, %region_7.7_spmd} | conditional | flops 720900 | bytes 6947016 | solution.py:415
  557.9 3.6 project.1
  561.5 9.7 %all_to_all.29.part_ref = bf16[4,144,512]{2,1,0:T(8,128)(2,1)S(1)} all-to-all(bf16[4,144,512]{2,1,0:T(8,128)(2,1)S(1)} %project.1), channel_id=1, replica_groups={{0,2,4,6},{1,3,5,7},{8,10,12,14},{9,11,13,15},{16,18,20,22},{17,19,21,2..., dimensions={0} | all-to-all | bytes 1179648 | tf_op jit(solution)/shard_map/while/body/eval_jaxpr/cond/branch_1_fun/all_to_all | solution.py:39
  572.8 6.3 collective-permute-done.27.first_ref
  580.5 8.8 %all_to_all.30.ctx_ref = bf16[4,128,256]{2,1,0:T(8,128)(2,1)S(1)} all-to-all(bf16[4,128,256]{2,1,0:T(8,128)(2,1)S(1)} %attend.1), channel_id=1, replica_groups={{0,2,4,6},{1,3,5,7},{8,10,12,14},{9,11,13,15},{16,18,20,22},{17,19,21,2..., dimensions={0} | all-to-all | bytes 524288 | tf_op jit(solution)/shard_map/while/body/eval_jaxpr/cond/branch_1_fun/all_to_all | solution.py:39
  589.3 3.9 output.1
  593.2 3.5 all-to-all-start.4
  596.7 7.9 %all-to-all-done.4 = bf16[4,128,512]{2,1,0:T(8,128)(2,1)S(1)} async-done(((bf16[4,128,512]{2,1,0:T(8,128)(2,1)}), bf16[4,128,512]{2,1,0:T(8,128)(2,1)S(1)}, u32[]{:S(2)}, u32[]{:S(2)}) %all-to-all-start.4) | async-done | bytes 524320 | tf_op jit(solution)/shard_map/while/body/eval_jaxpr/cond/branch_1_fun/all_to_all | solution.py:39
  606.4 12.1 %all-to-all-start.6 = ((bf16[8,128,512]{1,2,0:T(8,128)(2,1)}), bf16[8,128,512]{1,2,0:T(8,128)(2,1)S(1)}, u32[]{:S(2)}, u32[]{:S(2)}) async-start(bf16[8,128,512]{1,2,0:T(8,128)(2,1)} %pad_maximum_fusion.10), calls=%async_computation.6 | async-start | bytes 2097152 | tf_op jit(solution)/shard_map/all_to_all | solution.py:39
  618.5 11.8 %all-to-all-done.6 = bf16[8,128,512]{1,2,0:T(8,128)(2,1)S(1)} async-done(((bf16[8,128,512]{1,2,0:T(8,128)(2,1)}), bf16[8,128,512]{1,2,0:T(8,128)(2,1)S(1)}, u32[]{:S(2)}, u32[]{:S(2)}) %all-to-all-start.6) | async-done | bytes 1048608 | tf_op jit(solution)/shard_map/all_to_all | solution.py:39
  631.0 5.9 collective-permute-start.32
  (118 shorter events, 39.8 us)
Async XLA Ops:
  1.4 7.1 %collective-permute-start.28 = (bf16[128,128]{1,0:T(8,128)(2,1)S(1)}, bf16[128,128]{1,0:T(8,128)(2,1)S(1)}, u32[]{:S(2)}, u32[]{:S(2)}) collective-permute-start(bf16[128,128]{1,0:T(8,128)(2,1)S(1)} %dynamic-slice_bitcast_fusion.4), channel_id=1, source_target_pairs={{0,1},{1,0},{2,3},{3,2},{4,5},{5,4},{6,7},{7,6},{8,9},{9,8},{10,11... | collective-permute-start | bytes 98312 | tf_op jit(solution)/shard_map/ppermute | solution.py:43
  4.0 7.2 %collective-permute-start.30 = (bf16[128,128]{1,0:T(8,128)(2,1)S(1)}, bf16[128,128]{1,0:T(8,128)(2,1)S(1)}, u32[]{:S(2)}, u32[]{:S(2)}) collective-permute-start(bf16[128,128]{1,0:T(8,128)(2,1)S(1)} %dynamic-slice_bitcast_fusion.4), channel_id=1, source_target_pairs={{448,9},{449,8},{450,11},{451,10},{452,13},{453,12},{454,15},{455,... | collective-permute-start | bytes 98312 | tf_op jit(solution)/shard_map/ppermute | solution.py:326
  9.3 2.3 collective-permute-start.29
  15.4 4.7 copy-start.4
  15.4 4.9 copy-start.6
  15.4 30.5 %all-to-all-start = ((bf16[4,2048,128]{2,1,0:T(8,128)(2,1)}), bf16[4,2048,128]{2,1,0:T(8,128)(2,1)}, u32[]{:S(2)}, u32[]{:S(2)}) async-start(bf16[4,2048,128]{2,1,0:T(8,128)(2,1)} %bitcast.2), calls=%async_computation | async-start | bytes 4194304 | tf_op jit(solution)/shard_map/cond/branch_0_fun/all_to_all | solution.py:39
  20.3 34.1 %copy-start = (bf16[4,2,1024,128]{3,2,1,0:T(8,128)(2,1)S(1)}, bf16[4,2,1024,128]{3,2,1,0:T(8,128)(2,1)}, u32[]{:S(2)}) copy-start(bf16[4,2,1024,128]{3,2,1,0:T(8,128)(2,1)} %get-tuple-element.352) | copy-start | bytes 6291460 | tf_op jit(solution)/shard_map/cond
  45.9 9.6 %collective-permute-start.5 = (bf16[1,32,2048]{2,1,0:T(8,128)(2,1)S(1)}, bf16[1,32,2048]{2,1,0:T(8,128)(2,1)S(1)}, u32[]{:S(2)}, u32[]{:S(2)}) collective-permute-start(bf16[1,32,2048]{2,1,0:T(8,128)(2,1)S(1)} %get-tuple-element.515), channel_id=1, source_target_pairs={{0,2},{1,3},{2,4},{3,5},{4,6},{5,7},{6,0},{7,1},{8,10},{9,11},{10,... | collective-permute-start | bytes 393224 | tf_op jit(solution)/shard_map/cond/branch_0_fun/ppermute | solution.py:65
  48.1 7.5 %collective-permute-start.6 = (bf16[1,32,2048]{2,1,0:T(8,128)(2,1)S(1)}, bf16[1,32,2048]{2,1,0:T(8,128)(2,1)S(1)}, u32[]{:S(2)}, u32[]{:S(2)}) collective-permute-start(bf16[1,32,2048]{2,1,0:T(8,128)(2,1)S(1)} %get-tuple-element.514), channel_id=1, source_target_pairs={{0,4},{1,5},{2,6},{3,7},{4,0},{5,1},{6,2},{7,3},{8,12},{9,13},{10,... | collective-permute-start | bytes 393224 | tf_op jit(solution)/shard_map/cond/branch_0_fun/ppermute | solution.py:65
  51.8 7.4 %collective-permute-start.7 = (bf16[1,32,2048]{2,1,0:T(8,128)(2,1)S(1)}, bf16[1,32,2048]{2,1,0:T(8,128)(2,1)S(1)}, u32[]{:S(2)}, u32[]{:S(2)}) collective-permute-start(bf16[1,32,2048]{2,1,0:T(8,128)(2,1)S(1)} %get-tuple-element.513), channel_id=1, source_target_pairs={{0,6},{1,7},{2,0},{3,1},{4,2},{5,3},{6,4},{7,5},{8,14},{9,15},{10,... | collective-permute-start | bytes 393224 | tf_op jit(solution)/shard_map/cond/branch_0_fun/ppermute | solution.py:65
  59.3 77.5 %collective-permute-start.9 = (bf16[4,1024,128]{2,1,0:T(8,128)(2,1)}, bf16[4,1024,128]{2,1,0:T(8,128)(2,1)S(1)}, u32[]{:S(2)}, u32[]{:S(2)}) collective-permute-start(bf16[4,1024,128]{2,1,0:T(8,128)(2,1)} %get-tuple-element.354), channel_id=1, source_target_pairs={{0,8},{1,9},{2,10},{3,11},{4,12},{5,13},{6,14},{7,15},{8,0},{9,1},... | collective-permute-start | bytes 3145736 | tf_op jit(solution)/shard_map/cond/branch_0_fun/ppermute | solution.py:356
  137.0 15.9 %collective-permute-start.10 = (bf16[1,2048,128]{2,1,0:T(8,128)(2,1)S(1)}, bf16[1,2048,128]{2,1,0:T(8,128)(2,1)S(1)}, u32[]{:S(2)}, u32[]{:S(2)}) collective-permute-start(bf16[1,2048,128]{2,1,0:T(8,128)(2,1)S(1)} %get-tuple-element.498), channel_id=1, source_target_pairs={{0,16},{1,17},{2,18},{3,19},{4,20},{5,21},{6,22},{7,23},{8,24},{9,... | collective-permute-start | bytes 1572872 | tf_op jit(solution)/shard_map/cond/branch_0_fun/ppermute | solution.py:65
  140.2 25.1 %collective-permute-start.11 = (bf16[1,2048,128]{2,1,0:T(8,128)(2,1)S(1)}, bf16[1,2048,128]{2,1,0:T(8,128)(2,1)S(1)}, u32[]{:S(2)}, u32[]{:S(2)}) collective-permute-start(bf16[1,2048,128]{2,1,0:T(8,128)(2,1)S(1)} %get-tuple-element.497), channel_id=1, source_target_pairs={{0,32},{1,33},{2,34},{3,35},{4,36},{5,37},{6,38},{7,39},{8,40},{9,... | collective-permute-start | bytes 1572872 | tf_op jit(solution)/shard_map/cond/branch_0_fun/ppermute | solution.py:65
  144.8 22.0 %collective-permute-start.12 = (bf16[1,2048,128]{2,1,0:T(8,128)(2,1)S(1)}, bf16[1,2048,128]{2,1,0:T(8,128)(2,1)S(1)}, u32[]{:S(2)}, u32[]{:S(2)}) collective-permute-start(bf16[1,2048,128]{2,1,0:T(8,128)(2,1)S(1)} %get-tuple-element.496), channel_id=1, source_target_pairs={{0,48},{1,49},{2,50},{3,51},{4,52},{5,53},{6,54},{7,55},{8,56},{9,... | collective-permute-start | bytes 1572872 | tf_op jit(solution)/shard_map/cond/branch_0_fun/ppermute | solution.py:65
  147.8 30.8 %collective-permute-start.4 = (bf16[4,2048,128]{2,1,0:T(8,128)(2,1)}, bf16[4,2048,128]{2,1,0:T(8,128)(2,1)}, u32[]{:S(2)}, u32[]{:S(2)}) collective-permute-start(bf16[4,2048,128]{2,1,0:T(8,128)(2,1)} %all-to-all-done), channel_id=1, source_target_pairs={{0,1},{1,0},{2,3},{3,2},{4,5},{5,4},{6,7},{7,6},{8,9},{9,8},{10,11... | collective-permute-start | bytes 6291464 | tf_op jit(solution)/shard_map/cond/branch_0_fun/ppermute | solution.py:43
  166.8 8.9 %copy-start.11 = (s32[256,1]{0,1:T(1,128)S(1)}, s32[256,1]{0,1:T(1,128)}, u32[]{:S(2)}) copy-start(s32[256,1]{0,1:T(1,128)} %get-tuple-element.360) | copy-start | bytes 3076 | tf_op jit(solution)/shard_map/cond
  170.2 8.4 %collective-permute-start.13 = (bf16[4,2048,128]{2,1,0:T(8,128)(2,1)}, bf16[4,2048,128]{2,1,0:T(8,128)(2,1)}, u32[]{:S(2)}, u32[]{:S(2)}) collective-permute-start(bf16[4,2048,128]{2,1,0:T(8,128)(2,1)} %constant_dynamic-update-slice_fusion), channel_id=1, source_target_pairs={{0,1},{1,0},{2,3},{3,2},{4,5},{5,4},{6,7},{7,6},{8,9},{9,8},{10,11... | collective-permute-start | bytes 6291464 | tf_op jit(solution)/shard_map/cond/branch_0_fun/ppermute | solution.py:43
  173.6 4.5 collective-permute-start.8
  179.4 368.1 %collective-permute-start.2 = (bf16[128,512]{1,0:T(8,128)(2,1)S(1)}, bf16[128,512]{1,0:T(8,128)(2,1)}, u32[]{:S(2)}, u32[]{:S(2)}) collective-permute-start(bf16[128,512]{1,0:T(8,128)(2,1)S(1)} %param.6), channel_id=1, source_target_pairs={{0,72},{1,73},{2,74},{3,75},{4,76},{5,77},{6,78},{7,79},{8,64},{9,... | collective-permute-start | bytes 393224 | tf_op jit(solution)/shard_map/while/body/eval_jaxpr/cond/branch_1_fun/cond/branch_1_fun/ppermute | solution.py:407
  180.7 366.8 %collective-permute-start.3 = (bf16[128,512]{1,0:T(8,128)(2,1)S(1)}, bf16[128,512]{1,0:T(8,128)(2,1)}, u32[]{:S(2)}, u32[]{:S(2)}) collective-permute-start(bf16[128,512]{1,0:T(8,128)(2,1)S(1)} %param.6), channel_id=1, source_target_pairs={{0,64},{1,65},{2,66},{3,67},{4,68},{5,69},{6,70},{7,71},{8,72},{9,... | collective-permute-start | bytes 393224 | tf_op jit(solution)/shard_map/while/body/eval_jaxpr/cond/branch_1_fun/cond/branch_1_fun/ppermute | solution.py:407
  571.4 21.7 %copy-start.2 = (bf16[128,256]{1,0:T(8,128)(2,1)}, bf16[128,256]{1,0:T(8,128)(2,1)S(1)}, u32[]{:S(2)}) copy-start(bf16[128,256]{1,0:T(8,128)(2,1)S(1)} %get-tuple-element.660.own_ref) | copy-start | bytes 196612 | tf_op jit(solution)/shard_map/while/body/eval_jaxpr/cond
  571.5 7.6 %collective-permute-start.27 = (bf16[128,256]{1,0:T(8,128)(2,1)S(1)}, bf16[128,256]{1,0:T(8,128)(2,1)S(1)}, u32[]{:S(2)}, u32[]{:S(2)}) collective-permute-start(bf16[128,256]{1,0:T(8,128)(2,1)S(1)} %get-tuple-element.660.own_ref), channel_id=1, source_target_pairs={{0,1},{2,3},{4,5},{6,7},{8,9},{10,11},{12,13},{14,15},{16,17},{18,... | collective-permute-start | bytes 196616 | tf_op jit(solution)/shard_map/while/body/eval_jaxpr/cond/branch_1_fun/ppermute | solution.py:397
  593.2 11.4 %all-to-all-start.4 = ((bf16[4,128,512]{2,1,0:T(8,128)(2,1)}), bf16[4,128,512]{2,1,0:T(8,128)(2,1)S(1)}, u32[]{:S(2)}, u32[]{:S(2)}) async-start(bf16[4,128,512]{2,1,0:T(8,128)(2,1)} %output.1), calls=%async_computation.4 | async-start | bytes 1048576 | tf_op jit(solution)/shard_map/while/body/eval_jaxpr/cond/branch_1_fun/all_to_all | solution.py:39
  596.7 8.2 %copy-start.3 = (bf16[128,256]{1,0:T(8,128)(2,1)S(1)}, bf16[128,256]{1,0:T(8,128)(2,1)}, u32[]{:S(2)}) copy-start(bf16[128,256]{1,0:T(8,128)(2,1)} %copy-done.2) | copy-start | bytes 196612 | tf_op jit(solution)/shard_map/while/body/eval_jaxpr/cond
  605.3 13.2 %copy-start.10 = (s32[256,1]{0,1:T(1,128)S(1)}, s32[256,1]{0,1:T(1,128)}, u32[]{:S(2)}) copy-start(s32[256,1]{0,1:T(1,128)} %param.29) | copy-start | bytes 3076
  606.4 23.8 %all-to-all-start.6 = ((bf16[8,128,512]{1,2,0:T(8,128)(2,1)}), bf16[8,128,512]{1,2,0:T(8,128)(2,1)S(1)}, u32[]{:S(2)}, u32[]{:S(2)}) async-start(bf16[8,128,512]{1,2,0:T(8,128)(2,1)} %pad_maximum_fusion.10), calls=%async_computation.6 | async-start | bytes 2097152 | tf_op jit(solution)/shard_map/all_to_all | solution.py:39
  631.0 8.1 %collective-permute-start.32 = (bf16[8,2048]{1,0:T(8,128)(2,1)S(1)}, bf16[8,2048]{1,0:T(8,128)(2,1)S(1)}, u32[]{:S(2)}, u32[]{:S(2)}) collective-permute-start(bf16[8,2048]{1,0:T(8,128)(2,1)S(1)} %convolution_convert_fusion), channel_id=1, source_target_pairs={{0,1},{1,0},{2,3},{3,2},{4,5},{5,4},{6,7},{7,6},{8,9},{9,8},{10,11... | collective-permute-start | bytes 98312 | tf_op jit(solution)/shard_map/ppermute | solution.py:43
  637.1 3.1 collective-permute-start.31
